TPU v7x, 32 devices: a whole 2x2x4 slice. The times are simulated.
32 devices in a mesh: fluid: 4 (over z), solid: 8 (over y, x, core).
Axes of the slice: x: 2, y: 2, z: 4, core: 2. Of those that a mesh axis runs over, the one named last changes fastest.
Arguments:
- pressure: float32 [32768, 128], P(('fluid', 'solid')), may hold values from -24 to 24
- face_owner: int32 [32768, 1], P(('fluid', 'solid')), may hold values from 0 to 31; in each aligned block of 1024 rows (0 to 1023, 1024 to 2047, ...) at most 80 rows name the same one
- face_element: int32 [32768], P(('fluid', 'solid')), may hold values from 0 to 1023
- shape_table: float32 [24, 128], replicated, may hold values from -0.5 to 0.5
- stiffness: float32 [24, 24, 32768], P(None, None, ('fluid', 'solid')), as said below
- connectivity: int32 [8, 32768], P(None, ('fluid', 'solid')), may hold values from 0 to 1151, as said below
- support: float32 [3, 32768], P(None, ('fluid', 'solid')), may hold values from 0.5 to 5
Outputs:
- displacement: float32 [3, 32768], P(None, ('fluid', 'solid'))
- face_motion: float32 [32768, 128], P(('fluid', 'solid'))
Inputs may be any that keep to these rules, and one draw needn't show every extreme that they name: `face_owner`: in the rows of one device no owner is named by more than 80 faces, a bound that some block reaches. `connectivity`: an entry below 1024 names a node of the element's own partition; an entry j of 1024 or more names node j - 1024 of the next partition in the order of the index over fluid and solid together; elements of the last partition name their own nodes only. `stiffness`: each element's matrix is symmetric with a positive diagonal that exceeds the sum of magnitudes of the rest of its row.
All inputs are finite; a program needn't handle non-finite values.
Results may differ from a plain program's by a relative error of at most 0.0001.
Values sent between devices are 32-bit elements; how exact they have to be, the bound alone decides.
No kernel may reach another device: no remote copies, remote signals or barrier semaphores. Data moves between devices by JAX's collectives and lax.ppermute only.
A program may use at most 64 MiB of HBM per device.

v0:
```python
import jax
import jax.numpy as jnp
from jax import lax
from jax.sharding import PartitionSpec as P

ITERS = 3


def from_behind(value, axis, steps):
    count = lax.axis_size(axis)
    first, last = (max(0, -steps), min(count, count - steps))
    return lax.ppermute(value, axis, [(source, source + steps) for source in range(first, last)])


def project_rows(rows, shape_table):
    return lax.dot_general(
        rows,
        shape_table,
        (((1,), (1,)), ((), ())),
        precision=lax.Precision.HIGHEST,
        preferred_element_type=jnp.float32,
    )


def expand_rows(rows, shape_table):
    return lax.dot_general(
        rows,
        shape_table,
        (((1,), (0,)), ((), ())),
        precision=lax.Precision.HIGHEST,
        preferred_element_type=jnp.float32,
    )


def squares(vector):
    return lax.psum(jnp.sum(vector * vector), ("fluid", "solid"))


def shards(pressure, face_owner, face_element, shape_table, stiffness, connectivity, support):
    dev_count = lax.axis_size(("fluid", "solid"))
    face_count = pressure.shape[0]
    elem_count = stiffness.shape[2]
    node_count = support.shape[1]
    shared = elem_count // 8
    capacity = max(2, (5 * face_count + 2 * dev_count - 1) // (2 * dev_count))
    target = face_owner[:, 0]
    onehot = (target[:, None] == jnp.arange(dev_count, dtype=jnp.int32)[None, :]).astype(jnp.int32)
    slot_index = jnp.sum((jnp.cumsum(onehot, axis=0) - onehot) * onehot, axis=1)
    element_code = (
        jnp.zeros((dev_count, capacity), jnp.float32)
        .at[target, slot_index]
        .set(face_element.astype(jnp.float32))
    )
    outgoing_rows = project_rows(pressure, shape_table)
    row_width = outgoing_rows.shape[1]
    outgoing = (
        jnp.zeros((dev_count, capacity, row_width), jnp.float32)
        .at[target, slot_index]
        .set(outgoing_rows)
    )
    arrived, arrived_code = (
        lax.all_to_all(outgoing, ("fluid", "solid"), split_axis=0, concat_axis=0, tiled=True),
        lax.all_to_all(element_code, ("fluid", "solid"), split_axis=0, concat_axis=0, tiled=True),
    )
    arrived_rows = arrived.reshape(dev_count * capacity, row_width)
    element_ids = arrived_code.reshape(dev_count * capacity).astype(jnp.int32)
    element_loads = jax.ops.segment_sum(arrived_rows, element_ids, num_segments=elem_count).T

    def element_values(field):
        rim_nodes = field[:, :shared]
        remote = from_behind(rim_nodes, ("fluid", "solid"), -1)
        extended = jnp.concatenate([field, remote], axis=1)
        return extended[:, connectivity].reshape(24, elem_count)

    def assemble_terms(terms):
        totals = jnp.zeros((3, node_count + shared), jnp.float32)
        totals = totals.at[:, connectivity.reshape(-1)].add(terms.reshape(3, -1))
        incoming = from_behind(totals[:, node_count:], ("fluid", "solid"), 1)
        return totals[:, :node_count].at[:, :shared].add(incoming)

    nodal_loads = assemble_terms(element_loads)
    displacement = jnp.zeros((3, node_count), jnp.float32)
    residual = nodal_loads
    direction = nodal_loads
    norm_now = squares(residual)
    for iteration in range(ITERS):
        element_disp = element_values(direction)
        forces = jnp.einsum("abe,be->ae", stiffness, element_disp, precision=lax.Precision.HIGHEST)
        image = assemble_terms(forces) + support * direction
        curving = lax.psum(jnp.sum(direction * image), ("fluid", "solid"))
        step_size = norm_now / curving
        displacement = displacement + step_size * direction
        residual = residual - step_size * image
        if iteration + 1 < ITERS:
            norm_next = squares(residual)
            direction = residual + norm_next / norm_now * direction
            norm_now = norm_next
    final_values = element_values(displacement)
    picked = final_values[:, element_ids].T
    back_width = picked.shape[1]
    leaving = picked.reshape(dev_count, capacity, back_width)
    returned = lax.all_to_all(leaving, ("fluid", "solid"), split_axis=0, concat_axis=0, tiled=True)
    owned_rows = returned[target, slot_index]
    face_motion = expand_rows(owned_rows, shape_table)
    return (displacement, face_motion)


def solution(mesh):
    in_specs = (
        P(("fluid", "solid"), None),
        P(("fluid", "solid"), None),
        P(("fluid", "solid")),
        P(),
        P(None, None, ("fluid", "solid")),
        P(None, ("fluid", "solid")),
        P(None, ("fluid", "solid")),
    )
    out_specs = (P(None, ("fluid", "solid")), P(("fluid", "solid"), None))
    return jax.shard_map(shards, mesh=mesh, in_specs=in_specs, out_specs=out_specs, check_vma=False)
```

profile of v0, /device:TPU:0, one launch (start us, length us, event | category | flops | bytes accessed | tf_op | source)
XLA Modules:
  0.0 679.4 jit_solution(1847889649005151473)
XLA Ops:
  2.1 9.0 %reduce-window.6 = s32[32,8,128]{2,1,0:T(8,128)S(1)} reduce-window(s32[32,8,128]{2,1,0:T(8,128)S(1)} %fusion.15, s32[]{:T(128)} %constant.107.clone.1), window={size=1x1x128 pad=0_0x0_0x127_0}, to_apply=%region_0.0 | reduce-window | flops 4161536 | bytes 262148 | tf_op jit(solution)/shard_map/reduce-window
  14.5 4.3 scatter_custom_fusion.5
  19.5 7.3 %all-to-all-start = ((f32[32,1,80]{2,1,0:T(1,128)}), f32[32,1,80]{2,1,0:T(1,128)S(1)}, u32[]{:S(2)}, u32[]{:S(2)}) async-start(f32[32,1,80]{2,1,0:T(1,128)} %all_to_all.12), calls=%async_computation | async-start | bytes 32768 | tf_op jit(solution)/shard_map/all_to_all | solution.py:63
  28.9 3.4 scatter_custom_fusion.6
  33.9 5.4 all-to-all-start.1
  39.5 13.0 %all-to-all-done.1 = f32[32,80,24]{1,2,0:T(8,128)S(1)} async-done(((f32[32,80,24]{1,2,0:T(8,128)}), f32[32,80,24]{1,2,0:T(8,128)S(1)}, u32[]{:S(2)}, u32[]{:S(2)}) %all-to-all-start.1) | async-done | bytes 245792 | tf_op jit(solution)/shard_map/all_to_all | solution.py:62
  52.9 15.2 %scatter_custom_fusion = f32[1024,24]{1,0:T(8,128)S(1)} fusion(s32[2560]{0:T(1024)S(1)} %reshape.290, f32[2560,24]{1,0:T(8,128)S(1)} %bitcast.91, f32[]{:T(128)} %constant.106.clone.1), kind=kCustom, calls=%fused_computation.26 | custom fusion | flops 61440 | bytes 98308 | tf_op jit(solution)/shard_map/scatter-add | solution.py:67
  68.4 2.6 copy.143
  71.0 44.6 %scatter_custom_fusion.1 = f32[3,1152]{0,1:T(8,128)S(1)} fusion(s32[8192]{0:T(1024)S(1)} %bitcast.109, f32[8192,3]{1,0:T(8,128)} %copy.143, f32[]{:T(128)} %constant.106.clone.1), kind=kCustom, calls=%fused_computation.24 | custom fusion | flops 24576 | bytes 14336 | tf_op jit(solution)/shard_map/scatter-add | solution.py:77
  116.3 2.7 collective-permute-start
  129.7 27.7 %gather_fusion = f32[8192,3]{1,0:T(8,128)} fusion(f32[3,1152]{0,1:T(8,128)S(1)} %copy.147, s32[8192]{0:T(1024)S(1)} %bitcast_clamp_fusion), kind=kCustom, calls=%fused_computation | custom fusion | bytes 229376 | tf_op jit(solution)/shard_map/gather | solution.py:73
  157.4 2.9 copy.209
  163.5 44.4 %scatter_custom_fusion.2 = f32[3,1152]{0,1:T(8,128)S(1)} fusion(s32[8192]{0:T(1024)} %bitcast.110, f32[8192,3]{1,0:T(8,128)} %copy.149, f32[]{:T(128)} %constant.106.clone.1), kind=kCustom, calls=%fused_computation.22 | custom fusion | flops 24576 | bytes 14336 | tf_op jit(solution)/shard_map/scatter-add | solution.py:77
  209.5 4.3 collective-permute-start.2
  217.9 41.5 %all-reduce = (f32[]{:T(128)}, f32[]{:T(128)}) all-reduce(f32[]{:T(128)} %get-tuple-element.63, f32[]{:T(128)} %get-tuple-element.62), channel_id=1, replica_groups=mesh['fluid'=4,'solid'=8] {'fluid','solid'}, use_global_device_ids=true, to_apply=%region_9.10 | all-reduce | flops 2 | bytes 16 | tf_op jit(solution)/shard_map/psum | solution.py:36
  261.4 40.1 %psum.44 = f32[]{:T(128)} all-reduce(f32[]{:T(128)} %get-tuple-element.68), channel_id=1, replica_groups=mesh['fluid'=4,'solid'=8] {'fluid','solid'}, use_global_device_ids=true, to_apply=%region_14.15 | all-reduce | flops 1 | bytes 8 | tf_op jit(solution)/shard_map/psum | solution.py:36
  307.5 27.7 %gather_fusion.1 = f32[8192,3]{1,0:T(8,128)} fusion(f32[3,1152]{0,1:T(8,128)S(1)} %copy.153, s32[8192]{0:T(1024)S(1)} %bitcast_clamp_fusion), kind=kCustom, calls=%fused_computation.1 | custom fusion | bytes 229376 | tf_op jit(solution)/shard_map/gather | solution.py:73
  335.2 2.9 copy.210
  341.2 44.4 %scatter_custom_fusion.3 = f32[3,1152]{0,1:T(8,128)S(1)} fusion(s32[8192]{0:T(1024)} %bitcast.111, f32[8192,3]{1,0:T(8,128)} %copy.155, f32[]{:T(128)} %constant.106.clone.1), kind=kCustom, calls=%fused_computation.20 | custom fusion | flops 24576 | bytes 14336 | tf_op jit(solution)/shard_map/scatter-add | solution.py:77
  387.2 4.4 collective-permute-start.4
  396.5 39.9 %psum.45 = f32[]{:T(128)} all-reduce(f32[]{:T(128)} %multiply_reduce_fusion.5), channel_id=1, replica_groups=mesh['fluid'=4,'solid'=8] {'fluid','solid'}, use_global_device_ids=true, to_apply=%region_17.18 | all-reduce | flops 1 | bytes 8 | tf_op jit(solution)/shard_map/psum | solution.py:90
  439.0 40.1 %psum.46 = f32[]{:T(128)} all-reduce(f32[]{:T(128)} %get-tuple-element.66), channel_id=1, replica_groups=mesh['fluid'=4,'solid'=8] {'fluid','solid'}, use_global_device_ids=true, to_apply=%region_19.20 | all-reduce | flops 1 | bytes 8 | tf_op jit(solution)/shard_map/psum | solution.py:36
  485.1 27.7 %gather_fusion.2 = f32[8192,3]{1,0:T(8,128)} fusion(f32[3,1152]{0,1:T(8,128)S(1)} %copy.159, s32[8192]{0:T(1024)S(1)} %bitcast_clamp_fusion), kind=kCustom, calls=%fused_computation.2 | custom fusion | bytes 229376 | tf_op jit(solution)/shard_map/gather | solution.py:73
  512.8 2.9 copy.211
  518.8 44.4 %scatter_custom_fusion.4 = f32[3,1152]{0,1:T(8,128)S(1)} fusion(s32[8192]{0:T(1024)} %bitcast.112, f32[8192,3]{1,0:T(8,128)} %copy.161, f32[]{:T(128)} %constant.106.clone.1), kind=kCustom, calls=%fused_computation.18 | custom fusion | flops 24576 | bytes 14336 | tf_op jit(solution)/shard_map/scatter-add | solution.py:77
  563.3 4.4 collective-permute-start.6
  569.8 42.2 %psum.47 = f32[]{:T(128)} all-reduce(f32[]{:T(128)} %multiply_reduce_fusion.3), channel_id=1, replica_groups=mesh['fluid'=4,'solid'=8] {'fluid','solid'}, use_global_device_ids=true, to_apply=%region_22.23 | all-reduce | flops 1 | bytes 8 | tf_op jit(solution)/shard_map/psum | solution.py:90
  616.8 27.7 %gather_fusion.3 = f32[8192,3]{1,0:T(8,128)} fusion(f32[3,1152]{0,1:T(8,128)S(1)} %copy.165, s32[8192]{0:T(1024)S(1)} %bitcast_clamp_fusion), kind=kCustom, calls=%fused_computation.3 | custom fusion | bytes 229376 | tf_op jit(solution)/shard_map/gather | solution.py:73
  644.5 2.9 copy.166
  647.5 4.2 gather_fusion.4
  652.1 18.7 %all_to_all.19 = f32[32,80,24]{1,2,0:T(8,128)S(1)} all-to-all(f32[32,80,24]{1,2,0:T(8,128)S(1)} %copy.168), channel_id=1, replica_groups=mesh['fluid'=4,'solid'=8] {'fluid','solid'}, dimensions={0} | all-to-all | bytes 491520 | tf_op jit(solution)/shard_map/all_to_all | solution.py:102
  671.2 6.8 %gather_fusion.5 = f32[1024,24]{1,0:T(8,128)S(1)} fusion(f32[32,80,24]{2,1,0:T(8,128)S(1)} %copy.169, s32[1024]{0:T(1024)S(1)} %bitcast.83), kind=kCustom, calls=%fused_computation.5 | custom fusion | bytes 204800 | tf_op jit(solution)/shard_map/gather | solution.py:103
  (123 shorter events, 62.0 us)
Async XLA Ops:
  0.6 26.2 %copy-start = (f32[1024,128]{1,0:T(8,128)S(1)}, f32[1024,128]{1,0:T(8,128)}, u32[]{:S(2)}) copy-start(f32[1024,128]{1,0:T(8,128)} %param.15) | copy-start | bytes 1572868
  19.5 14.4 %all-to-all-start = ((f32[32,1,80]{2,1,0:T(1,128)}), f32[32,1,80]{2,1,0:T(1,128)S(1)}, u32[]{:S(2)}, u32[]{:S(2)}) async-start(f32[32,1,80]{2,1,0:T(1,128)} %all_to_all.12), calls=%async_computation | async-start | bytes 32768 | tf_op jit(solution)/shard_map/all_to_all | solution.py:63
  33.9 37.1 %copy-start.6 = (f32[32,1,80]{2,1,0:T(1,128)}, f32[32,1,80]{2,1,0:T(1,128)S(1)}, u32[]{:S(2)}) copy-start(f32[32,1,80]{2,1,0:T(1,128)S(1)} %all-to-all-done) | copy-start | bytes 30724
  33.9 18.6 %all-to-all-start.1 = ((f32[32,80,24]{1,2,0:T(8,128)}), f32[32,80,24]{1,2,0:T(8,128)S(1)}, u32[]{:S(2)}, u32[]{:S(2)}) async-start(f32[32,80,24]{1,2,0:T(8,128)} %copy.139), calls=%async_computation.1 | async-start | bytes 786432 | tf_op jit(solution)/shard_map/all_to_all | solution.py:62
  39.4 31.6 %copy-start.11 = (s32[8192,1]{0,1:T(1,128)}, s32[8192,1]{0,1:T(1,128)S(1)}, u32[]{:S(2)}) copy-start(s32[8192,1]{0,1:T(1,128)S(1)} %compare_select_fusion) | copy-start | bytes 98308
  71.0 89.3 %copy-start.1 = (f32[24,24,1024]{2,1,0:T(8,128)S(1)}, f32[24,24,1024]{2,1,0:T(8,128)}, u32[]{:S(2)}) copy-start(f32[24,24,1024]{2,1,0:T(8,128)} %param.19) | copy-start | bytes 7077892
  116.3 7.7 %collective-permute-start = (f32[3,128]{1,0:T(4,128)S(1)}, f32[3,128]{1,0:T(4,128)S(1)}, u32[]{:S(2)}, u32[]{:S(2)}) collective-permute-start(f32[3,128]{1,0:T(4,128)S(1)} %copy.196), channel_id=1, source_target_pairs={{0,1},{1,2},{2,3},{3,4},{4,5},{5,6},{6,7},{7,8},{8,9},{9,10},{10,1... | collective-permute-start | bytes 4616 | tf_op jit(solution)/shard_map/ppermute | solution.py:12
  124.6 3.6 collective-permute-start.1
  160.7 56.6 %copy-start.2 = (f32[3,1024]{1,0:T(4,128)S(1)}, f32[3,1024]{1,0:T(4,128)}, u32[]{:S(2)}) copy-start(f32[3,1024]{1,0:T(4,128)} %param.21) | copy-start | bytes 36868
  209.5 7.2 %collective-permute-start.2 = (f32[3,128]{1,0:T(4,128)S(1)}, f32[3,128]{1,0:T(4,128)S(1)}, u32[]{:S(2)}, u32[]{:S(2)}) collective-permute-start(f32[3,128]{1,0:T(4,128)S(1)} %copy.199), channel_id=1, source_target_pairs={{0,1},{1,2},{2,3},{3,4},{4,5},{5,6},{6,7},{7,8},{8,9},{9,10},{10,1... | collective-permute-start | bytes 4616 | tf_op jit(solution)/shard_map/ppermute | solution.py:12
  261.4 44.5 %copy-start.8 = (f32[3,1024]{1,0:T(4,128)}, f32[3,1024]{1,0:T(4,128)S(1)}, u32[]{:S(2)}) copy-start(f32[3,1024]{1,0:T(4,128)S(1)} %get-tuple-element.69) | copy-start | bytes 36868
  302.8 3.1 collective-permute-start.3
  387.2 7.4 %collective-permute-start.4 = (f32[3,128]{1,0:T(4,128)S(1)}, f32[3,128]{1,0:T(4,128)S(1)}, u32[]{:S(2)}, u32[]{:S(2)}) collective-permute-start(f32[3,128]{1,0:T(4,128)S(1)} %copy.202), channel_id=1, source_target_pairs={{0,1},{1,2},{2,3},{3,4},{4,5},{5,6},{6,7},{7,8},{8,9},{9,10},{10,1... | collective-permute-start | bytes 4616 | tf_op jit(solution)/shard_map/ppermute | solution.py:12
  480.4 3.1 copy-start.4
  480.4 3.1 collective-permute-start.5
  515.6 52.1 %copy-start.7 = (f32[32,1,80]{2,1,0:T(1,128)S(1)}, f32[32,1,80]{2,1,0:T(1,128)}, u32[]{:S(2)}) copy-start(f32[32,1,80]{2,1,0:T(1,128)} %copy-done.6) | copy-start | bytes 30724
  516.1 53.1 %copy-start.3 = (f32[3,1024]{1,0:T(4,128)S(1)}, f32[3,1024]{1,0:T(4,128)}, u32[]{:S(2)}) copy-start(f32[3,1024]{1,0:T(4,128)} %param.21) | copy-start | bytes 36868
  516.1 53.1 %copy-start.5 = (f32[3,1024]{1,0:T(4,128)S(1)}, f32[3,1024]{1,0:T(4,128)}, u32[]{:S(2)}) copy-start(f32[3,1024]{1,0:T(4,128)} %copy-done.4) | copy-start | bytes 36868
  563.3 5.2 collective-permute-start.6
  613.4 38.3 %copy-start.9 = (f32[3,1024]{1,0:T(4,128)}, f32[3,1024]{1,0:T(4,128)S(1)}, u32[]{:S(2)}) copy-start(f32[3,1024]{1,0:T(4,128)S(1)} %multiply_add_fusion) | copy-start | bytes 36868
  613.5 3.1 collective-permute-start.7
  652.1 25.9 %copy-start.10 = (f32[24,128]{1,0:T(8,128)S(1)}, f32[24,128]{1,0:T(8,128)}, u32[]{:S(2)}) copy-start(f32[24,128]{1,0:T(8,128)} %param.18) | copy-start | bytes 36868
where the time goes:
time: 681 us; the launch traced here: 679 us
  blocking collectives  223 us (33%)
  other arithmetic  220 us (32%)
  local copies, waits for them, and re-layouts  173 us (25%)
  starting transfers between devices  34.1 us (5%)
  waiting for transfers between devices  20.2 us (3%)
  between operations  7.74 us (1%)
    scatter-add x4, other arithmetic, assemble_terms(): totals = totals.at[:, connectivity.reshape(-1)].add(terms.reshape(3, -1))  178 us
    psum x3, blocking collectives, squares(): return lax.psum(jnp.sum(vector * vector), ('fluid', 'solid'))  122 us
    gather x5, local copies, waits for them, and re-layouts, element_values(): return extended[:, connectivity].reshape(24, elem_count)  114 us
    psum x2, blocking collectives, shards(): curving = lax.psum(jnp.sum(direction * image), ('fluid', 'solid'))  82.1 us
    unnamed x42, local copies, waits for them, and re-layouts  25.7 us
    ppermute x8, starting transfers between devices, from_behind(): lax.ppermute(value, axis, [(source, source + steps) for source in range(f...  21.4 us
    all_to_all x1, blocking collectives, shards(): lax.all_to_all(leaving, ('fluid', 'solid'), split_axis=0, concat_axis=0,...  18.7 us
    scatter-add x1, other arithmetic, shards(): jax.ops.segment_sum(arrived_rows, element_ids, num_segments=elem_count)  15.2 us
  transfers between devices with their start and end apart: 10, of which 7 were waited for; matrix products, arithmetic and copies ran while one was open for 3% of the time, Pallas kernels for 0%

commit v1 on v0

v1 whole, which is shorter than its diff:
```python
import functools

import jax
import jax.numpy as jnp
from jax import lax
from jax.experimental import pallas as pl
from jax.experimental.pallas import tpu as pltpu
from jax.sharding import PartitionSpec as P

AXES = ("fluid", "solid")
DOF = 24
CORNERS = 8
GROUPS = 5
ROWS_PER_FIELD = 8
WIDE = 256
VMEM_BYTES = 24 * 1024 * 1024
F32 = jnp.float32
BF16 = jnp.bfloat16


def iota(shape, axis):
    return lax.broadcasted_iota(jnp.int32, shape, axis)


def onehot(mask):
    return jnp.where(mask, 1.0, 0.0).astype(BF16)


def split(value):
    high = value.astype(BF16)
    return high, (value - high.astype(F32)).astype(BF16)


def dot_nt(left, right):
    return lax.dot_general(left, right, (((1,), (1,)), ((), ())), preferred_element_type=F32)


def dot_nn(left, right):
    return lax.dot_general(left, right, (((1,), (0,)), ((), ())), preferred_element_type=F32)


def take_lanes(table, index):
    return jnp.take_along_axis(table, index, axis=1, mode="promise_in_bounds")


def group_rows(group, sections, tail):
    kept = [jnp.where(group == i, section, 0.0) for i, section in enumerate(sections)]
    return jnp.concatenate(kept + [tail], axis=0)


def gather_corners(field, connectivity):
    elements = connectivity.shape[1]
    rows = {}
    for c in range(3):
        for h in range(9):
            row = field[c * ROWS_PER_FIELD + h // 2:c * ROWS_PER_FIELD + h // 2 + 1, (h % 2) * 128:(h % 2) * 128 + 128]
            rows[c, h] = jnp.broadcast_to(row, (CORNERS, 128))
    parts = [[], [], []]
    for start in range(0, elements, 128):
        index = connectivity[:, start:start + 128]
        low, high = index & 127, index >> 7
        masks = [high == h for h in range(9)]
        for c in range(3):
            total = jnp.zeros((CORNERS, 128), F32)
            for h in range(9):
                total = jnp.where(masks[h], take_lanes(rows[c, h], low), total)
            parts[c].append(total)
    return [jnp.concatenate(part, axis=1) for part in parts]


def assemble(terms, connectivity):
    elements = connectivity.shape[1]
    high, low = connectivity >> 8, connectivity & 255
    upper = terms.astype(BF16).astype(F32)
    lower = terms - upper
    total = jnp.zeros((2 * DOF, WIDE), F32)
    for k in range(CORNERS):
        mask = iota((ROWS_PER_FIELD, elements), 0) == high[k:k + 1]
        pieces = [
            jnp.where(mask, part[c * CORNERS + k:c * CORNERS + k + 1], 0.0)
            for part in (upper, lower)
            for c in range(3)
        ]
        left = jnp.concatenate(pieces, axis=0).astype(BF16)
        right = onehot(iota((WIDE, elements), 0) == low[k:k + 1])
        total = total + dot_nt(left, right)
    return total[:DOF] + total[DOF:]


def matvec(stiffness, values):
    elements = stiffness.shape[2]
    parts = []
    for start in range(0, elements, 128):
        total = jnp.zeros((DOF, 128), F32)
        for b in range(DOF):
            total = total + stiffness[b, :, start:start + 128] * values[b // 8][b % 8:b % 8 + 1, start:start + 128]
        parts.append(total)
    return jnp.concatenate(parts, axis=1)


def rim_rows(field, h):
    return [field[c * ROWS_PER_FIELD + h:c * ROWS_PER_FIELD + h + 1, :128] for c in range(3)]


def put_ends(partial, odd, own_rows, swap_a_ref, swap_b_ref):
    first = jnp.concatenate(rim_rows(partial, 0) + [jnp.zeros((5, 128), F32)], axis=0)
    over = jnp.concatenate(rim_rows(partial, own_rows) + [jnp.zeros((5, 128), F32)], axis=0)
    swap_a_ref[...] = jnp.where(odd, first, over)
    swap_b_ref[...] = jnp.where(odd, over, first)


def add_ends(partial, odd, own_rows, swap_a, swap_b):
    before = jnp.where(odd, swap_a, swap_b)
    after = jnp.where(odd, swap_b, swap_a)
    pad = jnp.zeros((1, WIDE - 128), F32)
    none = jnp.zeros((1, WIDE), F32)
    rows = []
    for c in range(3):
        for h in range(ROWS_PER_FIELD):
            if h == 0:
                rows.append(jnp.concatenate([before[c:c + 1], pad], axis=1))
            elif h == own_rows:
                rows.append(jnp.concatenate([after[c:c + 1], pad], axis=1))
            else:
                rows.append(none)
    return partial + jnp.concatenate(rows, axis=0)


def own_mask(own_rows):
    return (iota((DOF, WIDE), 0) % ROWS_PER_FIELD) < own_rows


def as_field(rows, own_rows):
    pieces = []
    for c in range(3):
        pieces += [rows[c:c + 1, h * WIDE:(h + 1) * WIDE] for h in range(own_rows)]
        pieces.append(jnp.zeros((ROWS_PER_FIELD - own_rows, WIDE), F32))
    return jnp.concatenate(pieces, axis=0)


def send_kernel(devices, per, pressure_ref, owner_ref, element_ref, table_ref, support_ref, stiffness_ref,
                out_ref, place_ref, diagonal_ref, sems):
    copies = [
        pltpu.make_async_copy(
            stiffness_ref.at[pl.ds(8 * i, 8), pl.ds(8 * i, 8)], diagonal_ref.at[i], sems.at[i])
        for i in range(3)
    ]
    for copy in copies:
        copy.start()
    faces = pressure_ref.shape[0]
    target, element = owner_ref[...], element_ref[...]
    named = iota((devices, faces), 0) == target
    named16 = onehot(named)
    upto = onehot(iota((WIDE, WIDE), 0) <= iota((WIDE, WIDE), 1))
    before = jnp.zeros((devices, 1), F32)
    ranks = []
    for start in range(0, faces, WIDE):
        counts = dot_nn(named16[:, start:start + WIDE], upto) + before
        ranks.append(jnp.sum(jnp.where(named[:, start:start + WIDE], counts, 0.0), axis=0, keepdims=True))
        before = counts[:, WIDE - 1:]
    rank = jnp.concatenate(ranks, axis=1).astype(jnp.int32) - 1
    group = jnp.zeros_like(rank)
    for i in range(1, GROUPS):
        group = group + (rank >= i * per).astype(jnp.int32)
    place = target * per + rank - group * per
    place_ref[...] = jnp.concatenate([place, group, jnp.zeros((6, faces), jnp.int32)], axis=0)

    table = jnp.concatenate([table_ref[...]] * GROUPS + [jnp.zeros((8, table_ref.shape[1]), F32)], axis=0)
    table_high, table_low = split(table)
    rows_high, rows_low = split(pressure_ref[...])
    projected = dot_nt(
        jnp.concatenate([table_high, table_low, table_high], axis=1),
        jnp.concatenate([rows_high, rows_high, rows_low], axis=1),
    )
    codes = jnp.where(iota((8, faces), 0) == group, element.astype(F32), 0.0)
    spread = group_rows(group, [projected[i * DOF:(i + 1) * DOF] for i in range(GROUPS)], codes)
    spread_high, spread_low = split(spread)
    chosen = onehot(iota((devices * per, faces), 0) == place)
    sent = dot_nt(chosen, jnp.concatenate([spread_high, spread_low], axis=0))

    for copy in copies:
        copy.wait()
    trace = jnp.zeros((8, faces), F32)
    for i in range(3):
        for j in range(8):
            trace = trace + jnp.where(iota((8, faces), 0) == j, diagonal_ref[i, j], 0.0)
    trace = jnp.sum(trace) + jnp.sum(support_ref[...])
    out_ref[...] = jnp.where(iota((devices * per, 128), 1) == 125, trace, sent[:, :128] + sent[:, 128:])


def load_kernel(devices, per, odd_ref, rows_ref, connectivity_ref, support_ref,
                partial_ref, swap_a_ref, swap_b_ref, weight_ref, scale_ref, code_ref):
    nodes = support_ref.shape[1]
    own_rows = nodes // WIDE
    rows = rows_ref[...]
    arrived = rows.T
    codes = arrived[GROUPS * DOF:].astype(jnp.int32)
    code_ref[...] = codes
    slots = rows.shape[0]
    total = jnp.zeros((4 * 2 * DOF, WIDE), F32)
    for g in range(GROUPS):
        terms = arrived[g * DOF:(g + 1) * DOF]
        upper = terms.astype(BF16).astype(F32)
        both = jnp.concatenate([upper, terms - upper], axis=0)
        code = codes[g:g + 1]
        left = jnp.concatenate([jnp.where((code >> 8) == i, both, 0.0) for i in range(4)], axis=0).astype(BF16)
        right = onehot(iota((WIDE, slots), 0) == (code & 255))
        total = total + dot_nt(left, right)
    loads = jnp.concatenate(
        [total[i * 2 * DOF:i * 2 * DOF + DOF] + total[i * 2 * DOF + DOF:(i + 1) * 2 * DOF] for i in range(4)], axis=1)
    partial = assemble(loads, connectivity_ref[...])
    partial_ref[...] = partial
    put_ends(partial, odd_ref[0] == 1, own_rows, swap_a_ref, swap_b_ref)
    trace = jnp.sum(rows[:, 125:126]) * (1.0 / per)
    inverse = jnp.full((8, 128), 3.0 * nodes * devices, F32) / jnp.full((8, 128), trace, F32)
    scale_ref[...] = inverse
    weight = as_field(support_ref[...], own_rows) * inverse[:1, :1] - 1.0
    weight_ref[...] = jnp.where(own_mask(own_rows), weight, 0.0)


def product_kernel(own_rows, odd_ref, partial_ref, swap_a_in, swap_b_in, weight_ref, scale_ref, connectivity_ref,
                   stiffness_ref, field_ref, next_ref, swap_a_ref, swap_b_ref):
    odd = odd_ref[0] == 1
    field = add_ends(partial_ref[...], odd, own_rows, swap_a_in[...], swap_b_in[...])
    field_ref[...] = field
    connectivity = connectivity_ref[...]
    forces = matvec(stiffness_ref, gather_corners(field, connectivity))
    partial = assemble(forces, connectivity) * scale_ref[:1, :1] + weight_ref[...] * field
    next_ref[...] = partial
    put_ends(partial, odd, own_rows, swap_a_ref, swap_b_ref)


def moment_kernel(own_rows, devices, odd_ref, partial_ref, swap_a_in, swap_b_in, weight_ref, scale_ref,
                  connectivity_ref, stiffness_ref, first_ref, second_ref, field_ref, moments_ref):
    odd = odd_ref[0] == 1
    third = add_ends(partial_ref[...], odd, own_rows, swap_a_in[...], swap_b_in[...])
    field_ref[...] = third
    values = gather_corners(third, connectivity_ref[...])
    forces = matvec(stiffness_ref, values)
    energy = jnp.sum(forces * jnp.concatenate(values, axis=0), axis=0, keepdims=True)
    own = own_mask(own_rows)
    first, second = jnp.where(own, first_ref[...], 0.0), jnp.where(own, second_ref[...], 0.0)
    owned = jnp.where(own, third, 0.0)
    moments = [
        jnp.sum(first * first),
        jnp.sum(first * second),
        jnp.sum(second * second),
        jnp.sum(second * owned),
        jnp.sum(owned * owned),
        jnp.sum(energy) * scale_ref[:1, :1] + jnp.sum(weight_ref[...] * owned * owned),
    ]
    lane = iota((devices, 128), 1)
    row = jnp.zeros((devices, 128), F32)
    for i, moment in enumerate(moments):
        row = jnp.where(lane == i, moment, row)
    moments_ref[...] = row


def step_weights(m):
    def dot(p, q):
        terms = [p[i] * q[j] * m[i + j] for i in range(3) for j in range(3) if p[i] is not None and q[j] is not None]
        return functools.reduce(lambda a, b: a + b, terms)

    def energy(p):
        terms = [p[i] * p[j] * (m[i + j + 1] + m[i + j]) for i in range(3) for j in range(3)
                 if p[i] is not None and p[j] is not None]
        return functools.reduce(lambda a, b: a + b, terms)

    norm0 = m[0]
    curve0 = m[0] + m[1]
    step0 = norm0 / curve0
    residual = [m[1] / curve0, -step0, None]
    norm1 = dot(residual, residual)
    turn0 = norm1 / norm0
    direction = [residual[0] + turn0, residual[1], None]
    step1 = norm1 / energy(direction)
    result = [step0 + step1 * direction[0], step1 * direction[1]]
    residual = [
        residual[0] - step1 * direction[0],
        residual[1] - step1 * (direction[0] + direction[1]),
        -step1 * direction[1],
    ]
    norm2 = dot(residual, residual)
    turn1 = norm2 / norm1
    direction = [residual[0] + turn1 * direction[0], residual[1] + turn1 * direction[1], residual[2]]
    step2 = norm2 / energy(direction)
    return [result[0] + step2 * direction[0], result[1] + step2 * direction[1], step2 * direction[2]]


def pick_kernel(own_rows, moments_ref, scale_ref, first_ref, second_ref, third_ref, connectivity_ref, code_ref,
                displacement_ref, out_ref):
    sums = jnp.sum(moments_ref[...], axis=0, keepdims=True)
    weights = step_weights([sums[:, i:i + 1] for i in range(6)])
    scale = scale_ref[:1, :1]
    field = (
        (weights[0] * scale) * first_ref[...]
        + (weights[1] * scale) * second_ref[...]
        + (weights[2] * scale) * third_ref[...]
    )
    for c in range(3):
        for h in range(own_rows):
            displacement_ref[c:c + 1, h * WIDE:(h + 1) * WIDE] = (
                field[c * ROWS_PER_FIELD + h:c * ROWS_PER_FIELD + h + 1])
    values = gather_corners(field, connectivity_ref[...])
    slots = code_ref.shape[1]
    tiles = []
    for start in range(0, slots, 128):
        sections = []
        for g in range(GROUPS):
            code = jnp.broadcast_to(code_ref[g:g + 1, start:start + 128], (8, 128))
            low, high = code & 127, code >> 7
            masks = [high == i for i in range(8)]
            for c in range(3):
                total = jnp.zeros((8, 128), F32)
                for i in range(8):
                    total = jnp.where(masks[i], take_lanes(values[c][:, i * 128:(i + 1) * 128], low), total)
                sections.append(total)
        sections.append(jnp.zeros((8, 128), F32))
        tiles.append(jnp.concatenate(sections, axis=0).T)
    out_ref[...] = jnp.concatenate(tiles, axis=0)


def motion_kernel(rows_ref, place_ref, table_ref, out_ref):
    returned = rows_ref[...].T
    high, low = split(returned)
    slots = returned.shape[1]
    place, group = place_ref[0:1], place_ref[1:2]
    faces = place.shape[1]
    chosen = onehot(iota((slots, faces), 0) == place)
    found = dot_nn(jnp.concatenate([high, low], axis=0), chosen)
    found = found[:128] + found[128:]
    owned = jnp.zeros((DOF, faces), F32)
    for i in range(GROUPS):
        owned = jnp.where(group == i, found[i * DOF:(i + 1) * DOF], owned)
    upper = owned.astype(BF16).astype(F32)
    lower = owned - upper
    left = jnp.concatenate([upper, lower, upper], axis=0).T.astype(BF16)
    table_high, table_low = split(table_ref[...])
    out_ref[...] = dot_nn(left, jnp.concatenate([table_high, table_high, table_low], axis=0))


def call(kernel, outs, args, scalars=0, hbm=(), scratch=()):
    in_specs = []
    for i in range(len(args)):
        if i < scalars:
            in_specs.append(pl.BlockSpec(memory_space=pltpu.SMEM))
        elif i in hbm:
            in_specs.append(pl.BlockSpec(memory_space=pl.ANY))
        else:
            in_specs.append(pl.BlockSpec(memory_space=pltpu.VMEM))
    return pl.pallas_call(
        kernel,
        out_shape=[jax.ShapeDtypeStruct(shape, dtype) for shape, dtype in outs],
        in_specs=in_specs,
        out_specs=[pl.BlockSpec(memory_space=pltpu.VMEM)] * len(outs),
        scratch_shapes=list(scratch),
        compiler_params=pltpu.CompilerParams(vmem_limit_bytes=VMEM_BYTES),
    )(*args)


def shards(pressure, face_owner, face_element, shape_table, stiffness, connectivity, support):
    devices = lax.axis_size(AXES)
    faces = pressure.shape[0]
    elements = stiffness.shape[2]
    nodes = support.shape[1]
    own_rows = nodes // WIDE
    capacity = max(2, (5 * faces + 2 * devices - 1) // (2 * devices))
    per = (capacity + GROUPS - 1) // GROUPS
    slots = devices * per
    odd = (lax.axis_index(AXES) % 2).astype(jnp.int32).reshape(1)
    evens = [(i, i + 1) for i in range(0, devices - 1, 2)]
    odds = [(i, i + 1) for i in range(1, devices - 1, 2)]
    pairs_a = evens + [(j, i) for i, j in evens]
    pairs_b = odds + [(j, i) for i, j in odds]

    def swap(a, b):
        return lax.ppermute(a, AXES, pairs_a), lax.ppermute(b, AXES, pairs_b)

    def everywhere(rows):
        return lax.all_to_all(rows, AXES, split_axis=0, concat_axis=0, tiled=True)

    field = ((DOF, WIDE), F32)
    ends = ((8, 128), F32)
    sent, place = call(
        functools.partial(send_kernel, devices, per),
        [((slots, 128), F32), ((8, faces), jnp.int32)],
        (pressure, face_owner.reshape(1, faces), face_element.reshape(1, faces), shape_table, support, stiffness),
        hbm=(5,),
        scratch=(pltpu.VMEM((3, 8, 8, elements), F32), pltpu.SemaphoreType.DMA((3,))),
    )
    arrived = everywhere(sent)
    partial, end_a, end_b, weight, scale, codes = call(
        functools.partial(load_kernel, devices, per),
        [field, ends, ends, field, ends, ((8, slots), jnp.int32)],
        (odd, arrived, connectivity, support),
        scalars=1,
    )
    fields = []
    for _ in range(2):
        end_a, end_b = swap(end_a, end_b)
        full, partial, end_a, end_b = call(
            functools.partial(product_kernel, own_rows),
            [field, field, ends, ends],
            (odd, partial, end_a, end_b, weight, scale, connectivity, stiffness),
            scalars=1,
        )
        fields.append(full)
    end_a, end_b = swap(end_a, end_b)
    third, moments = call(
        functools.partial(moment_kernel, own_rows, devices),
        [field, ((devices, 128), F32)],
        (odd, partial, end_a, end_b, weight, scale, connectivity, stiffness, fields[0], fields[1]),
        scalars=1,
    )
    moments = everywhere(moments)
    displacement, leaving = call(
        functools.partial(pick_kernel, own_rows),
        [((3, nodes), F32), ((slots, 128), F32)],
        (moments, scale, fields[0], fields[1], third, connectivity, codes),
    )
    returned = everywhere(leaving)
    (face_motion,) = call(motion_kernel, [((faces, 128), F32)], (returned, place, shape_table))
    return displacement, face_motion


def solution(mesh):
    in_specs = (
        P(AXES, None),
        P(AXES, None),
        P(AXES),
        P(),
        P(None, None, AXES),
        P(None, AXES),
        P(None, AXES),
    )
    out_specs = (P(None, AXES), P(AXES, None))
    return jax.shard_map(shards, mesh=mesh, in_specs=in_specs, out_specs=out_specs, check_vma=False)
```

time: 681 us -> 77.4 us (0.11)
  other arithmetic: 220 us -> 0 us
  blocking collectives: 223 us -> 30 us
  local copies, waits for them, and re-layouts: 173 us -> 5.51 us
  starting transfers between devices: 34.1 us -> 17.8 us
  Pallas kernels: 0 us -> 11.4 us
  waiting for transfers between devices: 20.2 us -> 11.4 us
  between operations: 7.74 us -> 0.75 us
    psum x5 -> x0, blocking collectives: 204 us -> none  [the longest x3 122 us: squares(): return lax.psum(jnp.sum(vector * vector), ('fluid', 'solid'))]
    scatter-add x9 -> x0, other arithmetic: 196 us -> none  [the longest x4 178 us: assemble_terms(): totals = totals.at[:, connectivity.reshape(-1)].add(terms.reshape(3, -1))]
    gather x7 -> x0, local copies, waits for them, and re-layouts: 125 us -> none  [the longest x5 114 us: element_values(): return extended[:, connectivity].reshape(24, elem_count)]
    unnamed x42 -> x20, local copies, waits for them, and re-layouts: 25.7 us -> 5.51 us
    reshape x11 -> x0, local copies, waits for them, and re-layouts: 11.8 us -> none  [the longest x8 10.8 us: assemble_terms(): totals = totals.at[:, connectivity.reshape(-1)].add(terms.reshape(3, -1))]
    pallas_call x0 -> x7, Pallas kernels: none -> 11.4 us  [call(): pl.pallas_call(kernel, out_shape=[jax.ShapeDtypeStruct(shape, dtype) for...]
    all_to_all x1 -> x2, blocking collectives: 18.7 us -> 30 us  [everywhere(): return lax.all_to_all(rows, AXES, split_axis=0, concat_axis=0, tiled=True)]
    ppermute x8 -> x6, starting transfers between devices: 21.4 us -> 10.5 us  [swap(): return (lax.ppermute(a, AXES, pairs_a), lax.ppermute(b, AXES, pairs_b))]
  transfers between devices with their start and end apart: 10 -> 7, of which waited for: 7 -> 4; matrix products, arithmetic and copies ran while one was open for 3% -> 0% of each run, Pallas kernels for 0% -> 0%
where the time goes in v1:
time: 77.4 us; the launch traced here: 76.9 us
  blocking collectives  30 us (39%)
  starting transfers between devices  17.8 us (23%)
  Pallas kernels  11.4 us (15%)
  waiting for transfers between devices  11.4 us (15%)
  local copies, waits for them, and re-layouts  5.51 us (7%)
    all_to_all x2, blocking collectives, everywhere(): return lax.all_to_all(rows, AXES, split_axis=0, concat_axis=0, tiled=True)  30 us
    pallas_call x7, Pallas kernels, call(): pl.pallas_call(kernel, out_shape=[jax.ShapeDtypeStruct(shape, dtype) for...  11.4 us
    all_to_all x1, waiting for transfers between devices, everywhere(): return lax.all_to_all(rows, AXES, split_axis=0, concat_axis=0, tiled=True)  10.6 us
    ppermute x6, starting transfers between devices, swap(): return (lax.ppermute(a, AXES, pairs_a), lax.ppermute(b, AXES, pairs_b))  10.5 us
    all_to_all x1, starting transfers between devices, everywhere(): return lax.all_to_all(rows, AXES, split_axis=0, concat_axis=0, tiled=True)  7.3 us
    unnamed x20, local copies, waits for them, and re-layouts  5.51 us
  transfers between devices with their start and end apart: 7, of which 4 were waited for; matrix products, arithmetic and copies ran while one was open for 0% of the time, Pallas kernels for 0%

profile of v1, /device:TPU:0, one launch (start us, length us, event | category | flops | bytes accessed | tf_op | source)
XLA Modules:
  0.0 76.9 jit_solution(12120576447780062726)
XLA Ops:
  0.6 0.0 copy-start
  0.6 1.7 %copy-done = f32[24,24,1024]{2,1,0:T(8,128)S(1)} copy-done((f32[24,24,1024]{2,1,0:T(8,128)S(1)}, f32[24,24,1024]{2,1,0:T(8,128)}, u32[]{:S(2)}) %copy-start) | copy-done | bytes 2359320
  2.3 1.0 %copy-done.3 = f32[1024,128]{1,0:T(8,128)S(1)} copy-done((f32[1024,128]{1,0:T(8,128)S(1)}, f32[1024,128]{1,0:T(8,128)}, u32[]{:S(2)}) %copy-start.3) | copy-done | bytes 524312
  3.3 0.7 copy-done.4
  4.1 0.7 copy-done.6
  4.8 0.7 copy-done.8
  5.5 0.7 copy-done.9
  6.1 1.9 %shard_map.86 = (f32[512,128]{1,0:T(8,128)}, s32[8,1024]{1,0:T(8,128)S(1)}) custom-call(f32[1024,128]{1,0:T(8,128)S(1)} %copy-done.3, s32[1,1024]{1,0:T(1,128)S(1)} %bitcast.16, s32[1,1024]{1,0:T(1,128)S(1)} %bitcast.17, f32[24,128]{1,0:T(8,128)S(1)} %copy-done.6, f32[3,1024]{1,0:T(4,128)S(1)} %copy-done.4, f32[24,24,1024]{2,1,0:T(8,128)S(1)} %copy-done), custom_call_target="tpu_custom_call" | custom-call | tf_op jit(solution)/shard_map/pallas_call | solution.py:351
  8.1 7.3 %all-to-all-start = ((f32[32,16,128]{2,1,0:T(8,128)}), f32[32,16,128]{2,1,0:T(8,128)S(1)}, u32[]{:S(2)}, u32[]{:S(2)}) async-start(f32[32,16,128]{2,1,0:T(8,128)} %bitcast.3), calls=%async_computation | async-start | bytes 524288 | tf_op jit(solution)/shard_map/all_to_all | solution.py:380
  15.4 10.6 %all-to-all-done = f32[32,16,128]{2,1,0:T(8,128)S(1)} async-done(((f32[32,16,128]{2,1,0:T(8,128)}), f32[32,16,128]{2,1,0:T(8,128)S(1)}, u32[]{:S(2)}, u32[]{:S(2)}) %all-to-all-start) | async-done | bytes 262176 | tf_op jit(solution)/shard_map/all_to_all | solution.py:380
  26.0 0.0 copy-done.2
  26.0 2.4 %shard_map.87 = (f32[24,256]{1,0:T(8,128)S(1)}, f32[8,128]{1,0:T(8,128)S(1)}, f32[8,128]{1,0:T(8,128)S(1)}, f32[24,256]{1,0:T(8,128)S(1)}, f32[8,128]{1,0:T(8,128)S(1)}, /*index=5*/s32[8,512]{1,0:T(8,128)S(1)}) custom-call(s32[1]{0:T(128)} %bitcast.odd_ref, f32[512,128]{1,0:T(8,128)S(1)} %bitcast.12, s32[8,1024]{1,0:T(8,128)S(1)} %copy-done.2, ...), custom_call_target="tpu_custom_call" | custom-call | tf_op jit(solution)/shard_map/pallas_call | solution.py:351
  28.4 0.1 collective-permute-start
  28.5 0.7 collective-permute-start.1
  29.2 0.5 collective-permute-done.swap_a_in
  29.7 0.0 collective-permute-done.1.swap_b_in
  29.7 1.6 %shard_map.88 = (f32[24,256]{1,0:T(8,128)S(1)}, f32[24,256]{1,0:T(8,128)S(1)}, f32[8,128]{1,0:T(8,128)S(1)}, f32[8,128]{1,0:T(8,128)S(1)}) custom-call(s32[1]{0:T(128)} %bitcast.odd_ref, f32[24,256]{1,0:T(8,128)S(1)} %get-tuple-element.23.partial_ref, f32[8,128]{1,0:T(8,128)S(1)} %collective-permute-done.swap_a_in, ...), custom_call_target="tpu_custom_call" | custom-call | tf_op jit(solution)/shard_map/pallas_call | solution.py:351
  31.3 4.3 %collective-permute-start.2 = (f32[8,128]{1,0:T(8,128)S(1)}, f32[8,128]{1,0:T(8,128)S(1)}, u32[]{:S(2)}, u32[]{:S(2)}) collective-permute-start(f32[8,128]{1,0:T(8,128)S(1)} %get-tuple-element.29), channel_id=1, source_target_pairs={{0,1},{2,3},{4,5},{6,7},{8,9},{10,11},{12,13},{14,15},{16,17},{18,... | collective-permute-start | bytes 12296 | tf_op jit(solution)/shard_map/ppermute | solution.py:377
  35.6 0.6 collective-permute-start.3
  36.3 0.2 collective-permute-done.2.swap_a_in
  36.4 0.0 collective-permute-done.3.swap_b_in
  36.4 1.6 %shard_map.89 = (f32[24,256]{1,0:T(8,128)S(1)}, f32[24,256]{1,0:T(8,128)S(1)}, f32[8,128]{1,0:T(8,128)S(1)}, f32[8,128]{1,0:T(8,128)S(1)}) custom-call(s32[1]{0:T(128)} %bitcast.odd_ref, f32[24,256]{1,0:T(8,128)S(1)} %get-tuple-element.28.partial_ref, f32[8,128]{1,0:T(8,128)S(1)} %collective-permute-done.2.swap_a_in, ...), custom_call_target="tpu_custom_call" | custom-call | tf_op jit(solution)/shard_map/pallas_call | solution.py:351
  38.1 4.2 %collective-permute-start.4 = (f32[8,128]{1,0:T(8,128)S(1)}, f32[8,128]{1,0:T(8,128)S(1)}, u32[]{:S(2)}, u32[]{:S(2)}) collective-permute-start(f32[8,128]{1,0:T(8,128)S(1)} %get-tuple-element.32), channel_id=1, source_target_pairs={{0,1},{2,3},{4,5},{6,7},{8,9},{10,11},{12,13},{14,15},{16,17},{18,... | collective-permute-start | bytes 12296 | tf_op jit(solution)/shard_map/ppermute | solution.py:377
  42.3 0.6 collective-permute-start.5
  42.9 0.2 collective-permute-done.4.swap_a_in
  43.1 0.0 collective-permute-done.5.swap_b_in
  43.1 0.6 shard_map.90
  43.7 17.7 %all_to_all.33 = f32[32,1,128]{2,1,0:T(1,128)S(1)} all-to-all(f32[32,1,128]{2,1,0:T(1,128)S(1)} %bitcast.15), channel_id=1, replica_groups=mesh['fluid'=4,'solid'=8] {'fluid','solid'}, dimensions={0} | all-to-all | bytes 32768 | tf_op jit(solution)/shard_map/all_to_all | solution.py:380
  61.4 1.7 %shard_map.91 = (f32[3,1024]{1,0:T(4,128)}, f32[512,128]{1,0:T(8,128)S(1)}) custom-call(f32[32,128]{1,0:T(8,128)S(1)} %bitcast.14, f32[8,128]{1,0:T(8,128)S(1)} %get-tuple-element.27.scale_ref, f32[24,256]{1,0:T(8,128)S(1)} %get-tuple-element.34.first_ref, f32[24,256]{1,0:T(8,128)S(1)} %get-tuple-element.35.second_ref, ...), custom_call_target="tpu_custom_call" | custom-call | tf_op jit(solution)/shard_map/pallas_call | solution.py:351
  63.0 12.3 %all_to_all.34 = f32[32,16,128]{2,1,0:T(8,128)S(1)} all-to-all(f32[32,16,128]{2,1,0:T(8,128)S(1)} %bitcast.13), channel_id=1, replica_groups=mesh['fluid'=4,'solid'=8] {'fluid','solid'}, dimensions={0} | all-to-all | bytes 524288 | tf_op jit(solution)/shard_map/all_to_all | solution.py:380
  75.3 0.0 copy-done.7
  75.3 1.6 %shard_map.92 = f32[1024,128]{1,0:T(8,128)} custom-call(f32[512,128]{1,0:T(8,128)S(1)} %bitcast.11, s32[8,1024]{1,0:T(8,128)S(1)} %get-tuple-element.41.place_ref, f32[24,128]{1,0:T(8,128)S(1)} %copy-done.7), custom_call_target="tpu_custom_call" | custom-call | tf_op jit(solution)/shard_map/pallas_call | solution.py:351
  (11 shorter events, 0.0 us)
Async XLA Ops:
  0.6 1.7 %copy-start = (f32[24,24,1024]{2,1,0:T(8,128)S(1)}, f32[24,24,1024]{2,1,0:T(8,128)}, u32[]{:S(2)}) copy-start(f32[24,24,1024]{2,1,0:T(8,128)} %stiffness_ref.7) | copy-start | bytes 7077892
  2.3 1.0 %copy-start.3 = (f32[1024,128]{1,0:T(8,128)S(1)}, f32[1024,128]{1,0:T(8,128)}, u32[]{:S(2)}) copy-start(f32[1024,128]{1,0:T(8,128)} %pressure_ref.1) | copy-start | bytes 1572868
  3.3 0.7 copy-start.4
  4.1 0.7 copy-start.6
  4.8 0.7 copy-start.8
  5.5 0.7 copy-start.9
  6.1 19.8 %copy-start.2 = (s32[8,1024]{1,0:T(8,128)S(1)}, s32[8,1024]{1,0:T(8,128)}, u32[]{:S(2)}) copy-start(s32[8,1024]{1,0:T(8,128)} %connectivity_ref.9) | copy-start | bytes 98308
  6.1 19.8 %copy-start.5 = (f32[3,1024]{1,0:T(4,128)S(1)}, f32[3,1024]{1,0:T(4,128)}, u32[]{:S(2)}) copy-start(f32[3,1024]{1,0:T(4,128)} %support_ref.3) | copy-start | bytes 36868
  6.1 23.5 %copy-start.1 = (f32[24,24,1024]{2,1,0:T(8,128)S(1)}, f32[24,24,1024]{2,1,0:T(8,128)}, u32[]{:S(2)}) copy-start(f32[24,24,1024]{2,1,0:T(8,128)} %stiffness_ref.7) | copy-start | bytes 7077892
  8.1 17.9 %all-to-all-start = ((f32[32,16,128]{2,1,0:T(8,128)}), f32[32,16,128]{2,1,0:T(8,128)S(1)}, u32[]{:S(2)}, u32[]{:S(2)}) async-start(f32[32,16,128]{2,1,0:T(8,128)} %bitcast.3), calls=%async_computation | async-start | bytes 524288 | tf_op jit(solution)/shard_map/all_to_all | solution.py:380
  28.4 1.2 %collective-permute-start = (f32[8,128]{1,0:T(8,128)S(1)}, f32[8,128]{1,0:T(8,128)S(1)}, u32[]{:S(2)}, u32[]{:S(2)}) collective-permute-start(f32[8,128]{1,0:T(8,128)S(1)} %get-tuple-element.24), channel_id=1, source_target_pairs={{0,1},{2,3},{4,5},{6,7},{8,9},{10,11},{12,13},{14,15},{16,17},{18,... | collective-permute-start | bytes 12296 | tf_op jit(solution)/shard_map/ppermute | solution.py:377
  28.5 1.2 %collective-permute-start.1 = (f32[8,128]{1,0:T(8,128)S(1)}, f32[8,128]{1,0:T(8,128)S(1)}, u32[]{:S(2)}, u32[]{:S(2)}) collective-permute-start(f32[8,128]{1,0:T(8,128)S(1)} %get-tuple-element.25), channel_id=1, source_target_pairs={{1,2},{3,4},{5,6},{7,8},{9,10},{11,12},{13,14},{15,16},{17,18},{19... | collective-permute-start | bytes 12296 | tf_op jit(solution)/shard_map/ppermute | solution.py:377
  31.3 5.1 %collective-permute-start.2 = (f32[8,128]{1,0:T(8,128)S(1)}, f32[8,128]{1,0:T(8,128)S(1)}, u32[]{:S(2)}, u32[]{:S(2)}) collective-permute-start(f32[8,128]{1,0:T(8,128)S(1)} %get-tuple-element.29), channel_id=1, source_target_pairs={{0,1},{2,3},{4,5},{6,7},{8,9},{10,11},{12,13},{14,15},{16,17},{18,... | collective-permute-start | bytes 12296 | tf_op jit(solution)/shard_map/ppermute | solution.py:377
  35.6 0.8 %collective-permute-start.3 = (f32[8,128]{1,0:T(8,128)S(1)}, f32[8,128]{1,0:T(8,128)S(1)}, u32[]{:S(2)}, u32[]{:S(2)}) collective-permute-start(f32[8,128]{1,0:T(8,128)S(1)} %get-tuple-element.30), channel_id=1, source_target_pairs={{1,2},{3,4},{5,6},{7,8},{9,10},{11,12},{13,14},{15,16},{17,18},{19... | collective-permute-start | bytes 12296 | tf_op jit(solution)/shard_map/ppermute | solution.py:377
  36.4 38.9 %copy-start.7 = (f32[24,128]{1,0:T(8,128)S(1)}, f32[24,128]{1,0:T(8,128)}, u32[]{:S(2)}) copy-start(f32[24,128]{1,0:T(8,128)} %table_ref.3) | copy-start | bytes 36868
  38.1 5.0 %collective-permute-start.4 = (f32[8,128]{1,0:T(8,128)S(1)}, f32[8,128]{1,0:T(8,128)S(1)}, u32[]{:S(2)}, u32[]{:S(2)}) collective-permute-start(f32[8,128]{1,0:T(8,128)S(1)} %get-tuple-element.32), channel_id=1, source_target_pairs={{0,1},{2,3},{4,5},{6,7},{8,9},{10,11},{12,13},{14,15},{16,17},{18,... | collective-permute-start | bytes 12296 | tf_op jit(solution)/shard_map/ppermute | solution.py:377
  42.3 0.8 %collective-permute-start.5 = (f32[8,128]{1,0:T(8,128)S(1)}, f32[8,128]{1,0:T(8,128)S(1)}, u32[]{:S(2)}, u32[]{:S(2)}) collective-permute-start(f32[8,128]{1,0:T(8,128)S(1)} %get-tuple-element.33), channel_id=1, source_target_pairs={{1,2},{3,4},{5,6},{7,8},{9,10},{11,12},{13,14},{15,16},{17,18},{19... | collective-permute-start | bytes 12296 | tf_op jit(solution)/shard_map/ppermute | solution.py:377

commit v2 on v1

--- a/solution.py
+++ b/solution.py
@@ -138,17 +138,18 @@
     return jnp.concatenate(pieces, axis=0)
 
 
-def send_kernel(devices, per, pressure_ref, owner_ref, element_ref, table_ref, support_ref, stiffness_ref,
-                out_ref, place_ref, diagonal_ref, sems):
-    copies = [
-        pltpu.make_async_copy(
-            stiffness_ref.at[pl.ds(8 * i, 8), pl.ds(8 * i, 8)], diagonal_ref.at[i], sems.at[i])
-        for i in range(3)
-    ]
+def send_kernel(devices, per, odd_ref, pressure_hbm, owner_hbm, element_hbm, table_hbm, support_hbm, stiffness_hbm,
+                out_ref, place_ref, pressure_ref, owner_ref, element_ref, table_ref, support_ref, diagonal_ref, sems):
+    del odd_ref
+    moves = [(owner_hbm, owner_ref), (table_hbm, table_ref), (pressure_hbm, pressure_ref), (element_hbm, element_ref),
+             (support_hbm, support_ref)]
+    moves += [(stiffness_hbm.at[pl.ds(8 * i, 8), pl.ds(8 * i, 8)], diagonal_ref.at[i]) for i in range(3)]
+    copies = [pltpu.make_async_copy(source, target, sems.at[i]) for i, (source, target) in enumerate(moves)]
     for copy in copies:
         copy.start()
     faces = pressure_ref.shape[0]
-    target, element = owner_ref[...], element_ref[...]
+    copies[0].wait()
+    target = owner_ref[...]
     named = iota((devices, faces), 0) == target
     named16 = onehot(named)
     upto = onehot(iota((WIDE, WIDE), 0) <= iota((WIDE, WIDE), 1))
@@ -165,6 +166,9 @@
     place = target * per + rank - group * per
     place_ref[...] = jnp.concatenate([place, group, jnp.zeros((6, faces), jnp.int32)], axis=0)
 
+    for copy in copies[1:4]:
+        copy.wait()
+    element = element_ref[...]
     table = jnp.concatenate([table_ref[...]] * GROUPS + [jnp.zeros((8, table_ref.shape[1]), F32)], axis=0)
     table_high, table_low = split(table)
     rows_high, rows_low = split(pressure_ref[...])
@@ -178,7 +182,7 @@
     chosen = onehot(iota((devices * per, faces), 0) == place)
     sent = dot_nt(chosen, jnp.concatenate([spread_high, spread_low], axis=0))
 
-    for copy in copies:
+    for copy in copies[4:]:
         copy.wait()
     trace = jnp.zeros((8, faces), F32)
     for i in range(3):
@@ -345,7 +349,7 @@
         if i < scalars:
             in_specs.append(pl.BlockSpec(memory_space=pltpu.SMEM))
         elif i in hbm:
-            in_specs.append(pl.BlockSpec(memory_space=pl.ANY))
+            in_specs.append(pl.BlockSpec(memory_space=pltpu.HBM))
         else:
             in_specs.append(pl.BlockSpec(memory_space=pltpu.VMEM))
     return pl.pallas_call(
@@ -355,7 +359,7 @@
         out_specs=[pl.BlockSpec(memory_space=pltpu.VMEM)] * len(outs),
         scratch_shapes=list(scratch),
         compiler_params=pltpu.CompilerParams(vmem_limit_bytes=VMEM_BYTES),
-    )(*args)
+    )(*[pltpu.with_memory_space_constraint(arg, pltpu.HBM) if i in hbm else arg for i, arg in enumerate(args)])
 
 
 def shards(pressure, face_owner, face_element, shape_table, stiffness, connectivity, support):
@@ -384,9 +388,18 @@
     sent, place = call(
         functools.partial(send_kernel, devices, per),
         [((slots, 128), F32), ((8, faces), jnp.int32)],
-        (pressure, face_owner.reshape(1, faces), face_element.reshape(1, faces), shape_table, support, stiffness),
-        hbm=(5,),
-        scratch=(pltpu.VMEM((3, 8, 8, elements), F32), pltpu.SemaphoreType.DMA((3,))),
+        (odd, pressure, face_owner.reshape(1, faces), face_element.reshape(1, faces), shape_table, support, stiffness),
+        scalars=1,
+        hbm=range(1, 7),
+        scratch=(
+            pltpu.VMEM(pressure.shape, F32),
+            pltpu.VMEM((1, faces), jnp.int32),
+            pltpu.VMEM((1, faces), jnp.int32),
+            pltpu.VMEM(shape_table.shape, F32),
+            pltpu.VMEM(support.shape, F32),
+            pltpu.VMEM((3, 8, 8, elements), F32),
+            pltpu.SemaphoreType.DMA((8,)),
+        ),
     )
     arrived = everywhere(sent)
     partial, end_a, end_b, weight, scale, codes = call(

time: 77.4 us -> 71.9 us (0.929)
  blocking collectives: 30 us -> 47.7 us
  waiting for transfers between devices: 11.4 us -> 0.82 us
  starting transfers between devices: 17.8 us -> 10.5 us
  local copies, waits for them, and re-layouts: 5.51 us -> 0.02 us
    all_to_all x2 -> x3, blocking collectives: 30 us -> 47.7 us  [everywhere(): return lax.all_to_all(rows, AXES, split_axis=0, concat_axis=0, tiled=True)]
    all_to_all x1 -> x0, waiting for transfers between devices: 10.6 us -> none  [everywhere(): return lax.all_to_all(rows, AXES, split_axis=0, concat_axis=0, tiled=True)]
    all_to_all x1 -> x0, starting transfers between devices: 7.3 us -> none  [everywhere(): return lax.all_to_all(rows, AXES, split_axis=0, concat_axis=0, tiled=True)]
    unnamed x20 -> x8, local copies, waits for them, and re-layouts: 5.51 us -> 0.02 us
  transfers between devices with their start and end apart: 7 -> 6, of which waited for: 4 -> 3; matrix products, arithmetic and copies ran while one was open for 0% -> 0% of each run, Pallas kernels for 0% -> 0%
where the time goes in v2:
time: 71.9 us; the launch traced here: 71.7 us
  blocking collectives  47.7 us (66%)
  Pallas kernels  11.9 us (17%)
  starting transfers between devices  10.5 us (15%)
  waiting for transfers between devices  0.82 us (1%)
  between operations  0.75 us (1%)
    all_to_all x3, blocking collectives, everywhere(): return lax.all_to_all(rows, AXES, split_axis=0, concat_axis=0, tiled=True)  47.7 us
    pallas_call x7, Pallas kernels, call(): pl.pallas_call(kernel, out_shape=[jax.ShapeDtypeStruct(shape, dtype) for...  11.9 us
    ppermute x6, starting transfers between devices, swap(): return (lax.ppermute(a, AXES, pairs_a), lax.ppermute(b, AXES, pairs_b))  10.5 us
  transfers between devices with their start and end apart: 6, of which 3 were waited for; matrix products, arithmetic and copies ran while one was open for 0% of the time, Pallas kernels for 0%

profile of v2, /device:TPU:0, one launch (start us, length us, event | category | flops | bytes accessed | tf_op | source)
XLA Modules:
  0.0 71.7 jit_solution(7470641023859954910)
XLA Ops:
  0.6 0.0 copy-start
  0.6 0.0 copy-start.2
  0.7 0.0 copy-start.1
  0.7 2.3 %shard_map.86 = (f32[512,128]{1,0:T(8,128)S(1)}, s32[8,1024]{1,0:T(8,128)S(1)}) custom-call(s32[1]{0:T(128)} %bitcast.odd_ref, f32[1024,128]{1,0:T(8,128)} %pressure_hbm.1, s32[1,1024]{1,0:T(1,128)} %bitcast.17, s32[1,1024]{1,0:T(1,128)} %bitcast.18, f32[24,128]{1,0:T(8,128)} %table_ref.1, f32[3,1024]{1,0:T(4,128)} %support_ref.1, f32[24,24,1024]{2,1,0:T(8,128)} %stiffness_ref.5), custom_call_target="tpu_custom_call" | custom-call | tf_op jit(solution)/shard_map/pallas_call | solution.py:355
  3.0 17.7 %all_to_all.33 = f32[32,16,128]{2,1,0:T(8,128)S(1)} all-to-all(f32[32,16,128]{2,1,0:T(8,128)S(1)} %bitcast.14), channel_id=1, replica_groups=mesh['fluid'=4,'solid'=8] {'fluid','solid'}, dimensions={0} | all-to-all | bytes 524288 | tf_op jit(solution)/shard_map/all_to_all | solution.py:384
  20.7 0.0 copy-done.2
  20.7 0.0 copy-done.1
  20.7 2.4 %shard_map.87 = (f32[24,256]{1,0:T(8,128)S(1)}, f32[8,128]{1,0:T(8,128)S(1)}, f32[8,128]{1,0:T(8,128)S(1)}, f32[24,256]{1,0:T(8,128)S(1)}, f32[8,128]{1,0:T(8,128)S(1)}, /*index=5*/s32[8,512]{1,0:T(8,128)S(1)}) custom-call(s32[1]{0:T(128)} %bitcast.odd_ref, f32[512,128]{1,0:T(8,128)S(1)} %bitcast.12, s32[8,1024]{1,0:T(8,128)S(1)} %copy-done.1, ...), custom_call_target="tpu_custom_call" | custom-call | tf_op jit(solution)/shard_map/pallas_call | solution.py:355
  23.2 0.1 collective-permute-start
  23.3 0.7 collective-permute-start.1
  23.9 0.5 collective-permute-done.swap_a_in
  24.4 0.0 collective-permute-done.1.swap_b_in
  24.4 0.0 copy-done
  24.4 1.6 %shard_map.88 = (f32[24,256]{1,0:T(8,128)S(1)}, f32[24,256]{1,0:T(8,128)S(1)}, f32[8,128]{1,0:T(8,128)S(1)}, f32[8,128]{1,0:T(8,128)S(1)}) custom-call(s32[1]{0:T(128)} %bitcast.odd_ref, f32[24,256]{1,0:T(8,128)S(1)} %get-tuple-element.23.partial_ref, f32[8,128]{1,0:T(8,128)S(1)} %collective-permute-done.swap_a_in, ...), custom_call_target="tpu_custom_call" | custom-call | tf_op jit(solution)/shard_map/pallas_call | solution.py:355
  26.0 4.3 %collective-permute-start.2 = (f32[8,128]{1,0:T(8,128)S(1)}, f32[8,128]{1,0:T(8,128)S(1)}, u32[]{:S(2)}, u32[]{:S(2)}) collective-permute-start(f32[8,128]{1,0:T(8,128)S(1)} %get-tuple-element.29), channel_id=1, source_target_pairs={{0,1},{2,3},{4,5},{6,7},{8,9},{10,11},{12,13},{14,15},{16,17},{18,... | collective-permute-start | bytes 12296 | tf_op jit(solution)/shard_map/ppermute | solution.py:381
  30.4 0.6 collective-permute-start.3
  31.0 0.2 collective-permute-done.2.swap_a_in
  31.2 0.0 collective-permute-done.3.swap_b_in
  31.2 0.0 copy-start.3
  31.2 1.6 %shard_map.89 = (f32[24,256]{1,0:T(8,128)S(1)}, f32[24,256]{1,0:T(8,128)S(1)}, f32[8,128]{1,0:T(8,128)S(1)}, f32[8,128]{1,0:T(8,128)S(1)}) custom-call(s32[1]{0:T(128)} %bitcast.odd_ref, f32[24,256]{1,0:T(8,128)S(1)} %get-tuple-element.28.partial_ref, f32[8,128]{1,0:T(8,128)S(1)} %collective-permute-done.2.swap_a_in, ...), custom_call_target="tpu_custom_call" | custom-call | tf_op jit(solution)/shard_map/pallas_call | solution.py:355
  32.8 4.2 %collective-permute-start.4 = (f32[8,128]{1,0:T(8,128)S(1)}, f32[8,128]{1,0:T(8,128)S(1)}, u32[]{:S(2)}, u32[]{:S(2)}) collective-permute-start(f32[8,128]{1,0:T(8,128)S(1)} %get-tuple-element.32), channel_id=1, source_target_pairs={{0,1},{2,3},{4,5},{6,7},{8,9},{10,11},{12,13},{14,15},{16,17},{18,... | collective-permute-start | bytes 12296 | tf_op jit(solution)/shard_map/ppermute | solution.py:381
  37.0 0.6 collective-permute-start.5
  37.7 0.2 collective-permute-done.4.swap_a_in
  37.8 0.0 collective-permute-done.5.swap_b_in
  37.8 0.6 shard_map.90
  38.4 17.7 %all_to_all.34 = f32[32,1,128]{2,1,0:T(1,128)S(1)} all-to-all(f32[32,1,128]{2,1,0:T(1,128)S(1)} %bitcast.16), channel_id=1, replica_groups=mesh['fluid'=4,'solid'=8] {'fluid','solid'}, dimensions={0} | all-to-all | bytes 32768 | tf_op jit(solution)/shard_map/all_to_all | solution.py:384
  56.1 1.7 %shard_map.91 = (f32[3,1024]{1,0:T(4,128)}, f32[512,128]{1,0:T(8,128)S(1)}) custom-call(f32[32,128]{1,0:T(8,128)S(1)} %bitcast.15, f32[8,128]{1,0:T(8,128)S(1)} %get-tuple-element.27.scale_ref, f32[24,256]{1,0:T(8,128)S(1)} %get-tuple-element.34.first_ref, f32[24,256]{1,0:T(8,128)S(1)} %get-tuple-element.35.second_ref, ...), custom_call_target="tpu_custom_call" | custom-call | tf_op jit(solution)/shard_map/pallas_call | solution.py:355
  57.8 12.3 %all_to_all.35 = f32[32,16,128]{2,1,0:T(8,128)S(1)} all-to-all(f32[32,16,128]{2,1,0:T(8,128)S(1)} %bitcast.13), channel_id=1, replica_groups=mesh['fluid'=4,'solid'=8] {'fluid','solid'}, dimensions={0} | all-to-all | bytes 524288 | tf_op jit(solution)/shard_map/all_to_all | solution.py:384
  70.1 0.0 copy-done.3
  70.1 1.6 %shard_map.92 = f32[1024,128]{1,0:T(8,128)} custom-call(f32[512,128]{1,0:T(8,128)S(1)} %bitcast.11, s32[8,1024]{1,0:T(8,128)S(1)} %get-tuple-element.41.place_ref, f32[24,128]{1,0:T(8,128)S(1)} %copy-done.3), custom_call_target="tpu_custom_call" | custom-call | tf_op jit(solution)/shard_map/pallas_call | solution.py:355
Async XLA Ops:
  0.6 23.8 %copy-start = (f32[24,24,1024]{2,1,0:T(8,128)S(1)}, f32[24,24,1024]{2,1,0:T(8,128)}, u32[]{:S(2)}) copy-start(f32[24,24,1024]{2,1,0:T(8,128)} %stiffness_ref.5) | copy-start | bytes 7077892
  0.6 20.1 %copy-start.2 = (f32[3,1024]{1,0:T(4,128)S(1)}, f32[3,1024]{1,0:T(4,128)}, u32[]{:S(2)}) copy-start(f32[3,1024]{1,0:T(4,128)} %support_ref.1) | copy-start | bytes 36868
  0.7 20.1 %copy-start.1 = (s32[8,1024]{1,0:T(8,128)S(1)}, s32[8,1024]{1,0:T(8,128)}, u32[]{:S(2)}) copy-start(s32[8,1024]{1,0:T(8,128)} %connectivity_ref.9) | copy-start | bytes 98308
  23.2 1.2 %collective-permute-start = (f32[8,128]{1,0:T(8,128)S(1)}, f32[8,128]{1,0:T(8,128)S(1)}, u32[]{:S(2)}, u32[]{:S(2)}) collective-permute-start(f32[8,128]{1,0:T(8,128)S(1)} %get-tuple-element.24), channel_id=1, source_target_pairs={{0,1},{2,3},{4,5},{6,7},{8,9},{10,11},{12,13},{14,15},{16,17},{18,... | collective-permute-start | bytes 12296 | tf_op jit(solution)/shard_map/ppermute | solution.py:381
  23.3 1.2 %collective-permute-start.1 = (f32[8,128]{1,0:T(8,128)S(1)}, f32[8,128]{1,0:T(8,128)S(1)}, u32[]{:S(2)}, u32[]{:S(2)}) collective-permute-start(f32[8,128]{1,0:T(8,128)S(1)} %get-tuple-element.25), channel_id=1, source_target_pairs={{1,2},{3,4},{5,6},{7,8},{9,10},{11,12},{13,14},{15,16},{17,18},{19... | collective-permute-start | bytes 12296 | tf_op jit(solution)/shard_map/ppermute | solution.py:381
  26.0 5.1 %collective-permute-start.2 = (f32[8,128]{1,0:T(8,128)S(1)}, f32[8,128]{1,0:T(8,128)S(1)}, u32[]{:S(2)}, u32[]{:S(2)}) collective-permute-start(f32[8,128]{1,0:T(8,128)S(1)} %get-tuple-element.29), channel_id=1, source_target_pairs={{0,1},{2,3},{4,5},{6,7},{8,9},{10,11},{12,13},{14,15},{16,17},{18,... | collective-permute-start | bytes 12296 | tf_op jit(solution)/shard_map/ppermute | solution.py:381
  30.4 0.8 %collective-permute-start.3 = (f32[8,128]{1,0:T(8,128)S(1)}, f32[8,128]{1,0:T(8,128)S(1)}, u32[]{:S(2)}, u32[]{:S(2)}) collective-permute-start(f32[8,128]{1,0:T(8,128)S(1)} %get-tuple-element.30), channel_id=1, source_target_pairs={{1,2},{3,4},{5,6},{7,8},{9,10},{11,12},{13,14},{15,16},{17,18},{19... | collective-permute-start | bytes 12296 | tf_op jit(solution)/shard_map/ppermute | solution.py:381
  31.2 38.9 %copy-start.3 = (f32[24,128]{1,0:T(8,128)S(1)}, f32[24,128]{1,0:T(8,128)}, u32[]{:S(2)}) copy-start(f32[24,128]{1,0:T(8,128)} %table_ref.1) | copy-start | bytes 36868
  32.8 5.0 %collective-permute-start.4 = (f32[8,128]{1,0:T(8,128)S(1)}, f32[8,128]{1,0:T(8,128)S(1)}, u32[]{:S(2)}, u32[]{:S(2)}) collective-permute-start(f32[8,128]{1,0:T(8,128)S(1)} %get-tuple-element.32), channel_id=1, source_target_pairs={{0,1},{2,3},{4,5},{6,7},{8,9},{10,11},{12,13},{14,15},{16,17},{18,... | collective-permute-start | bytes 12296 | tf_op jit(solution)/shard_map/ppermute | solution.py:381
  37.0 0.8 %collective-permute-start.5 = (f32[8,128]{1,0:T(8,128)S(1)}, f32[8,128]{1,0:T(8,128)S(1)}, u32[]{:S(2)}, u32[]{:S(2)}) collective-permute-start(f32[8,128]{1,0:T(8,128)S(1)} %get-tuple-element.33), channel_id=1, source_target_pairs={{1,2},{3,4},{5,6},{7,8},{9,10},{11,12},{13,14},{15,16},{17,18},{19... | collective-permute-start | bytes 12296 | tf_op jit(solution)/shard_map/ppermute | solution.py:381

commit v3 on v2

v3 whole, which is shorter than its diff:
```python
import functools

import jax
import jax.numpy as jnp
from jax import lax
from jax.experimental import pallas as pl
from jax.experimental.pallas import tpu as pltpu
from jax.sharding import PartitionSpec as P

AXES = ("fluid", "solid")
DOF = 24
CORNERS = 8
GROUPS = 5
FIELD_ROWS = 16
LANES = 128
WIDE = 256
VMEM_BYTES = 24 * 1024 * 1024
F32 = jnp.float32
BF16 = jnp.bfloat16


def iota(shape, axis):
    return lax.broadcasted_iota(jnp.int32, shape, axis)


def onehot(mask):
    return jnp.where(mask, 1.0, 0.0).astype(BF16)


def split(value):
    high = value.astype(BF16)
    return high, (value - high.astype(F32)).astype(BF16)


def dot_nt(left, right):
    return lax.dot_general(left, right, (((1,), (1,)), ((), ())), preferred_element_type=F32)


def dot_nn(left, right):
    return lax.dot_general(left, right, (((1,), (0,)), ((), ())), preferred_element_type=F32)


def take_lanes(table, index):
    return jnp.take_along_axis(table, index, axis=1, mode="promise_in_bounds")


def gather_corners(field, connectivity):
    elements = connectivity.shape[1]
    rows = {}
    for c in range(3):
        for h in range(9):
            rows[c, h] = jnp.broadcast_to(field[c * FIELD_ROWS + h:c * FIELD_ROWS + h + 1], (CORNERS, LANES))
    parts = [[], [], []]
    for start in range(0, elements, LANES):
        index = connectivity[:, start:start + LANES]
        low, high = index & 127, index >> 7
        masks = [high == h for h in range(9)]
        for c in range(3):
            total = jnp.zeros((CORNERS, LANES), F32)
            for h in range(9):
                total = jnp.where(masks[h], take_lanes(rows[c, h], low), total)
            parts[c].append(total)
    return [jnp.concatenate(part, axis=1) for part in parts]


def assemble(terms, connectivity):
    elements = connectivity.shape[1]
    high, low = connectivity >> 7, connectivity & 127
    upper = terms.astype(BF16).astype(F32)
    lower = terms - upper
    total = jnp.zeros((6 * FIELD_ROWS, LANES), F32)
    for k in range(CORNERS):
        mask = iota((FIELD_ROWS, elements), 0) == high[k:k + 1]
        pieces = [
            jnp.where(mask, part[c * CORNERS + k:c * CORNERS + k + 1], 0.0)
            for part in (upper, lower)
            for c in range(3)
        ]
        left = jnp.concatenate(pieces, axis=0).astype(BF16)
        total = total + dot_nt(left, onehot(iota((LANES, elements), 0) == low[k:k + 1]))
    return total[:3 * FIELD_ROWS] + total[3 * FIELD_ROWS:]


def matvec(stiffness, values):
    elements = stiffness.shape[2]
    parts = []
    for start in range(0, elements, 128):
        total = jnp.zeros((DOF, 128), F32)
        for b in range(DOF):
            total = total + stiffness[b, :, start:start + 128] * values[b // 8][b % 8:b % 8 + 1, start:start + 128]
        parts.append(total)
    return jnp.concatenate(parts, axis=1)


def put_ends(partial, odd, own_rows, swap_a_ref, swap_b_ref):
    pad = [jnp.zeros((5, LANES), F32)]
    first = jnp.concatenate([partial[c * FIELD_ROWS:c * FIELD_ROWS + 1] for c in range(3)] + pad, axis=0)
    over = jnp.concatenate(
        [partial[c * FIELD_ROWS + own_rows:c * FIELD_ROWS + own_rows + 1] for c in range(3)] + pad, axis=0)
    swap_a_ref[...] = jnp.where(odd, first, over)
    swap_b_ref[...] = jnp.where(odd, over, first)


def add_ends(partial, odd, own_rows, swap_a, swap_b):
    before = jnp.where(odd, swap_a, swap_b)
    after = jnp.where(odd, swap_b, swap_a)
    pieces = []
    for c in range(3):
        pieces += [
            before[c:c + 1],
            jnp.zeros((own_rows - 1, LANES), F32),
            after[c:c + 1],
            jnp.zeros((FIELD_ROWS - own_rows - 1, LANES), F32),
        ]
    return partial + jnp.concatenate(pieces, axis=0)


def own_mask(own_rows):
    return (iota((3 * FIELD_ROWS, LANES), 0) % FIELD_ROWS) < own_rows


def as_field(rows, own_rows):
    pieces = []
    for c in range(3):
        pieces += [rows[c:c + 1, h * LANES:(h + 1) * LANES] for h in range(own_rows)]
        pieces.append(jnp.zeros((FIELD_ROWS - own_rows, LANES), F32))
    return jnp.concatenate(pieces, axis=0)


def send_kernel(devices, per, odd_ref, pressure_hbm, owner_hbm, element_hbm, table_hbm, support_hbm, stiffness_hbm,
                out_ref, place_ref, pressure_ref, owner_ref, element_ref, table_ref, support_ref, diagonal_ref, sems):
    del odd_ref
    moves = [(owner_hbm, owner_ref), (element_hbm, element_ref), (table_hbm, table_ref), (pressure_hbm, pressure_ref),
             (support_hbm, support_ref)]
    moves += [(stiffness_hbm.at[i, pl.ds(i, 1)], diagonal_ref.at[pl.ds(i, 1)]) for i in range(DOF)]
    copies = [pltpu.make_async_copy(source, target, sems.at[i]) for i, (source, target) in enumerate(moves)]
    for copy in copies:
        copy.start()
    for copy in copies:
        copy.wait()
    faces = pressure_ref.shape[0]
    target = owner_ref[...]
    named = iota((devices, faces), 0) == target
    named16 = onehot(named)
    blocks = range(0, faces, WIDE)
    upto = onehot(iota((WIDE, WIDE), 0) <= iota((WIDE, WIDE), 1))
    counts = dot_nn(jnp.concatenate([named16[:, start:start + WIDE] for start in blocks], axis=0), upto)
    before = jnp.zeros((devices, 1), F32)
    ranks = []
    for i, start in enumerate(blocks):
        count = counts[i * devices:(i + 1) * devices]
        here = jnp.where(named[:, start:start + WIDE], count + before, 0.0)
        ranks.append(jnp.sum(here, axis=0, keepdims=True))
        before = before + count[:, WIDE - 1:]
    rank = jnp.concatenate(ranks, axis=1).astype(jnp.int32) - 1
    group = jnp.zeros_like(rank)
    for i in range(1, GROUPS):
        group = group + (rank >= i * per).astype(jnp.int32)
    place = target * per + rank - group * per
    place_ref[...] = jnp.concatenate([place, group, jnp.zeros((6, faces), jnp.int32)], axis=0)
    chosen = onehot(iota((devices * per, faces), 0) == place)

    pad = jnp.zeros((LANES - GROUPS * DOF, table_ref.shape[1]), F32)
    table_high, table_low = split(jnp.concatenate([table_ref[...]] * GROUPS + [pad], axis=0))
    rows_high, rows_low = split(pressure_ref[...])
    projected = dot_nt(
        jnp.concatenate([table_high, table_low, table_high], axis=1),
        jnp.concatenate([rows_high, rows_high, rows_low], axis=1),
    )
    spread = [jnp.where(group == i, projected[i * DOF:(i + 1) * DOF], 0.0) for i in range(GROUPS)]
    spread.append(jnp.where(iota((8, faces), 0) == group, element_ref[...].astype(F32), 0.0))
    spread_high, spread_low = split(jnp.concatenate(spread, axis=0))
    sent = dot_nt(chosen, jnp.concatenate([spread_high, spread_low], axis=0))

    trace = jnp.sum(diagonal_ref[...]) + jnp.sum(support_ref[...])
    out_ref[...] = jnp.where(iota((devices * per, LANES), 1) == 125, trace, sent[:, :LANES] + sent[:, LANES:])


def load_kernel(devices, per, odd_ref, rows_ref, connectivity_ref, support_ref,
                partial_ref, swap_a_ref, swap_b_ref, weight_ref, scale_ref, code_ref):
    nodes = support_ref.shape[1]
    own_rows = nodes // LANES
    rows = rows_ref[...]
    slots = rows.shape[0]
    arrived = rows.T
    codes = arrived[GROUPS * DOF:].astype(jnp.int32)
    code_ref[...] = codes
    total = jnp.zeros((4 * 2 * DOF, WIDE), F32)
    for g in range(GROUPS):
        terms = arrived[g * DOF:(g + 1) * DOF]
        upper = terms.astype(BF16).astype(F32)
        both = jnp.concatenate([upper, terms - upper], axis=0)
        code = codes[g:g + 1]
        left = jnp.concatenate([jnp.where((code >> 8) == i, both, 0.0) for i in range(4)], axis=0).astype(BF16)
        total = total + dot_nt(left, onehot(iota((WIDE, slots), 0) == (code & 255)))
    loads = jnp.concatenate(
        [total[i * 2 * DOF:i * 2 * DOF + DOF] + total[i * 2 * DOF + DOF:(i + 1) * 2 * DOF] for i in range(4)], axis=1)
    partial = assemble(loads, connectivity_ref[...])
    partial_ref[...] = partial
    put_ends(partial, odd_ref[0] == 1, own_rows, swap_a_ref, swap_b_ref)
    trace = jnp.sum(rows[:, 125:126]) * (1.0 / per)
    inverse = jnp.full((8, LANES), 3.0 * nodes * devices, F32) / jnp.full((8, LANES), trace, F32)
    scale_ref[...] = inverse
    weight = as_field(support_ref[...], own_rows) * inverse[:1, :1] - 1.0
    weight_ref[...] = jnp.where(own_mask(own_rows), weight, 0.0)


def product_kernel(own_rows, odd_ref, partial_ref, swap_a_in, swap_b_in, weight_ref, scale_ref, connectivity_ref,
                   stiffness_ref, field_ref, values_ref, next_ref, swap_a_ref, swap_b_ref):
    odd = odd_ref[0] == 1
    field = add_ends(partial_ref[...], odd, own_rows, swap_a_in[...], swap_b_in[...])
    field_ref[...] = field
    connectivity = connectivity_ref[...]
    values = gather_corners(field, connectivity)
    values_ref[...] = jnp.concatenate(values, axis=0)
    forces = matvec(stiffness_ref, values)
    partial = assemble(forces, connectivity) * scale_ref[:1, :1] + weight_ref[...] * field
    next_ref[...] = partial
    put_ends(partial, odd, own_rows, swap_a_ref, swap_b_ref)


def moment_kernel(own_rows, devices, odd_ref, partial_ref, swap_a_in, swap_b_in, weight_ref, scale_ref,
                  connectivity_ref, stiffness_ref, first_ref, second_ref, pick0_ref, pick1_ref,
                  field_ref, values_ref, moments_ref):
    del pick0_ref, pick1_ref
    odd = odd_ref[0] == 1
    third = add_ends(partial_ref[...], odd, own_rows, swap_a_in[...], swap_b_in[...])
    field_ref[...] = third
    values = gather_corners(third, connectivity_ref[...])
    forces = matvec(stiffness_ref, values)
    values = jnp.concatenate(values, axis=0)
    values_ref[...] = values
    energy = jnp.sum(forces * values, axis=0, keepdims=True)
    own = own_mask(own_rows)
    first, second = jnp.where(own, first_ref[...], 0.0), jnp.where(own, second_ref[...], 0.0)
    owned = jnp.where(own, third, 0.0)
    moments = [
        jnp.sum(first * first),
        jnp.sum(first * second),
        jnp.sum(second * second),
        jnp.sum(second * owned),
        jnp.sum(owned * owned),
        jnp.sum(energy) * scale_ref[:1, :1] + jnp.sum(weight_ref[...] * owned * owned),
    ]
    lane = iota((devices, LANES), 1)
    row = jnp.zeros((devices, LANES), F32)
    for i, moment in enumerate(moments):
        row = jnp.where(lane == i, moment, row)
    moments_ref[...] = row


def step_weights(m):
    def dot(p, q):
        terms = [p[i] * q[j] * m[i + j] for i in range(3) for j in range(3) if p[i] is not None and q[j] is not None]
        return functools.reduce(lambda a, b: a + b, terms)

    def energy(p):
        terms = [p[i] * p[j] * (m[i + j + 1] + m[i + j]) for i in range(3) for j in range(3)
                 if p[i] is not None and p[j] is not None]
        return functools.reduce(lambda a, b: a + b, terms)

    norm0 = m[0]
    curve0 = m[0] + m[1]
    step0 = norm0 / curve0
    residual = [m[1] / curve0, -step0, None]
    norm1 = dot(residual, residual)
    turn0 = norm1 / norm0
    direction = [residual[0] + turn0, residual[1], None]
    step1 = norm1 / energy(direction)
    result = [step0 + step1 * direction[0], step1 * direction[1]]
    residual = [
        residual[0] - step1 * direction[0],
        residual[1] - step1 * (direction[0] + direction[1]),
        -step1 * direction[1],
    ]
    norm2 = dot(residual, residual)
    turn1 = norm2 / norm1
    direction = [residual[0] + turn1 * direction[0], residual[1] + turn1 * direction[1], residual[2]]
    step2 = norm2 / energy(direction)
    return [result[0] + step2 * direction[0], result[1] + step2 * direction[1], step2 * direction[2]]


def pick(values, code_ref, out_ref, blend):
    for start in range(0, code_ref.shape[1], LANES):
        sections = []
        for g in range(GROUPS):
            code = jnp.broadcast_to(code_ref[g:g + 1, start:start + LANES], (CORNERS, LANES))
            low, high = code & 127, code >> 7
            masks = [high == i for i in range(8)]
            for c in range(3):
                total = jnp.zeros((CORNERS, LANES), F32)
                for i in range(8):
                    tile = values[c * CORNERS:(c + 1) * CORNERS, i * LANES:(i + 1) * LANES]
                    total = jnp.where(masks[i], take_lanes(tile, low), total)
                sections.append(total)
        sections.append(jnp.zeros((CORNERS, LANES), F32))
        rows = pl.ds(start, LANES)
        out_ref[rows, :] = blend(jnp.concatenate(sections, axis=0).T, rows)


def pick_kernel(values_ref, code_ref, after_ref, out_ref):
    del after_ref
    pick(values_ref[...], code_ref, out_ref, lambda tile, rows: tile)


def blend_kernel(moments_ref, scale_ref, code_ref, pick0_ref, pick1_ref, values_ref, weights_ref, out_ref):
    sums = jnp.sum(moments_ref[...], axis=0, keepdims=True)
    weights = step_weights([sums[:, i:i + 1] for i in range(6)])
    weights = [weight * scale_ref[:1, :1] for weight in weights]
    weights_ref[...] = jnp.concatenate([jnp.broadcast_to(weight, (8, LANES)) for weight in weights], axis=0)

    def blend(tile, rows):
        return weights[0] * pick0_ref[rows, :] + weights[1] * pick1_ref[rows, :] + weights[2] * tile

    pick(values_ref[...], code_ref, out_ref, blend)


def motion_kernel(own_rows, rows_ref, place_ref, table_ref, weights_ref, first_ref, second_ref, third_ref,
                  displacement_hbm, out_hbm, displacement_ref, out_ref, sems):
    field = weights_ref[:1] * first_ref[...] + weights_ref[8:9] * second_ref[...] + weights_ref[16:17] * third_ref[...]
    for c in range(3):
        for h in range(own_rows):
            displacement_ref[c:c + 1, h * LANES:(h + 1) * LANES] = field[c * FIELD_ROWS + h:c * FIELD_ROWS + h + 1]
    copies = [pltpu.make_async_copy(displacement_ref, displacement_hbm, sems.at[0])]
    copies[0].start()
    high, low = split(rows_ref[...].T)
    slots, faces = rows_ref.shape[0], place_ref.shape[1]
    place, group = place_ref[0:1], place_ref[1:2]
    found = dot_nn(jnp.concatenate([high, low], axis=0), onehot(iota((slots, faces), 0) == place))
    found = found[:LANES] + found[LANES:]
    owned = jnp.zeros((DOF, faces), F32)
    for g in range(GROUPS):
        owned = jnp.where(group == g, found[g * DOF:(g + 1) * DOF], owned)
    upper = owned.astype(BF16).astype(F32)
    lower = owned - upper
    parts = jnp.concatenate([upper, lower, upper], axis=0).T.astype(BF16)
    table_high, table_low = split(table_ref[...])
    right = jnp.concatenate([table_high, table_high, table_low], axis=0)
    for i, start in enumerate(range(0, faces, WIDE)):
        out_ref[start:start + WIDE, :] = dot_nn(parts[start:start + WIDE], right)
        copy = pltpu.make_async_copy(
            out_ref.at[pl.ds(start, WIDE)], out_hbm.at[pl.ds(start, WIDE)], sems.at[1 + i])
        copy.start()
        copies.append(copy)
    for copy in copies:
        copy.wait()


def call(kernel, outs, args, scalars=0, hbm=(), outs_hbm=(), scratch=(), time=1.0):
    in_specs = []
    for i in range(len(args)):
        if i < scalars:
            in_specs.append(pl.BlockSpec(memory_space=pltpu.SMEM))
        elif i in hbm:
            in_specs.append(pl.BlockSpec(memory_space=pltpu.HBM))
        else:
            in_specs.append(pl.BlockSpec(memory_space=pltpu.VMEM))
    return pl.pallas_call(
        kernel,
        name=getattr(kernel, "func", kernel).__name__,
        out_shape=[jax.ShapeDtypeStruct(shape, dtype) for shape, dtype in outs],
        in_specs=in_specs,
        out_specs=[
            pl.BlockSpec(memory_space=pltpu.HBM if i in outs_hbm else pltpu.VMEM) for i in range(len(outs))
        ],
        scratch_shapes=list(scratch),
        cost_estimate=pl.CostEstimate(flops=int(time * 1e9), transcendentals=0, bytes_accessed=int(time * 1e6)),
        compiler_params=pltpu.CompilerParams(vmem_limit_bytes=VMEM_BYTES),
    )(*[pltpu.with_memory_space_constraint(arg, pltpu.HBM) if i in hbm else arg for i, arg in enumerate(args)])


def shards(pressure, face_owner, face_element, shape_table, stiffness, connectivity, support):
    devices = lax.axis_size(AXES)
    faces = pressure.shape[0]
    elements = stiffness.shape[2]
    nodes = support.shape[1]
    own_rows = nodes // LANES
    capacity = max(2, (5 * faces + 2 * devices - 1) // (2 * devices))
    per = (capacity + GROUPS - 1) // GROUPS
    slots = devices * per
    odd = (lax.axis_index(AXES) % 2).astype(jnp.int32).reshape(1)
    evens = [(i, i + 1) for i in range(0, devices - 1, 2)]
    odds = [(i, i + 1) for i in range(1, devices - 1, 2)]
    pairs_a = evens + [(j, i) for i, j in evens]
    pairs_b = odds + [(j, i) for i, j in odds]

    def swap(a, b):
        return lax.ppermute(a, AXES, pairs_a), lax.ppermute(b, AXES, pairs_b)

    def everywhere(rows):
        return lax.all_to_all(rows, AXES, split_axis=0, concat_axis=0, tiled=True)

    field = ((3 * FIELD_ROWS, LANES), F32)
    values = ((DOF, elements), F32)
    ends = ((8, LANES), F32)
    block = ((slots, LANES), F32)
    sent, place = call(
        functools.partial(send_kernel, devices, per),
        [block, ((8, faces), jnp.int32)],
        (odd, pressure, face_owner.reshape(1, faces), face_element.reshape(1, faces), shape_table, support, stiffness),
        scalars=1,
        hbm=range(1, 7),
        scratch=(
            pltpu.VMEM(pressure.shape, F32),
            pltpu.VMEM((1, faces), jnp.int32),
            pltpu.VMEM((1, faces), jnp.int32),
            pltpu.VMEM(shape_table.shape, F32),
            pltpu.VMEM(support.shape, F32),
            pltpu.VMEM((DOF, elements), F32),
            pltpu.SemaphoreType.DMA((5 + DOF,)),
        ),
    )
    arrived = everywhere(sent)
    partial, end_a, end_b, weight, scale, codes = call(
        functools.partial(load_kernel, devices, per),
        [field, ends, ends, field, ends, ((8, slots), jnp.int32)],
        (odd, arrived, connectivity, support),
        scalars=1,
    )
    fields, picks = [], []
    end_a, end_b = swap(end_a, end_b)
    for _ in range(2):
        full, corners, partial, end_a, end_b = call(
            functools.partial(product_kernel, own_rows),
            [field, values, field, ends, ends],
            (odd, partial, end_a, end_b, weight, scale, connectivity, stiffness),
            scalars=1,
        )
        fields.append(full)
        end_a, end_b = swap(end_a, end_b)
        picks += call(pick_kernel, [block], (corners, codes, end_a), time=0.1)
    third, corners, moments = call(
        functools.partial(moment_kernel, own_rows, devices),
        [field, values, ((devices, LANES), F32)],
        (odd, partial, end_a, end_b, weight, scale, connectivity, stiffness, *fields, *picks),
        scalars=1,
    )
    moments = everywhere(moments)
    weights, leaving = call(
        blend_kernel,
        [((24, LANES), F32), block],
        (moments, scale, codes, *picks, corners),
    )
    returned = everywhere(leaving)
    return call(
        functools.partial(motion_kernel, own_rows),
        [((3, nodes), F32), ((faces, LANES), F32)],
        (returned, place, shape_table, weights, *fields, third),
        outs_hbm=(0, 1),
        scratch=(
            pltpu.VMEM((3, nodes), F32),
            pltpu.VMEM((faces, LANES), F32),
            pltpu.SemaphoreType.DMA((1 + faces // WIDE,)),
        ),
    )


def solution(mesh):
    in_specs = (
        P(AXES, None),
        P(AXES, None),
        P(AXES),
        P(),
        P(None, None, AXES),
        P(None, AXES),
        P(None, AXES),
    )
    out_specs = (P(None, AXES), P(AXES, None))
    return jax.shard_map(shards, mesh=mesh, in_specs=in_specs, out_specs=out_specs, check_vma=False)
```

time: 71.9 us -> 69.6 us (0.968)
  blocking collectives: 47.7 us -> 46.2 us
  Pallas kernels: 11.9 us -> 11.1 us
    all_to_all x3, blocking collectives: 47.7 us -> 46.2 us  [everywhere(): return lax.all_to_all(rows, AXES, split_axis=0, concat_axis=0, tiled=True)]
    pallas_call x7 -> x9, Pallas kernels: 11.9 us -> 11.1 us  [call(): pl.pallas_call(kernel, name=getattr(kernel, 'func', kernel).__name__, out...]
  transfers between devices with their start and end apart: 6 -> 6, of which waited for: 3 -> 2; matrix products, arithmetic and copies ran while one was open for 0% -> 0% of each run, Pallas kernels for 0% -> 2%
where the time goes in v3:
time: 69.6 us; the launch traced here: 69.3 us
  blocking collectives  46.2 us (66%)
  Pallas kernels  11.1 us (16%)
  starting transfers between devices  10.5 us (15%)
  between operations  0.76 us (1%)
    all_to_all x3, blocking collectives, everywhere(): return lax.all_to_all(rows, AXES, split_axis=0, concat_axis=0, tiled=True)  46.2 us
    pallas_call x9, Pallas kernels, call(): pl.pallas_call(kernel, name=getattr(kernel, 'func', kernel).__name__, out...  11.1 us
    ppermute x6, starting transfers between devices, swap(): return (lax.ppermute(a, AXES, pairs_a), lax.ppermute(b, AXES, pairs_b))  10.5 us
  transfers between devices with their start and end apart: 6, of which 2 were waited for; matrix products, arithmetic and copies ran while one was open for 0% of the time, Pallas kernels for 2%

profile of v3, /device:TPU:0, one launch (start us, length us, event | category | flops | bytes accessed | tf_op | source)
XLA Modules:
  0.0 69.3 jit_solution(13793286036858501852)
XLA Ops:
  0.6 0.0 copy-start.2
  0.6 0.0 copy-start.1
  0.7 2.2 %send_kernel.1 = (f32[512,128]{1,0:T(8,128)S(1)}, s32[8,1024]{1,0:T(8,128)S(1)}) custom-call(s32[1]{0:T(128)} %bitcast.odd_ref, f32[1024,128]{1,0:T(8,128)} %pressure_hbm.1, s32[1,1024]{1,0:T(1,128)} %bitcast.17, s32[1,1024]{1,0:T(1,128)} %bitcast.18, f32[24,128]{1,0:T(8,128)} %table_ref.1, f32[3,1024]{1,0:T(4,128)} %support_ref.1, f32[24,24,1024]{2,1,0:T(8,128)} %stiffness_ref.5), custom_call_target="tpu_custom_call" | custom-call | flops 1000000000 | bytes 1000000 | tf_op jit(solution)/shard_map/send_kernel/pallas_call | solution.py:358
  2.8 0.0 copy-start
  2.9 17.7 %all_to_all.33 = f32[32,16,128]{2,1,0:T(8,128)S(1)} all-to-all(f32[32,16,128]{2,1,0:T(8,128)S(1)} %bitcast.14), channel_id=1, replica_groups=mesh['fluid'=4,'solid'=8] {'fluid','solid'}, dimensions={0} | all-to-all | bytes 524288 | tf_op jit(solution)/shard_map/all_to_all | solution.py:391
  20.6 0.0 copy-done.2
  20.6 0.0 copy-done.1
  20.6 1.9 %load_kernel.1 = (f32[48,128]{1,0:T(8,128)S(1)}, f32[8,128]{1,0:T(8,128)S(1)}, f32[8,128]{1,0:T(8,128)S(1)}, f32[48,128]{1,0:T(8,128)S(1)}, f32[8,128]{1,0:T(8,128)S(1)}, /*index=5*/s32[8,512]{1,0:T(8,128)S(1)}) custom-call(s32[1]{0:T(128)} %bitcast.odd_ref, f32[512,128]{1,0:T(8,128)S(1)} %bitcast.13, s32[8,1024]{1,0:T(8,128)S(1)} %copy-done.1, ...), custom_call_target="tpu_custom_call" | custom-call | flops 1000000000 | bytes 1000000 | tf_op jit(solution)/shard_map/load_kernel/pallas_call | solution.py:358
  22.5 0.1 collective-permute-start
  22.6 0.7 collective-permute-start.1
  23.3 0.5 collective-permute-done.swap_a_in
  23.7 0.0 collective-permute-done.1.swap_b_in
  23.7 0.0 copy-done
  23.7 1.2 %product_kernel.2 = (f32[48,128]{1,0:T(8,128)S(1)}, f32[24,1024]{1,0:T(8,128)S(1)}, f32[48,128]{1,0:T(8,128)S(1)}, f32[8,128]{1,0:T(8,128)S(1)}, f32[8,128]{1,0:T(8,128)S(1)}) custom-call(s32[1]{0:T(128)} %bitcast.odd_ref, f32[48,128]{1,0:T(8,128)S(1)} %get-tuple-element.26.partial_ref, f32[8,128]{1,0:T(8,128)S(1)} %collective-permute-done.swap_a_in, ...), custom_call_target="tpu_custom_call" | custom-call | flops 1000000000 | bytes 1000000 | tf_op jit(solution)/shard_map/product_kernel/pallas_call | solution.py:358
  24.9 4.3 %collective-permute-start.2 = (f32[8,128]{1,0:T(8,128)S(1)}, f32[8,128]{1,0:T(8,128)S(1)}, u32[]{:S(2)}, u32[]{:S(2)}) collective-permute-start(f32[8,128]{1,0:T(8,128)S(1)} %get-tuple-element.32), channel_id=1, source_target_pairs={{0,1},{2,3},{4,5},{6,7},{8,9},{10,11},{12,13},{14,15},{16,17},{18,... | collective-permute-start | bytes 12296 | tf_op jit(solution)/shard_map/ppermute | solution.py:388
  29.3 0.6 collective-permute-start.3
  29.9 0.2 collective-permute-done.2.swap_a_in.after_ref
  30.1 0.0 collective-permute-done.3.swap_b_in
  30.1 1.2 %product_kernel.3 = (f32[48,128]{1,0:T(8,128)S(1)}, f32[24,1024]{1,0:T(8,128)S(1)}, f32[48,128]{1,0:T(8,128)S(1)}, f32[8,128]{1,0:T(8,128)S(1)}, f32[8,128]{1,0:T(8,128)S(1)}) custom-call(s32[1]{0:T(128)} %bitcast.odd_ref, f32[48,128]{1,0:T(8,128)S(1)} %get-tuple-element.31.partial_ref, f32[8,128]{1,0:T(8,128)S(1)} %collective-permute-done.2.swap_a_in.after_ref, ...), custom_call_target="tpu_custom_call" | custom-call | flops 1000000000 | bytes 1000000 | tf_op jit(solution)/shard_map/product_kernel/pallas_call | solution.py:358
  31.3 4.2 %collective-permute-start.4 = (f32[8,128]{1,0:T(8,128)S(1)}, f32[8,128]{1,0:T(8,128)S(1)}, u32[]{:S(2)}, u32[]{:S(2)}) collective-permute-start(f32[8,128]{1,0:T(8,128)S(1)} %get-tuple-element.35), channel_id=1, source_target_pairs={{0,1},{2,3},{4,5},{6,7},{8,9},{10,11},{12,13},{14,15},{16,17},{18,... | collective-permute-start | bytes 12296 | tf_op jit(solution)/shard_map/ppermute | solution.py:388
  35.5 0.6 collective-permute-start.5
  36.1 0.8 %pick_kernel.2.pick0_ref = f32[512,128]{1,0:T(8,128)S(1)} custom-call(f32[24,1024]{1,0:T(8,128)S(1)} %get-tuple-element.39.values_ref, s32[8,512]{1,0:T(8,128)S(1)} %get-tuple-element.40.code_ref, f32[8,128]{1,0:T(8,128)S(1)} %collective-permute-done.2.swap_a_in.after_ref), custom_call_target="tpu_custom_call" | custom-call | flops 100000000 | bytes 100000 | tf_op jit(solution)/shard_map/pick_kernel/pallas_call | solution.py:358
  36.9 0.0 collective-permute-done.4.after_ref.swap_a_in
  36.9 0.8 %pick_kernel.3.pick1_ref = f32[512,128]{1,0:T(8,128)S(1)} custom-call(f32[24,1024]{1,0:T(8,128)S(1)} %get-tuple-element.41.values_ref, s32[8,512]{1,0:T(8,128)S(1)} %get-tuple-element.40.code_ref, f32[8,128]{1,0:T(8,128)S(1)} %collective-permute-done.4.after_ref.swap_a_in), custom_call_target="tpu_custom_call" | custom-call | flops 100000000 | bytes 100000 | tf_op jit(solution)/shard_map/pick_kernel/pallas_call | solution.py:358
  37.8 0.0 collective-permute-done.5.swap_b_in
  37.8 0.6 moment_kernel.1
  38.4 0.0 copy-start.3
  38.4 16.2 %all_to_all.34 = f32[32,1,128]{2,1,0:T(1,128)S(1)} all-to-all(f32[32,1,128]{2,1,0:T(1,128)S(1)} %bitcast.15), channel_id=1, replica_groups=mesh['fluid'=4,'solid'=8] {'fluid','solid'}, dimensions={0} | all-to-all | bytes 32768 | tf_op jit(solution)/shard_map/all_to_all | solution.py:391
  54.6 0.9 %blend_kernel.1 = (f32[24,128]{1,0:T(8,128)S(1)}, f32[512,128]{1,0:T(8,128)S(1)}) custom-call(f32[32,128]{1,0:T(8,128)S(1)} %bitcast.16, f32[8,128]{1,0:T(8,128)S(1)} %get-tuple-element.30.scale_ref, s32[8,512]{1,0:T(8,128)S(1)} %get-tuple-element.40.code_ref, f32[512,128]{1,0:T(8,128)S(1)} %pick_kernel.2.pick0_ref, f32[512,128]{1,0:T(8,128)S(1)} %pick_kernel.3.pick1_ref, ...), custom_call_target="tpu_custom_call" | custom-call | flops 1000000000 | bytes 1000000 | tf_op jit(solution)/shard_map/blend_kernel/pallas_call | solution.py:358
  55.5 12.3 %all_to_all.35 = f32[32,16,128]{2,1,0:T(8,128)S(1)} all-to-all(f32[32,16,128]{2,1,0:T(8,128)S(1)} %bitcast.12), channel_id=1, replica_groups=mesh['fluid'=4,'solid'=8] {'fluid','solid'}, dimensions={0} | all-to-all | bytes 524288 | tf_op jit(solution)/shard_map/all_to_all | solution.py:391
  67.8 0.0 copy-done.3
  67.8 1.5 %motion_kernel.1 = (f32[3,1024]{1,0:T(4,128)}, f32[1024,128]{1,0:T(8,128)}) custom-call(f32[512,128]{1,0:T(8,128)S(1)} %bitcast.11, s32[8,1024]{1,0:T(8,128)S(1)} %get-tuple-element.45.place_ref, f32[24,128]{1,0:T(8,128)S(1)} %copy-done.3, f32[24,128]{1,0:T(8,128)S(1)} %get-tuple-element.46.weights_ref, f32[48,128]{1,0:T(8,128)S(1)} %get-tuple-element.37.first_ref, ...), custom_call_target="tpu_custom_call" | custom-call | flops 1000000000 | bytes 1000000 | tf_op jit(solution)/shard_map/motion_kernel/pallas_call | solution.py:358
Async XLA Ops:
  0.6 19.9 %copy-start.2 = (f32[3,1024]{1,0:T(4,128)S(1)}, f32[3,1024]{1,0:T(4,128)}, u32[]{:S(2)}) copy-start(f32[3,1024]{1,0:T(4,128)} %support_ref.1) | copy-start | bytes 36868
  0.6 19.9 %copy-start.1 = (s32[8,1024]{1,0:T(8,128)S(1)}, s32[8,1024]{1,0:T(8,128)}, u32[]{:S(2)}) copy-start(s32[8,1024]{1,0:T(8,128)} %connectivity_ref.7) | copy-start | bytes 98308
  2.8 20.9 %copy-start = (f32[24,24,1024]{2,1,0:T(8,128)S(1)}, f32[24,24,1024]{2,1,0:T(8,128)}, u32[]{:S(2)}) copy-start(f32[24,24,1024]{2,1,0:T(8,128)} %stiffness_ref.5) | copy-start | bytes 7077892
  22.5 1.2 %collective-permute-start = (f32[8,128]{1,0:T(8,128)S(1)}, f32[8,128]{1,0:T(8,128)S(1)}, u32[]{:S(2)}, u32[]{:S(2)}) collective-permute-start(f32[8,128]{1,0:T(8,128)S(1)} %get-tuple-element.27), channel_id=1, source_target_pairs={{0,1},{2,3},{4,5},{6,7},{8,9},{10,11},{12,13},{14,15},{16,17},{18,... | collective-permute-start | bytes 12296 | tf_op jit(solution)/shard_map/ppermute | solution.py:388
  22.6 1.2 %collective-permute-start.1 = (f32[8,128]{1,0:T(8,128)S(1)}, f32[8,128]{1,0:T(8,128)S(1)}, u32[]{:S(2)}, u32[]{:S(2)}) collective-permute-start(f32[8,128]{1,0:T(8,128)S(1)} %get-tuple-element.28), channel_id=1, source_target_pairs={{1,2},{3,4},{5,6},{7,8},{9,10},{11,12},{13,14},{15,16},{17,18},{19... | collective-permute-start | bytes 12296 | tf_op jit(solution)/shard_map/ppermute | solution.py:388
  24.9 5.1 %collective-permute-start.2 = (f32[8,128]{1,0:T(8,128)S(1)}, f32[8,128]{1,0:T(8,128)S(1)}, u32[]{:S(2)}, u32[]{:S(2)}) collective-permute-start(f32[8,128]{1,0:T(8,128)S(1)} %get-tuple-element.32), channel_id=1, source_target_pairs={{0,1},{2,3},{4,5},{6,7},{8,9},{10,11},{12,13},{14,15},{16,17},{18,... | collective-permute-start | bytes 12296 | tf_op jit(solution)/shard_map/ppermute | solution.py:388
  29.3 0.8 %collective-permute-start.3 = (f32[8,128]{1,0:T(8,128)S(1)}, f32[8,128]{1,0:T(8,128)S(1)}, u32[]{:S(2)}, u32[]{:S(2)}) collective-permute-start(f32[8,128]{1,0:T(8,128)S(1)} %get-tuple-element.33), channel_id=1, source_target_pairs={{1,2},{3,4},{5,6},{7,8},{9,10},{11,12},{13,14},{15,16},{17,18},{19... | collective-permute-start | bytes 12296 | tf_op jit(solution)/shard_map/ppermute | solution.py:388
  31.3 5.7 %collective-permute-start.4 = (f32[8,128]{1,0:T(8,128)S(1)}, f32[8,128]{1,0:T(8,128)S(1)}, u32[]{:S(2)}, u32[]{:S(2)}) collective-permute-start(f32[8,128]{1,0:T(8,128)S(1)} %get-tuple-element.35), channel_id=1, source_target_pairs={{0,1},{2,3},{4,5},{6,7},{8,9},{10,11},{12,13},{14,15},{16,17},{18,... | collective-permute-start | bytes 12296 | tf_op jit(solution)/shard_map/ppermute | solution.py:388
  35.5 2.3 %collective-permute-start.5 = (f32[8,128]{1,0:T(8,128)S(1)}, f32[8,128]{1,0:T(8,128)S(1)}, u32[]{:S(2)}, u32[]{:S(2)}) collective-permute-start(f32[8,128]{1,0:T(8,128)S(1)} %get-tuple-element.36), channel_id=1, source_target_pairs={{1,2},{3,4},{5,6},{7,8},{9,10},{11,12},{13,14},{15,16},{17,18},{19... | collective-permute-start | bytes 12296 | tf_op jit(solution)/shard_map/ppermute | solution.py:388
  38.4 29.4 %copy-start.3 = (f32[24,128]{1,0:T(8,128)S(1)}, f32[24,128]{1,0:T(8,128)}, u32[]{:S(2)}) copy-start(f32[24,128]{1,0:T(8,128)} %table_ref.1) | copy-start | bytes 36868

commit v4 on v3

--- a/solution.py
+++ b/solution.py
@@ -201,12 +201,11 @@
     trace = jnp.sum(rows[:, 125:126]) * (1.0 / per)
     inverse = jnp.full((8, LANES), 3.0 * nodes * devices, F32) / jnp.full((8, LANES), trace, F32)
     scale_ref[...] = inverse
-    weight = as_field(support_ref[...], own_rows) * inverse[:1, :1] - 1.0
-    weight_ref[...] = jnp.where(own_mask(own_rows), weight, 0.0)
+    weight_ref[...] = as_field(support_ref[...], own_rows) * inverse[:1, :1]
 
 
 def product_kernel(own_rows, odd_ref, partial_ref, swap_a_in, swap_b_in, weight_ref, scale_ref, connectivity_ref,
-                   stiffness_ref, field_ref, values_ref, next_ref, swap_a_ref, swap_b_ref):
+                   stiffness_ref, field_ref, values_ref, forces_ref, next_ref, swap_a_ref, swap_b_ref):
     odd = odd_ref[0] == 1
     field = add_ends(partial_ref[...], odd, own_rows, swap_a_in[...], swap_b_in[...])
     field_ref[...] = field
@@ -214,70 +213,117 @@
     values = gather_corners(field, connectivity)
     values_ref[...] = jnp.concatenate(values, axis=0)
     forces = matvec(stiffness_ref, values)
+    forces_ref[...] = forces
     partial = assemble(forces, connectivity) * scale_ref[:1, :1] + weight_ref[...] * field
     next_ref[...] = partial
     put_ends(partial, odd, own_rows, swap_a_ref, swap_b_ref)
 
 
+def entries(pairs):
+    lane = iota((1, LANES), 1)
+    row = jnp.zeros((1, LANES), F32)
+    for i, value in pairs:
+        row = jnp.where(lane == i, value, row)
+    return row
+
+
+def share(value, norm):
+    return jnp.full((1, LANES), value, F32) / jnp.maximum(jnp.full((1, LANES), norm, F32), 1e-30)
+
+
+def lower_kernel(own_rows, weight_ref, scale_ref, first_ref, second_ref, values0_ref, values1_ref,
+                 forces0_ref, forces1_ref, after_ref, own0_ref, own1_ref, turned_ref, numbers_ref):
+    del after_ref
+    own, weight = own_mask(own_rows), weight_ref[...]
+    first, second = jnp.where(own, first_ref[...], 0.0), jnp.where(own, second_ref[...], 0.0)
+    norm0 = jnp.sum(first * first)
+    theta = share(jnp.sum(first * second), norm0)
+    second = second - theta * first
+    own0_ref[...], own1_ref[...] = first, second
+    scale, part = scale_ref[:1, :1], theta[:, :1]
+    values0, forces0 = values0_ref[...], forces0_ref[...]
+    values1, forces1 = values1_ref[...] - part * values0, forces1_ref[...] - part * forces0
+    turned_ref[...] = values1
+    norm1 = jnp.sum(second * second)
+    row = entries([
+        (0, norm0),
+        (1, jnp.sum(first * second)),
+        (2, norm1),
+        (6, jnp.sum(values0 * forces0) * scale + jnp.sum(weight * first * first)),
+        (7, jnp.sum(values0 * forces1) * scale + jnp.sum(weight * first * second)),
+        (8, jnp.sum(values1 * forces1) * scale + jnp.sum(weight * second * second)),
+        (12, theta),
+    ])
+    numbers_ref[...] = jnp.concatenate(
+        [row, share(1.0, norm0), share(1.0, norm1), jnp.zeros((5, LANES), F32)], axis=0)
+
+
 def moment_kernel(own_rows, devices, odd_ref, partial_ref, swap_a_in, swap_b_in, weight_ref, scale_ref,
-                  connectivity_ref, stiffness_ref, first_ref, second_ref, pick0_ref, pick1_ref,
-                  field_ref, values_ref, moments_ref):
+                  connectivity_ref, stiffness_ref, own0_ref, own1_ref, values0_ref, turned_ref, numbers_ref,
+                  pick0_ref, pick1_ref, field_ref, values_ref, moments_ref):
     del pick0_ref, pick1_ref
     odd = odd_ref[0] == 1
-    third = add_ends(partial_ref[...], odd, own_rows, swap_a_in[...], swap_b_in[...])
-    field_ref[...] = third
-    values = gather_corners(third, connectivity_ref[...])
-    forces = matvec(stiffness_ref, values)
-    values = jnp.concatenate(values, axis=0)
-    values_ref[...] = values
-    energy = jnp.sum(forces * values, axis=0, keepdims=True)
-    own = own_mask(own_rows)
-    first, second = jnp.where(own, first_ref[...], 0.0), jnp.where(own, second_ref[...], 0.0)
-    owned = jnp.where(own, third, 0.0)
-    moments = [
-        jnp.sum(first * first),
-        jnp.sum(first * second),
-        jnp.sum(second * second),
-        jnp.sum(second * owned),
-        jnp.sum(owned * owned),
-        jnp.sum(energy) * scale_ref[:1, :1] + jnp.sum(weight_ref[...] * owned * owned),
+    field = add_ends(partial_ref[...], odd, own_rows, swap_a_in[...], swap_b_in[...])
+    field_ref[...] = field
+    weight, scale = weight_ref[...], scale_ref[:1, :1]
+    first, second = own0_ref[...], own1_ref[...]
+    third = jnp.where(own_mask(own_rows), field, 0.0)
+    phi = jnp.sum(first * third) * numbers_ref[1:2]
+    psi = jnp.sum(second * third) * numbers_ref[2:3]
+    third = third - psi * second - phi * first
+    values0, values1 = values0_ref[...], turned_ref[...]
+    values2 = jnp.concatenate(gather_corners(field, connectivity_ref[...]), axis=0)
+    values_ref[...] = values2
+    values2 = values2 - psi[:, :1] * values1 - phi[:, :1] * values0
+    forces2 = matvec(stiffness_ref, [values2[c * CORNERS:(c + 1) * CORNERS] for c in range(3)])
+    weighted = weight * third
+    row = numbers_ref[:1] + entries([
+        (3, jnp.sum(first * third)),
+        (4, jnp.sum(second * third)),
+        (5, jnp.sum(third * third)),
+        (9, jnp.sum(values0 * forces2) * scale + jnp.sum(first * weighted)),
+        (10, jnp.sum(values1 * forces2) * scale + jnp.sum(second * weighted)),
+        (11, jnp.sum(values2 * forces2) * scale + jnp.sum(third * weighted)),
+        (13, psi),
+        (14, phi),
+    ])
+    moments_ref[...] = jnp.broadcast_to(row, (devices, LANES))
+
+
+def step_weights(rows):
+    column = [rows[:, i:i + 1] for i in range(15)]
+    norms, energies, (theta, psi, phi) = column[:6], column[6:12], column[12:]
+
+    def square(matrix, y):
+        total = y[0] * y[0] * matrix[0]
+        if len(y) > 1:
+            total = total + y[1] * (2.0 * y[0] * matrix[1] + y[1] * matrix[2])
+        if len(y) > 2:
+            total = total + y[2] * (2.0 * (y[0] * matrix[3] + y[1] * matrix[4]) + y[2] * matrix[5])
+        return jnp.sum(total, axis=0, keepdims=True)
+
+    norm0 = jnp.sum(norms[0], axis=0, keepdims=True)
+    step0 = norm0 / jnp.sum(energies[0], axis=0, keepdims=True)
+    residual = [1.0 - step0 * theta, -step0]
+    norm1 = square(norms, residual)
+    turn0 = norm1 / norm0
+    direction = [residual[0] + turn0, -step0]
+    step1 = norm1 / square(energies, direction)
+    lead = 1.0 + turn0
+    residual = [
+        residual[0] - step1 * (lead * theta - step0 * phi),
+        -step0 - step1 * (lead - step0 * psi),
+        step1 * step0,
     ]
-    lane = iota((devices, LANES), 1)
-    row = jnp.zeros((devices, LANES), F32)
-    for i, moment in enumerate(moments):
-        row = jnp.where(lane == i, moment, row)
-    moments_ref[...] = row
-
-
-def step_weights(m):
-    def dot(p, q):
-        terms = [p[i] * q[j] * m[i + j] for i in range(3) for j in range(3) if p[i] is not None and q[j] is not None]
-        return functools.reduce(lambda a, b: a + b, terms)
-
-    def energy(p):
-        terms = [p[i] * p[j] * (m[i + j + 1] + m[i + j]) for i in range(3) for j in range(3)
-                 if p[i] is not None and p[j] is not None]
-        return functools.reduce(lambda a, b: a + b, terms)
-
-    norm0 = m[0]
-    curve0 = m[0] + m[1]
-    step0 = norm0 / curve0
-    residual = [m[1] / curve0, -step0, None]
-    norm1 = dot(residual, residual)
-    turn0 = norm1 / norm0
-    direction = [residual[0] + turn0, residual[1], None]
-    step1 = norm1 / energy(direction)
-    result = [step0 + step1 * direction[0], step1 * direction[1]]
-    residual = [
-        residual[0] - step1 * direction[0],
-        residual[1] - step1 * (direction[0] + direction[1]),
-        -step1 * direction[1],
+    norm2 = square(norms, residual)
+    turn1 = norm2 / norm1
+    direction = [residual[0] + turn1 * direction[0], residual[1] - turn1 * step0, residual[2]]
+    step2 = norm2 / square(energies, direction)
+    return [
+        step0 + step1 * lead + step2 * (1.0 + turn1 * lead),
+        -step1 * step0 - step2 * (step0 + step1 * lead + turn1 * step0),
+        step2 * step1 * step0,
     ]
-    norm2 = dot(residual, residual)
-    turn1 = norm2 / norm1
-    direction = [residual[0] + turn1 * direction[0], residual[1] + turn1 * direction[1], residual[2]]
-    step2 = norm2 / energy(direction)
-    return [result[0] + step2 * direction[0], result[1] + step2 * direction[1], step2 * direction[2]]
 
 
 def pick(values, code_ref, out_ref, blend):
@@ -304,8 +350,7 @@
 
 
 def blend_kernel(moments_ref, scale_ref, code_ref, pick0_ref, pick1_ref, values_ref, weights_ref, out_ref):
-    sums = jnp.sum(moments_ref[...], axis=0, keepdims=True)
-    weights = step_weights([sums[:, i:i + 1] for i in range(6)])
+    weights = step_weights(moments_ref[...])
     weights = [weight * scale_ref[:1, :1] for weight in weights]
     weights_ref[...] = jnp.concatenate([jnp.broadcast_to(weight, (8, LANES)) for weight in weights], axis=0)
 
@@ -417,35 +462,43 @@
         (odd, arrived, connectivity, support),
         scalars=1,
     )
-    fields, picks = [], []
+    stage = (
+        functools.partial(product_kernel, own_rows),
+        [field, values, values, field, ends, ends],
+    )
     end_a, end_b = swap(end_a, end_b)
-    for _ in range(2):
-        full, corners, partial, end_a, end_b = call(
-            functools.partial(product_kernel, own_rows),
-            [field, values, field, ends, ends],
-            (odd, partial, end_a, end_b, weight, scale, connectivity, stiffness),
-            scalars=1,
-        )
-        fields.append(full)
-        end_a, end_b = swap(end_a, end_b)
-        picks += call(pick_kernel, [block], (corners, codes, end_a), time=0.1)
-    third, corners, moments = call(
+    first, values0, forces0, partial, end_a, end_b = call(
+        *stage, (odd, partial, end_a, end_b, weight, scale, connectivity, stiffness), scalars=1)
+    end_a, end_b = swap(end_a, end_b)
+    (pick0,) = call(pick_kernel, [block], (values0, codes, end_a), time=0.1)
+    second, values1, forces1, partial, end_a, end_b = call(
+        *stage, (odd, partial, end_a, end_b, weight, scale, connectivity, stiffness), scalars=1)
+    end_a, end_b = swap(end_a, end_b)
+    (pick1,) = call(pick_kernel, [block], (values1, codes, end_a), time=0.1)
+    own0, own1, turned, numbers = call(
+        functools.partial(lower_kernel, own_rows),
+        [field, field, values, ends],
+        (weight, scale, first, second, values0, values1, forces0, forces1, end_a),
+        time=0.1,
+    )
+    third, values2, moments = call(
         functools.partial(moment_kernel, own_rows, devices),
         [field, values, ((devices, LANES), F32)],
-        (odd, partial, end_a, end_b, weight, scale, connectivity, stiffness, *fields, *picks),
+        (odd, partial, end_a, end_b, weight, scale, connectivity, stiffness, own0, own1, values0, turned, numbers,
+         pick0, pick1),
         scalars=1,
     )
     moments = everywhere(moments)
     weights, leaving = call(
         blend_kernel,
         [((24, LANES), F32), block],
-        (moments, scale, codes, *picks, corners),
+        (moments, scale, codes, pick0, pick1, values2),
     )
     returned = everywhere(leaving)
     return call(
         functools.partial(motion_kernel, own_rows),
         [((3, nodes), F32), ((faces, LANES), F32)],
-        (returned, place, shape_table, weights, *fields, third),
+        (returned, place, shape_table, weights, first, second, third),
         outs_hbm=(0, 1),
         scratch=(
             pltpu.VMEM((3, nodes), F32),

time: 69.6 us -> 69.7 us (level)
    pallas_call x9 -> x10, Pallas kernels: 11.1 us -> 11.6 us  [call(): pl.pallas_call(kernel, name=getattr(kernel, 'func', kernel).__name__, out...]
  transfers between devices with their start and end apart: 6 -> 6, of which waited for: 2 -> 2; matrix products, arithmetic and copies ran while one was open for 0% -> 0% of each run, Pallas kernels for 2% -> 3%
where the time goes in v4:
time: 69.7 us; the launch traced here: 69.4 us
  blocking collectives  45.8 us (66%)
  Pallas kernels  11.6 us (17%)
  starting transfers between devices  10.5 us (15%)
  between operations  0.75 us (1%)
    all_to_all x3, blocking collectives, everywhere(): return lax.all_to_all(rows, AXES, split_axis=0, concat_axis=0, tiled=True)  45.8 us
    pallas_call x10, Pallas kernels, call(): pl.pallas_call(kernel, name=getattr(kernel, 'func', kernel).__name__, out...  11.6 us
    ppermute x6, starting transfers between devices, swap(): return (lax.ppermute(a, AXES, pairs_a), lax.ppermute(b, AXES, pairs_b))  10.5 us
  transfers between devices with their start and end apart: 6, of which 2 were waited for; matrix products, arithmetic and copies ran while one was open for 0% of the time, Pallas kernels for 3%

profile of v4, /device:TPU:0, one launch (start us, length us, event | category | flops | bytes accessed | tf_op | source)
XLA Modules:
  0.0 69.4 jit_solution(7584819602818313893)
XLA Ops:
  0.6 0.0 copy-start.2
  0.6 0.0 copy-start.1
  0.7 2.2 %send_kernel.1 = (f32[512,128]{1,0:T(8,128)S(1)}, s32[8,1024]{1,0:T(8,128)S(1)}) custom-call(s32[1]{0:T(128)} %bitcast.odd_ref, f32[1024,128]{1,0:T(8,128)} %pressure_hbm.1, s32[1,1024]{1,0:T(1,128)} %bitcast.17, s32[1,1024]{1,0:T(1,128)} %bitcast.18, f32[24,128]{1,0:T(8,128)} %table_ref.1, f32[3,1024]{1,0:T(4,128)} %support_ref.1, f32[24,24,1024]{2,1,0:T(8,128)} %stiffness_ref.5), custom_call_target="tpu_custom_call" | custom-call | flops 1000000000 | bytes 1000000 | tf_op jit(solution)/shard_map/send_kernel/pallas_call | solution.py:403
  2.8 0.0 copy-start
  2.9 17.7 %all_to_all.33 = f32[32,16,128]{2,1,0:T(8,128)S(1)} all-to-all(f32[32,16,128]{2,1,0:T(8,128)S(1)} %bitcast.14), channel_id=1, replica_groups=mesh['fluid'=4,'solid'=8] {'fluid','solid'}, dimensions={0} | all-to-all | bytes 524288 | tf_op jit(solution)/shard_map/all_to_all | solution.py:436
  20.6 0.0 copy-done.2
  20.6 0.0 copy-done.1
  20.6 1.9 %load_kernel.1 = (f32[48,128]{1,0:T(8,128)S(1)}, f32[8,128]{1,0:T(8,128)S(1)}, f32[8,128]{1,0:T(8,128)S(1)}, f32[48,128]{1,0:T(8,128)S(1)}, f32[8,128]{1,0:T(8,128)S(1)}, /*index=5*/s32[8,512]{1,0:T(8,128)S(1)}) custom-call(s32[1]{0:T(128)} %bitcast.odd_ref, f32[512,128]{1,0:T(8,128)S(1)} %bitcast.13, s32[8,1024]{1,0:T(8,128)S(1)} %copy-done.1, ...), custom_call_target="tpu_custom_call" | custom-call | flops 1000000000 | bytes 1000000 | tf_op jit(solution)/shard_map/load_kernel/pallas_call | solution.py:403
  22.5 0.1 collective-permute-start
  22.6 0.7 collective-permute-start.1
  23.3 0.5 collective-permute-done.swap_a_in
  23.7 0.0 collective-permute-done.1.swap_b_in
  23.7 0.0 copy-done
  23.7 1.2 %product_kernel.2 = (f32[48,128]{1,0:T(8,128)S(1)}, f32[24,1024]{1,0:T(8,128)S(1)}, f32[24,1024]{1,0:T(8,128)S(1)}, f32[48,128]{1,0:T(8,128)S(1)}, f32[8,128]{1,0:T(8,128)S(1)}, /*index=5*/f32[8,128]{1,0:T(8,128)S(1)}) custom-call(s32[1]{0:T(128)} %bitcast.odd_ref, f32[48,128]{1,0:T(8,128)S(1)} %get-tuple-element.32.partial_ref, ...), custom_call_target="tpu_custom_call" | custom-call | flops 1000000000 | bytes 1000000 | tf_op jit(solution)/shard_map/product_kernel/pallas_call | solution.py:403
  24.9 4.3 %collective-permute-start.2 = (f32[8,128]{1,0:T(8,128)S(1)}, f32[8,128]{1,0:T(8,128)S(1)}, u32[]{:S(2)}, u32[]{:S(2)}) collective-permute-start(f32[8,128]{1,0:T(8,128)S(1)} %get-tuple-element.38), channel_id=1, source_target_pairs={{0,1},{2,3},{4,5},{6,7},{8,9},{10,11},{12,13},{14,15},{16,17},{18,... | collective-permute-start | bytes 12296 | tf_op jit(solution)/shard_map/ppermute | solution.py:433
  29.3 0.6 collective-permute-start.3
  29.9 0.2 collective-permute-done.2.swap_a_in.after_ref
  30.1 0.0 collective-permute-done.3.swap_b_in
  30.1 1.2 %product_kernel.3 = (f32[48,128]{1,0:T(8,128)S(1)}, f32[24,1024]{1,0:T(8,128)S(1)}, f32[24,1024]{1,0:T(8,128)S(1)}, f32[48,128]{1,0:T(8,128)S(1)}, f32[8,128]{1,0:T(8,128)S(1)}, /*index=5*/f32[8,128]{1,0:T(8,128)S(1)}) custom-call(s32[1]{0:T(128)} %bitcast.odd_ref, f32[48,128]{1,0:T(8,128)S(1)} %get-tuple-element.37.partial_ref, ...), custom_call_target="tpu_custom_call" | custom-call | flops 1000000000 | bytes 1000000 | tf_op jit(solution)/shard_map/product_kernel/pallas_call | solution.py:403
  31.3 4.2 %collective-permute-start.4 = (f32[8,128]{1,0:T(8,128)S(1)}, f32[8,128]{1,0:T(8,128)S(1)}, u32[]{:S(2)}, u32[]{:S(2)}) collective-permute-start(f32[8,128]{1,0:T(8,128)S(1)} %get-tuple-element.41), channel_id=1, source_target_pairs={{0,1},{2,3},{4,5},{6,7},{8,9},{10,11},{12,13},{14,15},{16,17},{18,... | collective-permute-start | bytes 12296 | tf_op jit(solution)/shard_map/ppermute | solution.py:433
  35.5 0.6 collective-permute-start.5
  36.1 0.8 %pick_kernel.2.pick0_ref = f32[512,128]{1,0:T(8,128)S(1)} custom-call(f32[24,1024]{1,0:T(8,128)S(1)} %get-tuple-element.45.values0_ref.values_ref, s32[8,512]{1,0:T(8,128)S(1)} %get-tuple-element.53.code_ref, f32[8,128]{1,0:T(8,128)S(1)} %collective-permute-done.2.swap_a_in.after_ref), custom_call_target="tpu_custom_call" | custom-call | flops 100000000 | bytes 100000 | tf_op jit(solution)/shard_map/pick_kernel/pallas_call | solution.py:403
  36.9 0.0 collective-permute-done.4.after_ref.swap_a_in
  36.9 0.8 %pick_kernel.3.pick1_ref = f32[512,128]{1,0:T(8,128)S(1)} custom-call(f32[24,1024]{1,0:T(8,128)S(1)} %get-tuple-element.46.values1_ref.values_ref, s32[8,512]{1,0:T(8,128)S(1)} %get-tuple-element.53.code_ref, f32[8,128]{1,0:T(8,128)S(1)} %collective-permute-done.4.after_ref.swap_a_in), custom_call_target="tpu_custom_call" | custom-call | flops 100000000 | bytes 100000 | tf_op jit(solution)/shard_map/pick_kernel/pallas_call | solution.py:403
  37.8 0.4 lower_kernel.1
  38.1 0.0 collective-permute-done.5.swap_b_in
  38.1 0.7 %moment_kernel.1 = (f32[48,128]{1,0:T(8,128)S(1)}, f32[24,1024]{1,0:T(8,128)S(1)}, f32[32,128]{1,0:T(8,128)S(1)}) custom-call(s32[1]{0:T(128)} %bitcast.odd_ref, f32[48,128]{1,0:T(8,128)S(1)} %get-tuple-element.40.partial_ref, f32[8,128]{1,0:T(8,128)S(1)} %collective-permute-done.4.after_ref.swap_a_in, f32[8,128]{1,0:T(8,128)S(1)} %collective-permute-done.5.swap_b_in, ...), custom_call_target="tpu_custom_call" | custom-call | flops 1000000000 | bytes 1000000 | tf_op jit(solution)/shard_map/moment_kernel/pallas_call | solution.py:403
  38.9 15.8 %all_to_all.34 = f32[32,1,128]{2,1,0:T(1,128)S(1)} all-to-all(f32[32,1,128]{2,1,0:T(1,128)S(1)} %bitcast.15), channel_id=1, replica_groups=mesh['fluid'=4,'solid'=8] {'fluid','solid'}, dimensions={0} | all-to-all | bytes 32768 | tf_op jit(solution)/shard_map/all_to_all | solution.py:436
  54.7 0.9 %blend_kernel.1 = (f32[24,128]{1,0:T(8,128)S(1)}, f32[512,128]{1,0:T(8,128)S(1)}) custom-call(f32[32,128]{1,0:T(8,128)S(1)} %bitcast.16, f32[8,128]{1,0:T(8,128)S(1)} %get-tuple-element.36.scale_ref, s32[8,512]{1,0:T(8,128)S(1)} %get-tuple-element.53.code_ref, f32[512,128]{1,0:T(8,128)S(1)} %pick_kernel.2.pick0_ref, f32[512,128]{1,0:T(8,128)S(1)} %pick_kernel.3.pick1_ref, ...), custom_call_target="tpu_custom_call" | custom-call | flops 1000000000 | bytes 1000000 | tf_op jit(solution)/shard_map/blend_kernel/pallas_call | solution.py:403
  55.6 12.3 %all_to_all.35 = f32[32,16,128]{2,1,0:T(8,128)S(1)} all-to-all(f32[32,16,128]{2,1,0:T(8,128)S(1)} %bitcast.12), channel_id=1, replica_groups=mesh['fluid'=4,'solid'=8] {'fluid','solid'}, dimensions={0} | all-to-all | bytes 524288 | tf_op jit(solution)/shard_map/all_to_all | solution.py:436
  67.9 0.0 copy-done.3
  67.9 1.5 %motion_kernel.1 = (f32[3,1024]{1,0:T(4,128)}, f32[1024,128]{1,0:T(8,128)}) custom-call(f32[512,128]{1,0:T(8,128)S(1)} %bitcast.11, s32[8,1024]{1,0:T(8,128)S(1)} %get-tuple-element.57.place_ref, f32[24,128]{1,0:T(8,128)S(1)} %copy-done.3, f32[24,128]{1,0:T(8,128)S(1)} %get-tuple-element.58.weights_ref, f32[48,128]{1,0:T(8,128)S(1)} %get-tuple-element.43.first_ref, ...), custom_call_target="tpu_custom_call" | custom-call | flops 1000000000 | bytes 1000000 | tf_op jit(solution)/shard_map/motion_kernel/pallas_call | solution.py:403
  (1 shorter events, 0.0 us)
Async XLA Ops:
  0.6 19.9 %copy-start.2 = (f32[3,1024]{1,0:T(4,128)S(1)}, f32[3,1024]{1,0:T(4,128)}, u32[]{:S(2)}) copy-start(f32[3,1024]{1,0:T(4,128)} %support_ref.1) | copy-start | bytes 36868
  0.6 19.9 %copy-start.1 = (s32[8,1024]{1,0:T(8,128)S(1)}, s32[8,1024]{1,0:T(8,128)}, u32[]{:S(2)}) copy-start(s32[8,1024]{1,0:T(8,128)} %connectivity_ref.7) | copy-start | bytes 98308
  2.8 20.9 %copy-start = (f32[24,24,1024]{2,1,0:T(8,128)S(1)}, f32[24,24,1024]{2,1,0:T(8,128)}, u32[]{:S(2)}) copy-start(f32[24,24,1024]{2,1,0:T(8,128)} %stiffness_ref.5) | copy-start | bytes 7077892
  22.5 1.2 %collective-permute-start = (f32[8,128]{1,0:T(8,128)S(1)}, f32[8,128]{1,0:T(8,128)S(1)}, u32[]{:S(2)}, u32[]{:S(2)}) collective-permute-start(f32[8,128]{1,0:T(8,128)S(1)} %get-tuple-element.33), channel_id=1, source_target_pairs={{0,1},{2,3},{4,5},{6,7},{8,9},{10,11},{12,13},{14,15},{16,17},{18,... | collective-permute-start | bytes 12296 | tf_op jit(solution)/shard_map/ppermute | solution.py:433
  22.6 1.2 %collective-permute-start.1 = (f32[8,128]{1,0:T(8,128)S(1)}, f32[8,128]{1,0:T(8,128)S(1)}, u32[]{:S(2)}, u32[]{:S(2)}) collective-permute-start(f32[8,128]{1,0:T(8,128)S(1)} %get-tuple-element.34), channel_id=1, source_target_pairs={{1,2},{3,4},{5,6},{7,8},{9,10},{11,12},{13,14},{15,16},{17,18},{19... | collective-permute-start | bytes 12296 | tf_op jit(solution)/shard_map/ppermute | solution.py:433
  24.9 5.1 %collective-permute-start.2 = (f32[8,128]{1,0:T(8,128)S(1)}, f32[8,128]{1,0:T(8,128)S(1)}, u32[]{:S(2)}, u32[]{:S(2)}) collective-permute-start(f32[8,128]{1,0:T(8,128)S(1)} %get-tuple-element.38), channel_id=1, source_target_pairs={{0,1},{2,3},{4,5},{6,7},{8,9},{10,11},{12,13},{14,15},{16,17},{18,... | collective-permute-start | bytes 12296 | tf_op jit(solution)/shard_map/ppermute | solution.py:433
  29.3 0.8 %collective-permute-start.3 = (f32[8,128]{1,0:T(8,128)S(1)}, f32[8,128]{1,0:T(8,128)S(1)}, u32[]{:S(2)}, u32[]{:S(2)}) collective-permute-start(f32[8,128]{1,0:T(8,128)S(1)} %get-tuple-element.39), channel_id=1, source_target_pairs={{1,2},{3,4},{5,6},{7,8},{9,10},{11,12},{13,14},{15,16},{17,18},{19... | collective-permute-start | bytes 12296 | tf_op jit(solution)/shard_map/ppermute | solution.py:433
  31.3 5.7 %collective-permute-start.4 = (f32[8,128]{1,0:T(8,128)S(1)}, f32[8,128]{1,0:T(8,128)S(1)}, u32[]{:S(2)}, u32[]{:S(2)}) collective-permute-start(f32[8,128]{1,0:T(8,128)S(1)} %get-tuple-element.41), channel_id=1, source_target_pairs={{0,1},{2,3},{4,5},{6,7},{8,9},{10,11},{12,13},{14,15},{16,17},{18,... | collective-permute-start | bytes 12296 | tf_op jit(solution)/shard_map/ppermute | solution.py:433
  35.5 2.7 %collective-permute-start.5 = (f32[8,128]{1,0:T(8,128)S(1)}, f32[8,128]{1,0:T(8,128)S(1)}, u32[]{:S(2)}, u32[]{:S(2)}) collective-permute-start(f32[8,128]{1,0:T(8,128)S(1)} %get-tuple-element.42), channel_id=1, source_target_pairs={{1,2},{3,4},{5,6},{7,8},{9,10},{11,12},{13,14},{15,16},{17,18},{19... | collective-permute-start | bytes 12296 | tf_op jit(solution)/shard_map/ppermute | solution.py:433
  38.9 29.0 %copy-start.3 = (f32[24,128]{1,0:T(8,128)S(1)}, f32[24,128]{1,0:T(8,128)}, u32[]{:S(2)}) copy-start(f32[24,128]{1,0:T(8,128)} %table_ref.1) | copy-start | bytes 36868

commit v5 on v4

--- a/solution.py
+++ b/solution.py
@@ -63,7 +63,7 @@
     return [jnp.concatenate(part, axis=1) for part in parts]
 
 
-def assemble(terms, connectivity):
+def assemble(terms, connectivity, columns_ref=None):
     elements = connectivity.shape[1]
     high, low = connectivity >> 7, connectivity & 127
     upper = terms.astype(BF16).astype(F32)
@@ -77,8 +77,18 @@
             for c in range(3)
         ]
         left = jnp.concatenate(pieces, axis=0).astype(BF16)
-        total = total + dot_nt(left, onehot(iota((LANES, elements), 0) == low[k:k + 1]))
+        if columns_ref is None:
+            total = total + dot_nt(left, onehot(iota((LANES, elements), 0) == low[k:k + 1]))
+        else:
+            total = total + dot_nn(left, columns_ref[k])
     return total[:3 * FIELD_ROWS] + total[3 * FIELD_ROWS:]
+
+
+def columns_kernel(connectivity_ref, after_ref, out_ref):
+    del after_ref
+    low = connectivity_ref[...] & 127
+    for k in range(CORNERS):
+        out_ref[k] = jnp.where(iota((LANES, low.shape[1]), 0) == low[k:k + 1], 1.0, 0.0).T.astype(BF16)
 
 
 def matvec(stiffness, values):
@@ -177,44 +187,52 @@
 
 
 def load_kernel(devices, per, odd_ref, rows_ref, connectivity_ref, support_ref,
-                partial_ref, swap_a_ref, swap_b_ref, weight_ref, scale_ref, code_ref):
+                partial_ref, swap_a_ref, swap_b_ref, weight_ref, scale_ref, code_ref, loads_ref):
     nodes = support_ref.shape[1]
     own_rows = nodes // LANES
-    rows = rows_ref[...]
-    slots = rows.shape[0]
-    arrived = rows.T
-    codes = arrived[GROUPS * DOF:].astype(jnp.int32)
-    code_ref[...] = codes
-    total = jnp.zeros((4 * 2 * DOF, WIDE), F32)
-    for g in range(GROUPS):
-        terms = arrived[g * DOF:(g + 1) * DOF]
-        upper = terms.astype(BF16).astype(F32)
-        both = jnp.concatenate([upper, terms - upper], axis=0)
-        code = codes[g:g + 1]
-        left = jnp.concatenate([jnp.where((code >> 8) == i, both, 0.0) for i in range(4)], axis=0).astype(BF16)
-        total = total + dot_nt(left, onehot(iota((WIDE, slots), 0) == (code & 255)))
-    loads = jnp.concatenate(
-        [total[i * 2 * DOF:i * 2 * DOF + DOF] + total[i * 2 * DOF + DOF:(i + 1) * 2 * DOF] for i in range(4)], axis=1)
-    partial = assemble(loads, connectivity_ref[...])
+
+    @pl.when(odd_ref[0] >= 0)
+    def _():
+        rows = rows_ref[...]
+        arrived = rows.T
+        codes = arrived[GROUPS * DOF:].astype(jnp.int32)
+        code_ref[...] = codes
+        slots = rows.shape[0]
+        total = jnp.zeros((4 * 2 * DOF, WIDE), F32)
+        for g in range(GROUPS):
+            terms = arrived[g * DOF:(g + 1) * DOF]
+            upper = terms.astype(BF16).astype(F32)
+            both = jnp.concatenate([upper, terms - upper], axis=0)
+            code = codes[g:g + 1]
+            left = jnp.concatenate([jnp.where((code >> 8) == i, both, 0.0) for i in range(4)], axis=0).astype(BF16)
+            total = total + dot_nt(left, onehot(iota((WIDE, slots), 0) == (code & 255)))
+        for i in range(4):
+            start = i * 2 * DOF
+            loads_ref[:, i * WIDE:(i + 1) * WIDE] = total[start:start + DOF] + total[start + DOF:start + 2 * DOF]
+
+    partial = assemble(loads_ref[...], connectivity_ref[...])
     partial_ref[...] = partial
     put_ends(partial, odd_ref[0] == 1, own_rows, swap_a_ref, swap_b_ref)
-    trace = jnp.sum(rows[:, 125:126]) * (1.0 / per)
+    trace = jnp.sum(rows_ref[:, 125:126]) * (1.0 / per)
     inverse = jnp.full((8, LANES), 3.0 * nodes * devices, F32) / jnp.full((8, LANES), trace, F32)
     scale_ref[...] = inverse
     weight_ref[...] = as_field(support_ref[...], own_rows) * inverse[:1, :1]
 
 
 def product_kernel(own_rows, odd_ref, partial_ref, swap_a_in, swap_b_in, weight_ref, scale_ref, connectivity_ref,
-                   stiffness_ref, field_ref, values_ref, forces_ref, next_ref, swap_a_ref, swap_b_ref):
+                   stiffness_ref, columns_ref, field_ref, values_ref, forces_ref, next_ref, swap_a_ref, swap_b_ref):
     odd = odd_ref[0] == 1
-    field = add_ends(partial_ref[...], odd, own_rows, swap_a_in[...], swap_b_in[...])
-    field_ref[...] = field
-    connectivity = connectivity_ref[...]
-    values = gather_corners(field, connectivity)
-    values_ref[...] = jnp.concatenate(values, axis=0)
-    forces = matvec(stiffness_ref, values)
-    forces_ref[...] = forces
-    partial = assemble(forces, connectivity) * scale_ref[:1, :1] + weight_ref[...] * field
+
+    @pl.when(odd_ref[0] >= 0)
+    def _():
+        field = add_ends(partial_ref[...], odd, own_rows, swap_a_in[...], swap_b_in[...])
+        field_ref[...] = field
+        values = gather_corners(field, connectivity_ref[...])
+        values_ref[...] = jnp.concatenate(values, axis=0)
+        forces_ref[...] = matvec(stiffness_ref, values)
+
+    partial = assemble(forces_ref[...], connectivity_ref[...], columns_ref)
+    partial = partial * scale_ref[:1, :1] + weight_ref[...] * field_ref[...]
     next_ref[...] = partial
     put_ends(partial, odd, own_rows, swap_a_ref, swap_b_ref)
 
@@ -461,18 +479,21 @@
         [field, ends, ends, field, ends, ((8, slots), jnp.int32)],
         (odd, arrived, connectivity, support),
         scalars=1,
+        scratch=(pltpu.VMEM((DOF, elements), F32),),
     )
     stage = (
         functools.partial(product_kernel, own_rows),
         [field, values, values, field, ends, ends],
     )
     end_a, end_b = swap(end_a, end_b)
+    (columns,) = call(
+        columns_kernel, [((CORNERS, elements, LANES), BF16)], (connectivity, end_a), time=0.1)
     first, values0, forces0, partial, end_a, end_b = call(
-        *stage, (odd, partial, end_a, end_b, weight, scale, connectivity, stiffness), scalars=1)
+        *stage, (odd, partial, end_a, end_b, weight, scale, connectivity, stiffness, columns), scalars=1)
     end_a, end_b = swap(end_a, end_b)
     (pick0,) = call(pick_kernel, [block], (values0, codes, end_a), time=0.1)
     second, values1, forces1, partial, end_a, end_b = call(
-        *stage, (odd, partial, end_a, end_b, weight, scale, connectivity, stiffness), scalars=1)
+        *stage, (odd, partial, end_a, end_b, weight, scale, connectivity, stiffness, columns), scalars=1)
     end_a, end_b = swap(end_a, end_b)
     (pick1,) = call(pick_kernel, [block], (values1, codes, end_a), time=0.1)
     own0, own1, turned, numbers = call(

time: 69.7 us -> 68.8 us (0.987)
  starting transfers between devices: 10.5 us -> 9.79 us
    ppermute x6, starting transfers between devices: 10.5 us -> 9.79 us  [swap(): return (lax.ppermute(a, AXES, pairs_a), lax.ppermute(b, AXES, pairs_b))]
    pallas_call x10 -> x11, Pallas kernels: 11.6 us -> 11.5 us  [call(): pl.pallas_call(kernel, name=getattr(kernel, 'func', kernel).__name__, out...]
  transfers between devices with their start and end apart: 6 -> 6, of which waited for: 2 -> 2; matrix products, arithmetic and copies ran while one was open for 0% -> 0% of each run, Pallas kernels for 3% -> 4%
where the time goes in v5:
time: 68.8 us; the launch traced here: 68.5 us
  blocking collectives  45.8 us (67%)
  Pallas kernels  11.5 us (17%)
  starting transfers between devices  9.79 us (14%)
  between operations  0.75 us (1%)
    all_to_all x3, blocking collectives, everywhere(): return lax.all_to_all(rows, AXES, split_axis=0, concat_axis=0, tiled=True)  45.8 us
    pallas_call x11, Pallas kernels, call(): pl.pallas_call(kernel, name=getattr(kernel, 'func', kernel).__name__, out...  11.5 us
    ppermute x6, starting transfers between devices, swap(): return (lax.ppermute(a, AXES, pairs_a), lax.ppermute(b, AXES, pairs_b))  9.79 us
  transfers between devices with their start and end apart: 6, of which 2 were waited for; matrix products, arithmetic and copies ran while one was open for 0% of the time, Pallas kernels for 4%

profile of v5, /device:TPU:0, one launch (start us, length us, event | category | flops | bytes accessed | tf_op | source)
XLA Modules:
  0.0 68.5 jit_solution(1432188496311196557)
XLA Ops:
  0.6 0.0 copy-start.2
  0.6 0.0 copy-start.1
  0.7 2.2 %send_kernel.1 = (f32[512,128]{1,0:T(8,128)S(1)}, s32[8,1024]{1,0:T(8,128)S(1)}) custom-call(s32[1]{0:T(128)} %bitcast.odd_ref, f32[1024,128]{1,0:T(8,128)} %pressure_hbm.1, s32[1,1024]{1,0:T(1,128)} %bitcast.17, s32[1,1024]{1,0:T(1,128)} %bitcast.18, f32[24,128]{1,0:T(8,128)} %table_ref.1, f32[3,1024]{1,0:T(4,128)} %support_ref.1, f32[24,24,1024]{2,1,0:T(8,128)} %stiffness_ref.5), custom_call_target="tpu_custom_call" | custom-call | flops 1000000000 | bytes 1000000 | tf_op jit(solution)/shard_map/send_kernel/pallas_call | solution.py:421
  2.8 17.7 %all_to_all.33 = f32[32,16,128]{2,1,0:T(8,128)S(1)} all-to-all(f32[32,16,128]{2,1,0:T(8,128)S(1)} %bitcast.14), channel_id=1, replica_groups=mesh['fluid'=4,'solid'=8] {'fluid','solid'}, dimensions={0} | all-to-all | bytes 524288 | tf_op jit(solution)/shard_map/all_to_all | solution.py:454
  20.5 0.0 copy-done.2
  20.6 0.0 copy-done.1
  20.6 1.5 %load_kernel.1 = (f32[48,128]{1,0:T(8,128)S(1)}, f32[8,128]{1,0:T(8,128)S(1)}, f32[8,128]{1,0:T(8,128)S(1)}, f32[48,128]{1,0:T(8,128)S(1)}, f32[8,128]{1,0:T(8,128)S(1)}, /*index=5*/s32[8,512]{1,0:T(8,128)S(1)}) custom-call(s32[1]{0:T(128)} %bitcast.odd_ref, f32[512,128]{1,0:T(8,128)S(1)} %bitcast.13, s32[8,1024]{1,0:T(8,128)S(1)} %copy-done.1, ...), custom_call_target="tpu_custom_call" | custom-call | flops 1000000000 | bytes 1000000 | tf_op jit(solution)/shard_map/load_kernel/pallas_call | solution.py:421
  22.1 0.1 collective-permute-start
  22.2 0.7 collective-permute-start.1
  22.8 0.5 collective-permute-done.after_ref.swap_a_in
  23.3 0.7 %columns_kernel.1.columns_ref = bf16[8,1024,128]{2,1,0:T(8,128)(2,1)S(1)} custom-call(s32[8,1024]{1,0:T(8,128)S(1)} %copy-done.1, f32[8,128]{1,0:T(8,128)S(1)} %collective-permute-done.after_ref.swap_a_in), custom_call_target="tpu_custom_call" | custom-call | flops 100000000 | bytes 100000 | tf_op jit(solution)/shard_map/columns_kernel/pallas_call | solution.py:421
  24.0 0.0 collective-permute-done.1.swap_b_in
  24.1 0.0 copy-done
  24.1 1.0 %product_kernel.2 = (f32[48,128]{1,0:T(8,128)S(1)}, f32[24,1024]{1,0:T(8,128)S(1)}, f32[24,1024]{1,0:T(8,128)S(1)}, f32[48,128]{1,0:T(8,128)S(1)}, f32[8,128]{1,0:T(8,128)S(1)}, /*index=5*/f32[8,128]{1,0:T(8,128)S(1)}) custom-call(s32[1]{0:T(128)} %bitcast.odd_ref, f32[48,128]{1,0:T(8,128)S(1)} %get-tuple-element.32.partial_ref, ...), custom_call_target="tpu_custom_call" | custom-call | flops 1000000000 | bytes 1000000 | tf_op jit(solution)/shard_map/product_kernel/pallas_call | solution.py:421
  25.0 3.6 %collective-permute-start.2 = (f32[8,128]{1,0:T(8,128)S(1)}, f32[8,128]{1,0:T(8,128)S(1)}, u32[]{:S(2)}, u32[]{:S(2)}) collective-permute-start(f32[8,128]{1,0:T(8,128)S(1)} %get-tuple-element.38), channel_id=1, source_target_pairs={{0,1},{2,3},{4,5},{6,7},{8,9},{10,11},{12,13},{14,15},{16,17},{18,... | collective-permute-start | bytes 12296 | tf_op jit(solution)/shard_map/ppermute | solution.py:451
  28.6 0.6 collective-permute-start.3
  29.3 0.2 collective-permute-done.2.swap_a_in.after_ref
  29.4 0.0 collective-permute-done.3.swap_b_in
  29.4 0.9 %product_kernel.3 = (f32[48,128]{1,0:T(8,128)S(1)}, f32[24,1024]{1,0:T(8,128)S(1)}, f32[24,1024]{1,0:T(8,128)S(1)}, f32[48,128]{1,0:T(8,128)S(1)}, f32[8,128]{1,0:T(8,128)S(1)}, /*index=5*/f32[8,128]{1,0:T(8,128)S(1)}) custom-call(s32[1]{0:T(128)} %bitcast.odd_ref, f32[48,128]{1,0:T(8,128)S(1)} %get-tuple-element.37.partial_ref, ...), custom_call_target="tpu_custom_call" | custom-call | flops 1000000000 | bytes 1000000 | tf_op jit(solution)/shard_map/product_kernel/pallas_call | solution.py:421
  30.4 4.2 %collective-permute-start.4 = (f32[8,128]{1,0:T(8,128)S(1)}, f32[8,128]{1,0:T(8,128)S(1)}, u32[]{:S(2)}, u32[]{:S(2)}) collective-permute-start(f32[8,128]{1,0:T(8,128)S(1)} %get-tuple-element.41), channel_id=1, source_target_pairs={{0,1},{2,3},{4,5},{6,7},{8,9},{10,11},{12,13},{14,15},{16,17},{18,... | collective-permute-start | bytes 12296 | tf_op jit(solution)/shard_map/ppermute | solution.py:451
  34.6 0.6 collective-permute-start.5
  35.2 0.8 %pick_kernel.2.pick0_ref = f32[512,128]{1,0:T(8,128)S(1)} custom-call(f32[24,1024]{1,0:T(8,128)S(1)} %get-tuple-element.45.values0_ref.values_ref, s32[8,512]{1,0:T(8,128)S(1)} %get-tuple-element.53.code_ref, f32[8,128]{1,0:T(8,128)S(1)} %collective-permute-done.2.swap_a_in.after_ref), custom_call_target="tpu_custom_call" | custom-call | flops 100000000 | bytes 100000 | tf_op jit(solution)/shard_map/pick_kernel/pallas_call | solution.py:421
  36.0 0.0 collective-permute-done.4.after_ref.swap_a_in
  36.0 0.8 %pick_kernel.3.pick1_ref = f32[512,128]{1,0:T(8,128)S(1)} custom-call(f32[24,1024]{1,0:T(8,128)S(1)} %get-tuple-element.46.values1_ref.values_ref, s32[8,512]{1,0:T(8,128)S(1)} %get-tuple-element.53.code_ref, f32[8,128]{1,0:T(8,128)S(1)} %collective-permute-done.4.after_ref.swap_a_in), custom_call_target="tpu_custom_call" | custom-call | flops 100000000 | bytes 100000 | tf_op jit(solution)/shard_map/pick_kernel/pallas_call | solution.py:421
  36.9 0.4 lower_kernel.1
  37.2 0.0 collective-permute-done.5.swap_b_in
  37.2 0.7 %moment_kernel.1 = (f32[48,128]{1,0:T(8,128)S(1)}, f32[24,1024]{1,0:T(8,128)S(1)}, f32[32,128]{1,0:T(8,128)S(1)}) custom-call(s32[1]{0:T(128)} %bitcast.odd_ref, f32[48,128]{1,0:T(8,128)S(1)} %get-tuple-element.40.partial_ref, f32[8,128]{1,0:T(8,128)S(1)} %collective-permute-done.4.after_ref.swap_a_in, f32[8,128]{1,0:T(8,128)S(1)} %collective-permute-done.5.swap_b_in, ...), custom_call_target="tpu_custom_call" | custom-call | flops 1000000000 | bytes 1000000 | tf_op jit(solution)/shard_map/moment_kernel/pallas_call | solution.py:421
  38.0 15.8 %all_to_all.34 = f32[32,1,128]{2,1,0:T(1,128)S(1)} all-to-all(f32[32,1,128]{2,1,0:T(1,128)S(1)} %bitcast.15), channel_id=1, replica_groups=mesh['fluid'=4,'solid'=8] {'fluid','solid'}, dimensions={0} | all-to-all | bytes 32768 | tf_op jit(solution)/shard_map/all_to_all | solution.py:454
  53.8 0.9 %blend_kernel.1 = (f32[24,128]{1,0:T(8,128)S(1)}, f32[512,128]{1,0:T(8,128)S(1)}) custom-call(f32[32,128]{1,0:T(8,128)S(1)} %bitcast.16, f32[8,128]{1,0:T(8,128)S(1)} %get-tuple-element.36.scale_ref, s32[8,512]{1,0:T(8,128)S(1)} %get-tuple-element.53.code_ref, f32[512,128]{1,0:T(8,128)S(1)} %pick_kernel.2.pick0_ref, f32[512,128]{1,0:T(8,128)S(1)} %pick_kernel.3.pick1_ref, ...), custom_call_target="tpu_custom_call" | custom-call | flops 1000000000 | bytes 1000000 | tf_op jit(solution)/shard_map/blend_kernel/pallas_call | solution.py:421
  54.7 12.3 %all_to_all.35 = f32[32,16,128]{2,1,0:T(8,128)S(1)} all-to-all(f32[32,16,128]{2,1,0:T(8,128)S(1)} %bitcast.12), channel_id=1, replica_groups=mesh['fluid'=4,'solid'=8] {'fluid','solid'}, dimensions={0} | all-to-all | bytes 524288 | tf_op jit(solution)/shard_map/all_to_all | solution.py:454
  67.0 0.0 copy-done.3
  67.0 1.5 %motion_kernel.1 = (f32[3,1024]{1,0:T(4,128)}, f32[1024,128]{1,0:T(8,128)}) custom-call(f32[512,128]{1,0:T(8,128)S(1)} %bitcast.11, s32[8,1024]{1,0:T(8,128)S(1)} %get-tuple-element.57.place_ref, f32[24,128]{1,0:T(8,128)S(1)} %copy-done.3, f32[24,128]{1,0:T(8,128)S(1)} %get-tuple-element.58.weights_ref, f32[48,128]{1,0:T(8,128)S(1)} %get-tuple-element.43.first_ref, ...), custom_call_target="tpu_custom_call" | custom-call | flops 1000000000 | bytes 1000000 | tf_op jit(solution)/shard_map/motion_kernel/pallas_call | solution.py:421
  (2 shorter events, 0.0 us)
Async XLA Ops:
  0.6 19.9 %copy-start.2 = (f32[3,1024]{1,0:T(4,128)S(1)}, f32[3,1024]{1,0:T(4,128)}, u32[]{:S(2)}) copy-start(f32[3,1024]{1,0:T(4,128)} %support_ref.1) | copy-start | bytes 36868
  0.6 19.9 %copy-start.1 = (s32[8,1024]{1,0:T(8,128)S(1)}, s32[8,1024]{1,0:T(8,128)}, u32[]{:S(2)}) copy-start(s32[8,1024]{1,0:T(8,128)} %connectivity_ref.9) | copy-start | bytes 98308
  20.6 3.5 %copy-start = (f32[24,24,1024]{2,1,0:T(8,128)S(1)}, f32[24,24,1024]{2,1,0:T(8,128)}, u32[]{:S(2)}) copy-start(f32[24,24,1024]{2,1,0:T(8,128)} %stiffness_ref.5) | copy-start | bytes 7077892
  22.1 1.2 %collective-permute-start = (f32[8,128]{1,0:T(8,128)S(1)}, f32[8,128]{1,0:T(8,128)S(1)}, u32[]{:S(2)}, u32[]{:S(2)}) collective-permute-start(f32[8,128]{1,0:T(8,128)S(1)} %get-tuple-element.33), channel_id=1, source_target_pairs={{0,1},{2,3},{4,5},{6,7},{8,9},{10,11},{12,13},{14,15},{16,17},{18,... | collective-permute-start | bytes 12296 | tf_op jit(solution)/shard_map/ppermute | solution.py:451
  22.2 1.9 %collective-permute-start.1 = (f32[8,128]{1,0:T(8,128)S(1)}, f32[8,128]{1,0:T(8,128)S(1)}, u32[]{:S(2)}, u32[]{:S(2)}) collective-permute-start(f32[8,128]{1,0:T(8,128)S(1)} %get-tuple-element.34), channel_id=1, source_target_pairs={{1,2},{3,4},{5,6},{7,8},{9,10},{11,12},{13,14},{15,16},{17,18},{19... | collective-permute-start | bytes 12296 | tf_op jit(solution)/shard_map/ppermute | solution.py:451
  25.0 4.4 %collective-permute-start.2 = (f32[8,128]{1,0:T(8,128)S(1)}, f32[8,128]{1,0:T(8,128)S(1)}, u32[]{:S(2)}, u32[]{:S(2)}) collective-permute-start(f32[8,128]{1,0:T(8,128)S(1)} %get-tuple-element.38), channel_id=1, source_target_pairs={{0,1},{2,3},{4,5},{6,7},{8,9},{10,11},{12,13},{14,15},{16,17},{18,... | collective-permute-start | bytes 12296 | tf_op jit(solution)/shard_map/ppermute | solution.py:451
  28.6 0.8 %collective-permute-start.3 = (f32[8,128]{1,0:T(8,128)S(1)}, f32[8,128]{1,0:T(8,128)S(1)}, u32[]{:S(2)}, u32[]{:S(2)}) collective-permute-start(f32[8,128]{1,0:T(8,128)S(1)} %get-tuple-element.39), channel_id=1, source_target_pairs={{1,2},{3,4},{5,6},{7,8},{9,10},{11,12},{13,14},{15,16},{17,18},{19... | collective-permute-start | bytes 12296 | tf_op jit(solution)/shard_map/ppermute | solution.py:451
  30.4 5.6 %collective-permute-start.4 = (f32[8,128]{1,0:T(8,128)S(1)}, f32[8,128]{1,0:T(8,128)S(1)}, u32[]{:S(2)}, u32[]{:S(2)}) collective-permute-start(f32[8,128]{1,0:T(8,128)S(1)} %get-tuple-element.41), channel_id=1, source_target_pairs={{0,1},{2,3},{4,5},{6,7},{8,9},{10,11},{12,13},{14,15},{16,17},{18,... | collective-permute-start | bytes 12296 | tf_op jit(solution)/shard_map/ppermute | solution.py:451
  34.6 2.7 %collective-permute-start.5 = (f32[8,128]{1,0:T(8,128)S(1)}, f32[8,128]{1,0:T(8,128)S(1)}, u32[]{:S(2)}, u32[]{:S(2)}) collective-permute-start(f32[8,128]{1,0:T(8,128)S(1)} %get-tuple-element.42), channel_id=1, source_target_pairs={{1,2},{3,4},{5,6},{7,8},{9,10},{11,12},{13,14},{15,16},{17,18},{19... | collective-permute-start | bytes 12296 | tf_op jit(solution)/shard_map/ppermute | solution.py:451
  38.0 29.0 %copy-start.3 = (f32[24,128]{1,0:T(8,128)S(1)}, f32[24,128]{1,0:T(8,128)}, u32[]{:S(2)}) copy-start(f32[24,128]{1,0:T(8,128)} %table_ref.1) | copy-start | bytes 36868

commit v6 on v5

--- a/solution.py
+++ b/solution.py
@@ -142,7 +142,8 @@
     del odd_ref
     moves = [(owner_hbm, owner_ref), (element_hbm, element_ref), (table_hbm, table_ref), (pressure_hbm, pressure_ref),
              (support_hbm, support_ref)]
-    moves += [(stiffness_hbm.at[i, pl.ds(i, 1)], diagonal_ref.at[pl.ds(i, 1)]) for i in range(DOF)]
+    moves += [
+        (stiffness_hbm.at[c * CORNERS, pl.ds(c * CORNERS, 1)], diagonal_ref.at[pl.ds(c, 1)]) for c in range(3)]
     copies = [pltpu.make_async_copy(source, target, sems.at[i]) for i, (source, target) in enumerate(moves)]
     for copy in copies:
         copy.start()
@@ -182,7 +183,7 @@
     spread_high, spread_low = split(jnp.concatenate(spread, axis=0))
     sent = dot_nt(chosen, jnp.concatenate([spread_high, spread_low], axis=0))
 
-    trace = jnp.sum(diagonal_ref[...]) + jnp.sum(support_ref[...])
+    trace = CORNERS * jnp.sum(diagonal_ref[...]) + jnp.sum(support_ref[...])
     out_ref[...] = jnp.where(iota((devices * per, LANES), 1) == 125, trace, sent[:, :LANES] + sent[:, LANES:])
 
 
@@ -469,8 +470,8 @@
             pltpu.VMEM((1, faces), jnp.int32),
             pltpu.VMEM(shape_table.shape, F32),
             pltpu.VMEM(support.shape, F32),
-            pltpu.VMEM((DOF, elements), F32),
-            pltpu.SemaphoreType.DMA((5 + DOF,)),
+            pltpu.VMEM((3, elements), F32),
+            pltpu.SemaphoreType.DMA((8,)),
         ),
     )
     arrived = everywhere(sent)

time: 68.8 us -> 68.6 us (level)
  no operation moved by 1% of the time
where the time goes in v6:
time: 68.6 us; the launch traced here: 68.3 us
  blocking collectives  45.8 us (67%)
  Pallas kernels  11.2 us (16%)
  starting transfers between devices  9.79 us (14%)
  between operations  0.75 us (1%)
    all_to_all x3, blocking collectives, everywhere(): return lax.all_to_all(rows, AXES, split_axis=0, concat_axis=0, tiled=True)  45.8 us
    pallas_call x11, Pallas kernels, call(): pl.pallas_call(kernel, name=getattr(kernel, 'func', kernel).__name__, out...  11.2 us
    ppermute x6, starting transfers between devices, swap(): return (lax.ppermute(a, AXES, pairs_a), lax.ppermute(b, AXES, pairs_b))  9.79 us
  transfers between devices with their start and end apart: 6, of which 2 were waited for; matrix products, arithmetic and copies ran while one was open for 0% of the time, Pallas kernels for 4%

profile of v6, /device:TPU:0, one launch (start us, length us, event | category | flops | bytes accessed | tf_op | source)
XLA Modules:
  0.0 68.3 jit_solution(4317879013487447797)
XLA Ops:
  0.6 0.0 copy-start.2
  0.6 0.0 copy-start.1
  0.7 2.0 %send_kernel.1 = (f32[512,128]{1,0:T(8,128)S(1)}, s32[8,1024]{1,0:T(8,128)S(1)}) custom-call(s32[1]{0:T(128)} %bitcast.odd_ref, f32[1024,128]{1,0:T(8,128)} %pressure_hbm.1, s32[1,1024]{1,0:T(1,128)} %bitcast.17, s32[1,1024]{1,0:T(1,128)} %bitcast.18, f32[24,128]{1,0:T(8,128)} %table_ref.1, f32[3,1024]{1,0:T(4,128)} %support_ref.1, f32[24,24,1024]{2,1,0:T(8,128)} %stiffness_ref.5), custom_call_target="tpu_custom_call" | custom-call | flops 1000000000 | bytes 1000000 | tf_op jit(solution)/shard_map/send_kernel/pallas_call | solution.py:422
  2.6 17.7 %all_to_all.33 = f32[32,16,128]{2,1,0:T(8,128)S(1)} all-to-all(f32[32,16,128]{2,1,0:T(8,128)S(1)} %bitcast.14), channel_id=1, replica_groups=mesh['fluid'=4,'solid'=8] {'fluid','solid'}, dimensions={0} | all-to-all | bytes 524288 | tf_op jit(solution)/shard_map/all_to_all | solution.py:455
  20.3 0.0 copy-done.2
  20.3 0.0 copy-done.1
  20.3 1.5 %load_kernel.1 = (f32[48,128]{1,0:T(8,128)S(1)}, f32[8,128]{1,0:T(8,128)S(1)}, f32[8,128]{1,0:T(8,128)S(1)}, f32[48,128]{1,0:T(8,128)S(1)}, f32[8,128]{1,0:T(8,128)S(1)}, /*index=5*/s32[8,512]{1,0:T(8,128)S(1)}) custom-call(s32[1]{0:T(128)} %bitcast.odd_ref, f32[512,128]{1,0:T(8,128)S(1)} %bitcast.13, s32[8,1024]{1,0:T(8,128)S(1)} %copy-done.1, ...), custom_call_target="tpu_custom_call" | custom-call | flops 1000000000 | bytes 1000000 | tf_op jit(solution)/shard_map/load_kernel/pallas_call | solution.py:422
  21.9 0.1 collective-permute-start
  22.0 0.7 collective-permute-start.1
  22.6 0.5 collective-permute-done.after_ref.swap_a_in
  23.1 0.7 %columns_kernel.1.columns_ref = bf16[8,1024,128]{2,1,0:T(8,128)(2,1)S(1)} custom-call(s32[8,1024]{1,0:T(8,128)S(1)} %copy-done.1, f32[8,128]{1,0:T(8,128)S(1)} %collective-permute-done.after_ref.swap_a_in), custom_call_target="tpu_custom_call" | custom-call | flops 100000000 | bytes 100000 | tf_op jit(solution)/shard_map/columns_kernel/pallas_call | solution.py:422
  23.8 0.0 collective-permute-done.1.swap_b_in
  23.8 0.0 copy-done
  23.8 1.0 %product_kernel.2 = (f32[48,128]{1,0:T(8,128)S(1)}, f32[24,1024]{1,0:T(8,128)S(1)}, f32[24,1024]{1,0:T(8,128)S(1)}, f32[48,128]{1,0:T(8,128)S(1)}, f32[8,128]{1,0:T(8,128)S(1)}, /*index=5*/f32[8,128]{1,0:T(8,128)S(1)}) custom-call(s32[1]{0:T(128)} %bitcast.odd_ref, f32[48,128]{1,0:T(8,128)S(1)} %get-tuple-element.32.partial_ref, ...), custom_call_target="tpu_custom_call" | custom-call | flops 1000000000 | bytes 1000000 | tf_op jit(solution)/shard_map/product_kernel/pallas_call | solution.py:422
  24.8 3.6 %collective-permute-start.2 = (f32[8,128]{1,0:T(8,128)S(1)}, f32[8,128]{1,0:T(8,128)S(1)}, u32[]{:S(2)}, u32[]{:S(2)}) collective-permute-start(f32[8,128]{1,0:T(8,128)S(1)} %get-tuple-element.38), channel_id=1, source_target_pairs={{0,1},{2,3},{4,5},{6,7},{8,9},{10,11},{12,13},{14,15},{16,17},{18,... | collective-permute-start | bytes 12296 | tf_op jit(solution)/shard_map/ppermute | solution.py:452
  28.4 0.6 collective-permute-start.3
  29.0 0.2 collective-permute-done.2.swap_a_in.after_ref
  29.2 0.0 collective-permute-done.3.swap_b_in
  29.2 0.9 %product_kernel.3 = (f32[48,128]{1,0:T(8,128)S(1)}, f32[24,1024]{1,0:T(8,128)S(1)}, f32[24,1024]{1,0:T(8,128)S(1)}, f32[48,128]{1,0:T(8,128)S(1)}, f32[8,128]{1,0:T(8,128)S(1)}, /*index=5*/f32[8,128]{1,0:T(8,128)S(1)}) custom-call(s32[1]{0:T(128)} %bitcast.odd_ref, f32[48,128]{1,0:T(8,128)S(1)} %get-tuple-element.37.partial_ref, ...), custom_call_target="tpu_custom_call" | custom-call | flops 1000000000 | bytes 1000000 | tf_op jit(solution)/shard_map/product_kernel/pallas_call | solution.py:422
  30.2 4.2 %collective-permute-start.4 = (f32[8,128]{1,0:T(8,128)S(1)}, f32[8,128]{1,0:T(8,128)S(1)}, u32[]{:S(2)}, u32[]{:S(2)}) collective-permute-start(f32[8,128]{1,0:T(8,128)S(1)} %get-tuple-element.41), channel_id=1, source_target_pairs={{0,1},{2,3},{4,5},{6,7},{8,9},{10,11},{12,13},{14,15},{16,17},{18,... | collective-permute-start | bytes 12296 | tf_op jit(solution)/shard_map/ppermute | solution.py:452
  34.3 0.6 collective-permute-start.5
  35.0 0.8 %pick_kernel.2.pick0_ref = f32[512,128]{1,0:T(8,128)S(1)} custom-call(f32[24,1024]{1,0:T(8,128)S(1)} %get-tuple-element.45.values0_ref.values_ref, s32[8,512]{1,0:T(8,128)S(1)} %get-tuple-element.53.code_ref, f32[8,128]{1,0:T(8,128)S(1)} %collective-permute-done.2.swap_a_in.after_ref), custom_call_target="tpu_custom_call" | custom-call | flops 100000000 | bytes 100000 | tf_op jit(solution)/shard_map/pick_kernel/pallas_call | solution.py:422
  35.8 0.0 collective-permute-done.4.after_ref.swap_a_in
  35.8 0.8 %pick_kernel.3.pick1_ref = f32[512,128]{1,0:T(8,128)S(1)} custom-call(f32[24,1024]{1,0:T(8,128)S(1)} %get-tuple-element.46.values1_ref.values_ref, s32[8,512]{1,0:T(8,128)S(1)} %get-tuple-element.53.code_ref, f32[8,128]{1,0:T(8,128)S(1)} %collective-permute-done.4.after_ref.swap_a_in), custom_call_target="tpu_custom_call" | custom-call | flops 100000000 | bytes 100000 | tf_op jit(solution)/shard_map/pick_kernel/pallas_call | solution.py:422
  36.6 0.4 lower_kernel.1
  37.0 0.0 collective-permute-done.5.swap_b_in
  37.0 0.7 %moment_kernel.1 = (f32[48,128]{1,0:T(8,128)S(1)}, f32[24,1024]{1,0:T(8,128)S(1)}, f32[32,128]{1,0:T(8,128)S(1)}) custom-call(s32[1]{0:T(128)} %bitcast.odd_ref, f32[48,128]{1,0:T(8,128)S(1)} %get-tuple-element.40.partial_ref, f32[8,128]{1,0:T(8,128)S(1)} %collective-permute-done.4.after_ref.swap_a_in, f32[8,128]{1,0:T(8,128)S(1)} %collective-permute-done.5.swap_b_in, ...), custom_call_target="tpu_custom_call" | custom-call | flops 1000000000 | bytes 1000000 | tf_op jit(solution)/shard_map/moment_kernel/pallas_call | solution.py:422
  37.8 15.8 %all_to_all.34 = f32[32,1,128]{2,1,0:T(1,128)S(1)} all-to-all(f32[32,1,128]{2,1,0:T(1,128)S(1)} %bitcast.15), channel_id=1, replica_groups=mesh['fluid'=4,'solid'=8] {'fluid','solid'}, dimensions={0} | all-to-all | bytes 32768 | tf_op jit(solution)/shard_map/all_to_all | solution.py:455
  53.6 0.9 %blend_kernel.1 = (f32[24,128]{1,0:T(8,128)S(1)}, f32[512,128]{1,0:T(8,128)S(1)}) custom-call(f32[32,128]{1,0:T(8,128)S(1)} %bitcast.16, f32[8,128]{1,0:T(8,128)S(1)} %get-tuple-element.36.scale_ref, s32[8,512]{1,0:T(8,128)S(1)} %get-tuple-element.53.code_ref, f32[512,128]{1,0:T(8,128)S(1)} %pick_kernel.2.pick0_ref, f32[512,128]{1,0:T(8,128)S(1)} %pick_kernel.3.pick1_ref, ...), custom_call_target="tpu_custom_call" | custom-call | flops 1000000000 | bytes 1000000 | tf_op jit(solution)/shard_map/blend_kernel/pallas_call | solution.py:422
  54.5 12.3 %all_to_all.35 = f32[32,16,128]{2,1,0:T(8,128)S(1)} all-to-all(f32[32,16,128]{2,1,0:T(8,128)S(1)} %bitcast.12), channel_id=1, replica_groups=mesh['fluid'=4,'solid'=8] {'fluid','solid'}, dimensions={0} | all-to-all | bytes 524288 | tf_op jit(solution)/shard_map/all_to_all | solution.py:455
  66.8 0.0 copy-done.3
  66.8 1.5 %motion_kernel.1 = (f32[3,1024]{1,0:T(4,128)}, f32[1024,128]{1,0:T(8,128)}) custom-call(f32[512,128]{1,0:T(8,128)S(1)} %bitcast.11, s32[8,1024]{1,0:T(8,128)S(1)} %get-tuple-element.57.place_ref, f32[24,128]{1,0:T(8,128)S(1)} %copy-done.3, f32[24,128]{1,0:T(8,128)S(1)} %get-tuple-element.58.weights_ref, f32[48,128]{1,0:T(8,128)S(1)} %get-tuple-element.43.first_ref, ...), custom_call_target="tpu_custom_call" | custom-call | flops 1000000000 | bytes 1000000 | tf_op jit(solution)/shard_map/motion_kernel/pallas_call | solution.py:422
  (2 shorter events, 0.0 us)
Async XLA Ops:
  0.6 19.7 %copy-start.2 = (f32[3,1024]{1,0:T(4,128)S(1)}, f32[3,1024]{1,0:T(4,128)}, u32[]{:S(2)}) copy-start(f32[3,1024]{1,0:T(4,128)} %support_ref.1) | copy-start | bytes 36868
  0.6 19.7 %copy-start.1 = (s32[8,1024]{1,0:T(8,128)S(1)}, s32[8,1024]{1,0:T(8,128)}, u32[]{:S(2)}) copy-start(s32[8,1024]{1,0:T(8,128)} %connectivity_ref.9) | copy-start | bytes 98308
  20.3 3.5 %copy-start = (f32[24,24,1024]{2,1,0:T(8,128)S(1)}, f32[24,24,1024]{2,1,0:T(8,128)}, u32[]{:S(2)}) copy-start(f32[24,24,1024]{2,1,0:T(8,128)} %stiffness_ref.5) | copy-start | bytes 7077892
  21.9 1.2 %collective-permute-start = (f32[8,128]{1,0:T(8,128)S(1)}, f32[8,128]{1,0:T(8,128)S(1)}, u32[]{:S(2)}, u32[]{:S(2)}) collective-permute-start(f32[8,128]{1,0:T(8,128)S(1)} %get-tuple-element.33), channel_id=1, source_target_pairs={{0,1},{2,3},{4,5},{6,7},{8,9},{10,11},{12,13},{14,15},{16,17},{18,... | collective-permute-start | bytes 12296 | tf_op jit(solution)/shard_map/ppermute | solution.py:452
  22.0 1.9 %collective-permute-start.1 = (f32[8,128]{1,0:T(8,128)S(1)}, f32[8,128]{1,0:T(8,128)S(1)}, u32[]{:S(2)}, u32[]{:S(2)}) collective-permute-start(f32[8,128]{1,0:T(8,128)S(1)} %get-tuple-element.34), channel_id=1, source_target_pairs={{1,2},{3,4},{5,6},{7,8},{9,10},{11,12},{13,14},{15,16},{17,18},{19... | collective-permute-start | bytes 12296 | tf_op jit(solution)/shard_map/ppermute | solution.py:452
  24.8 4.4 %collective-permute-start.2 = (f32[8,128]{1,0:T(8,128)S(1)}, f32[8,128]{1,0:T(8,128)S(1)}, u32[]{:S(2)}, u32[]{:S(2)}) collective-permute-start(f32[8,128]{1,0:T(8,128)S(1)} %get-tuple-element.38), channel_id=1, source_target_pairs={{0,1},{2,3},{4,5},{6,7},{8,9},{10,11},{12,13},{14,15},{16,17},{18,... | collective-permute-start | bytes 12296 | tf_op jit(solution)/shard_map/ppermute | solution.py:452
  28.4 0.8 %collective-permute-start.3 = (f32[8,128]{1,0:T(8,128)S(1)}, f32[8,128]{1,0:T(8,128)S(1)}, u32[]{:S(2)}, u32[]{:S(2)}) collective-permute-start(f32[8,128]{1,0:T(8,128)S(1)} %get-tuple-element.39), channel_id=1, source_target_pairs={{1,2},{3,4},{5,6},{7,8},{9,10},{11,12},{13,14},{15,16},{17,18},{19... | collective-permute-start | bytes 12296 | tf_op jit(solution)/shard_map/ppermute | solution.py:452
  30.2 5.6 %collective-permute-start.4 = (f32[8,128]{1,0:T(8,128)S(1)}, f32[8,128]{1,0:T(8,128)S(1)}, u32[]{:S(2)}, u32[]{:S(2)}) collective-permute-start(f32[8,128]{1,0:T(8,128)S(1)} %get-tuple-element.41), channel_id=1, source_target_pairs={{0,1},{2,3},{4,5},{6,7},{8,9},{10,11},{12,13},{14,15},{16,17},{18,... | collective-permute-start | bytes 12296 | tf_op jit(solution)/shard_map/ppermute | solution.py:452
  34.3 2.7 %collective-permute-start.5 = (f32[8,128]{1,0:T(8,128)S(1)}, f32[8,128]{1,0:T(8,128)S(1)}, u32[]{:S(2)}, u32[]{:S(2)}) collective-permute-start(f32[8,128]{1,0:T(8,128)S(1)} %get-tuple-element.42), channel_id=1, source_target_pairs={{1,2},{3,4},{5,6},{7,8},{9,10},{11,12},{13,14},{15,16},{17,18},{19... | collective-permute-start | bytes 12296 | tf_op jit(solution)/shard_map/ppermute | solution.py:452
  37.8 29.0 %copy-start.3 = (f32[24,128]{1,0:T(8,128)S(1)}, f32[24,128]{1,0:T(8,128)}, u32[]{:S(2)}) copy-start(f32[24,128]{1,0:T(8,128)} %table_ref.1) | copy-start | bytes 36868

commit v7 on v5

--- a/solution.py
+++ b/solution.py
@@ -142,12 +142,15 @@
     del odd_ref
     moves = [(owner_hbm, owner_ref), (element_hbm, element_ref), (table_hbm, table_ref), (pressure_hbm, pressure_ref),
              (support_hbm, support_ref)]
-    moves += [(stiffness_hbm.at[i, pl.ds(i, 1)], diagonal_ref.at[pl.ds(i, 1)]) for i in range(DOF)]
     copies = [pltpu.make_async_copy(source, target, sems.at[i]) for i, (source, target) in enumerate(moves)]
     for copy in copies:
         copy.start()
+    for i in range(DOF):
+        pltpu.make_async_copy(
+            stiffness_hbm.at[i, pl.ds(i, 1)], diagonal_ref.at[pl.ds(i, 1)], sems.at[len(moves)]).start()
     for copy in copies:
         copy.wait()
+    pltpu.make_async_copy(stiffness_hbm.at[0], diagonal_ref, sems.at[len(moves)]).wait()
     faces = pressure_ref.shape[0]
     target = owner_ref[...]
     named = iota((devices, faces), 0) == target
@@ -470,7 +473,7 @@
             pltpu.VMEM(shape_table.shape, F32),
             pltpu.VMEM(support.shape, F32),
             pltpu.VMEM((DOF, elements), F32),
-            pltpu.SemaphoreType.DMA((5 + DOF,)),
+            pltpu.SemaphoreType.DMA((6,)),
         ),
     )
     arrived = everywhere(sent)

time: 68.8 us -> 68.5 us (level)
  no operation moved by 1% of the time
where the time goes in v7:
time: 68.5 us; the launch traced here: 68.3 us
  blocking collectives  45.8 us (67%)
  Pallas kernels  11.2 us (16%)
  starting transfers between devices  9.79 us (14%)
  between operations  0.75 us (1%)
    all_to_all x3, blocking collectives, everywhere(): return lax.all_to_all(rows, AXES, split_axis=0, concat_axis=0, tiled=True)  45.8 us
    pallas_call x11, Pallas kernels, call(): pl.pallas_call(kernel, name=getattr(kernel, 'func', kernel).__name__, out...  11.2 us
    ppermute x6, starting transfers between devices, swap(): return (lax.ppermute(a, AXES, pairs_a), lax.ppermute(b, AXES, pairs_b))  9.79 us
  transfers between devices with their start and end apart: 6, of which 2 were waited for; matrix products, arithmetic and copies ran while one was open for 0% of the time, Pallas kernels for 4%

profile of v7, /device:TPU:0, one launch (start us, length us, event | category | flops | bytes accessed | tf_op | source)
XLA Modules:
  0.0 68.3 jit_solution(9954600619207667345)
XLA Ops:
  0.6 0.0 copy-start.2
  0.6 0.0 copy-start.1
  0.7 1.9 %send_kernel.1 = (f32[512,128]{1,0:T(8,128)S(1)}, s32[8,1024]{1,0:T(8,128)S(1)}) custom-call(s32[1]{0:T(128)} %bitcast.odd_ref, f32[1024,128]{1,0:T(8,128)} %pressure_hbm.1, s32[1,1024]{1,0:T(1,128)} %bitcast.17, s32[1,1024]{1,0:T(1,128)} %bitcast.18, f32[24,128]{1,0:T(8,128)} %table_ref.1, f32[3,1024]{1,0:T(4,128)} %support_ref.1, f32[24,24,1024]{2,1,0:T(8,128)} %stiffness_ref.5), custom_call_target="tpu_custom_call" | custom-call | flops 1000000000 | bytes 1000000 | tf_op jit(solution)/shard_map/send_kernel/pallas_call | solution.py:424
  2.6 17.7 %all_to_all.33 = f32[32,16,128]{2,1,0:T(8,128)S(1)} all-to-all(f32[32,16,128]{2,1,0:T(8,128)S(1)} %bitcast.14), channel_id=1, replica_groups=mesh['fluid'=4,'solid'=8] {'fluid','solid'}, dimensions={0} | all-to-all | bytes 524288 | tf_op jit(solution)/shard_map/all_to_all | solution.py:457
  20.3 0.0 copy-done.2
  20.3 0.0 copy-done.1
  20.3 1.5 %load_kernel.1 = (f32[48,128]{1,0:T(8,128)S(1)}, f32[8,128]{1,0:T(8,128)S(1)}, f32[8,128]{1,0:T(8,128)S(1)}, f32[48,128]{1,0:T(8,128)S(1)}, f32[8,128]{1,0:T(8,128)S(1)}, /*index=5*/s32[8,512]{1,0:T(8,128)S(1)}) custom-call(s32[1]{0:T(128)} %bitcast.odd_ref, f32[512,128]{1,0:T(8,128)S(1)} %bitcast.13, s32[8,1024]{1,0:T(8,128)S(1)} %copy-done.1, ...), custom_call_target="tpu_custom_call" | custom-call | flops 1000000000 | bytes 1000000 | tf_op jit(solution)/shard_map/load_kernel/pallas_call | solution.py:424
  21.8 0.1 collective-permute-start
  21.9 0.7 collective-permute-start.1
  22.6 0.5 collective-permute-done.after_ref.swap_a_in
  23.1 0.7 %columns_kernel.1.columns_ref = bf16[8,1024,128]{2,1,0:T(8,128)(2,1)S(1)} custom-call(s32[8,1024]{1,0:T(8,128)S(1)} %copy-done.1, f32[8,128]{1,0:T(8,128)S(1)} %collective-permute-done.after_ref.swap_a_in), custom_call_target="tpu_custom_call" | custom-call | flops 100000000 | bytes 100000 | tf_op jit(solution)/shard_map/columns_kernel/pallas_call | solution.py:424
  23.8 0.0 collective-permute-done.1.swap_b_in
  23.8 0.0 copy-done
  23.8 1.0 %product_kernel.2 = (f32[48,128]{1,0:T(8,128)S(1)}, f32[24,1024]{1,0:T(8,128)S(1)}, f32[24,1024]{1,0:T(8,128)S(1)}, f32[48,128]{1,0:T(8,128)S(1)}, f32[8,128]{1,0:T(8,128)S(1)}, /*index=5*/f32[8,128]{1,0:T(8,128)S(1)}) custom-call(s32[1]{0:T(128)} %bitcast.odd_ref, f32[48,128]{1,0:T(8,128)S(1)} %get-tuple-element.32.partial_ref, ...), custom_call_target="tpu_custom_call" | custom-call | flops 1000000000 | bytes 1000000 | tf_op jit(solution)/shard_map/product_kernel/pallas_call | solution.py:424
  24.8 3.6 %collective-permute-start.2 = (f32[8,128]{1,0:T(8,128)S(1)}, f32[8,128]{1,0:T(8,128)S(1)}, u32[]{:S(2)}, u32[]{:S(2)}) collective-permute-start(f32[8,128]{1,0:T(8,128)S(1)} %get-tuple-element.38), channel_id=1, source_target_pairs={{0,1},{2,3},{4,5},{6,7},{8,9},{10,11},{12,13},{14,15},{16,17},{18,... | collective-permute-start | bytes 12296 | tf_op jit(solution)/shard_map/ppermute | solution.py:454
  28.4 0.6 collective-permute-start.3
  29.0 0.2 collective-permute-done.2.swap_a_in.after_ref
  29.2 0.0 collective-permute-done.3.swap_b_in
  29.2 0.9 %product_kernel.3 = (f32[48,128]{1,0:T(8,128)S(1)}, f32[24,1024]{1,0:T(8,128)S(1)}, f32[24,1024]{1,0:T(8,128)S(1)}, f32[48,128]{1,0:T(8,128)S(1)}, f32[8,128]{1,0:T(8,128)S(1)}, /*index=5*/f32[8,128]{1,0:T(8,128)S(1)}) custom-call(s32[1]{0:T(128)} %bitcast.odd_ref, f32[48,128]{1,0:T(8,128)S(1)} %get-tuple-element.37.partial_ref, ...), custom_call_target="tpu_custom_call" | custom-call | flops 1000000000 | bytes 1000000 | tf_op jit(solution)/shard_map/product_kernel/pallas_call | solution.py:424
  30.1 4.2 %collective-permute-start.4 = (f32[8,128]{1,0:T(8,128)S(1)}, f32[8,128]{1,0:T(8,128)S(1)}, u32[]{:S(2)}, u32[]{:S(2)}) collective-permute-start(f32[8,128]{1,0:T(8,128)S(1)} %get-tuple-element.41), channel_id=1, source_target_pairs={{0,1},{2,3},{4,5},{6,7},{8,9},{10,11},{12,13},{14,15},{16,17},{18,... | collective-permute-start | bytes 12296 | tf_op jit(solution)/shard_map/ppermute | solution.py:454
  34.3 0.6 collective-permute-start.5
  35.0 0.8 %pick_kernel.2.pick0_ref = f32[512,128]{1,0:T(8,128)S(1)} custom-call(f32[24,1024]{1,0:T(8,128)S(1)} %get-tuple-element.45.values0_ref.values_ref, s32[8,512]{1,0:T(8,128)S(1)} %get-tuple-element.53.code_ref, f32[8,128]{1,0:T(8,128)S(1)} %collective-permute-done.2.swap_a_in.after_ref), custom_call_target="tpu_custom_call" | custom-call | flops 100000000 | bytes 100000 | tf_op jit(solution)/shard_map/pick_kernel/pallas_call | solution.py:424
  35.8 0.0 collective-permute-done.4.after_ref.swap_a_in
  35.8 0.8 %pick_kernel.3.pick1_ref = f32[512,128]{1,0:T(8,128)S(1)} custom-call(f32[24,1024]{1,0:T(8,128)S(1)} %get-tuple-element.46.values1_ref.values_ref, s32[8,512]{1,0:T(8,128)S(1)} %get-tuple-element.53.code_ref, f32[8,128]{1,0:T(8,128)S(1)} %collective-permute-done.4.after_ref.swap_a_in), custom_call_target="tpu_custom_call" | custom-call | flops 100000000 | bytes 100000 | tf_op jit(solution)/shard_map/pick_kernel/pallas_call | solution.py:424
  36.6 0.4 lower_kernel.1
  37.0 0.0 collective-permute-done.5.swap_b_in
  37.0 0.7 %moment_kernel.1 = (f32[48,128]{1,0:T(8,128)S(1)}, f32[24,1024]{1,0:T(8,128)S(1)}, f32[32,128]{1,0:T(8,128)S(1)}) custom-call(s32[1]{0:T(128)} %bitcast.odd_ref, f32[48,128]{1,0:T(8,128)S(1)} %get-tuple-element.40.partial_ref, f32[8,128]{1,0:T(8,128)S(1)} %collective-permute-done.4.after_ref.swap_a_in, f32[8,128]{1,0:T(8,128)S(1)} %collective-permute-done.5.swap_b_in, ...), custom_call_target="tpu_custom_call" | custom-call | flops 1000000000 | bytes 1000000 | tf_op jit(solution)/shard_map/moment_kernel/pallas_call | solution.py:424
  37.7 15.8 %all_to_all.34 = f32[32,1,128]{2,1,0:T(1,128)S(1)} all-to-all(f32[32,1,128]{2,1,0:T(1,128)S(1)} %bitcast.15), channel_id=1, replica_groups=mesh['fluid'=4,'solid'=8] {'fluid','solid'}, dimensions={0} | all-to-all | bytes 32768 | tf_op jit(solution)/shard_map/all_to_all | solution.py:457
  53.6 0.9 %blend_kernel.1 = (f32[24,128]{1,0:T(8,128)S(1)}, f32[512,128]{1,0:T(8,128)S(1)}) custom-call(f32[32,128]{1,0:T(8,128)S(1)} %bitcast.16, f32[8,128]{1,0:T(8,128)S(1)} %get-tuple-element.36.scale_ref, s32[8,512]{1,0:T(8,128)S(1)} %get-tuple-element.53.code_ref, f32[512,128]{1,0:T(8,128)S(1)} %pick_kernel.2.pick0_ref, f32[512,128]{1,0:T(8,128)S(1)} %pick_kernel.3.pick1_ref, ...), custom_call_target="tpu_custom_call" | custom-call | flops 1000000000 | bytes 1000000 | tf_op jit(solution)/shard_map/blend_kernel/pallas_call | solution.py:424
  54.4 12.3 %all_to_all.35 = f32[32,16,128]{2,1,0:T(8,128)S(1)} all-to-all(f32[32,16,128]{2,1,0:T(8,128)S(1)} %bitcast.12), channel_id=1, replica_groups=mesh['fluid'=4,'solid'=8] {'fluid','solid'}, dimensions={0} | all-to-all | bytes 524288 | tf_op jit(solution)/shard_map/all_to_all | solution.py:457
  66.8 0.0 copy-done.3
  66.8 1.5 %motion_kernel.1 = (f32[3,1024]{1,0:T(4,128)}, f32[1024,128]{1,0:T(8,128)}) custom-call(f32[512,128]{1,0:T(8,128)S(1)} %bitcast.11, s32[8,1024]{1,0:T(8,128)S(1)} %get-tuple-element.57.place_ref, f32[24,128]{1,0:T(8,128)S(1)} %copy-done.3, f32[24,128]{1,0:T(8,128)S(1)} %get-tuple-element.58.weights_ref, f32[48,128]{1,0:T(8,128)S(1)} %get-tuple-element.43.first_ref, ...), custom_call_target="tpu_custom_call" | custom-call | flops 1000000000 | bytes 1000000 | tf_op jit(solution)/shard_map/motion_kernel/pallas_call | solution.py:424
  (2 shorter events, 0.0 us)
Async XLA Ops:
  0.6 19.7 %copy-start.2 = (f32[3,1024]{1,0:T(4,128)S(1)}, f32[3,1024]{1,0:T(4,128)}, u32[]{:S(2)}) copy-start(f32[3,1024]{1,0:T(4,128)} %support_ref.1) | copy-start | bytes 36868
  0.6 19.7 %copy-start.1 = (s32[8,1024]{1,0:T(8,128)S(1)}, s32[8,1024]{1,0:T(8,128)}, u32[]{:S(2)}) copy-start(s32[8,1024]{1,0:T(8,128)} %connectivity_ref.9) | copy-start | bytes 98308
  20.3 3.5 %copy-start = (f32[24,24,1024]{2,1,0:T(8,128)S(1)}, f32[24,24,1024]{2,1,0:T(8,128)}, u32[]{:S(2)}) copy-start(f32[24,24,1024]{2,1,0:T(8,128)} %stiffness_ref.5) | copy-start | bytes 7077892
  21.8 1.2 %collective-permute-start = (f32[8,128]{1,0:T(8,128)S(1)}, f32[8,128]{1,0:T(8,128)S(1)}, u32[]{:S(2)}, u32[]{:S(2)}) collective-permute-start(f32[8,128]{1,0:T(8,128)S(1)} %get-tuple-element.33), channel_id=1, source_target_pairs={{0,1},{2,3},{4,5},{6,7},{8,9},{10,11},{12,13},{14,15},{16,17},{18,... | collective-permute-start | bytes 12296 | tf_op jit(solution)/shard_map/ppermute | solution.py:454
  21.9 1.9 %collective-permute-start.1 = (f32[8,128]{1,0:T(8,128)S(1)}, f32[8,128]{1,0:T(8,128)S(1)}, u32[]{:S(2)}, u32[]{:S(2)}) collective-permute-start(f32[8,128]{1,0:T(8,128)S(1)} %get-tuple-element.34), channel_id=1, source_target_pairs={{1,2},{3,4},{5,6},{7,8},{9,10},{11,12},{13,14},{15,16},{17,18},{19... | collective-permute-start | bytes 12296 | tf_op jit(solution)/shard_map/ppermute | solution.py:454
  24.8 4.4 %collective-permute-start.2 = (f32[8,128]{1,0:T(8,128)S(1)}, f32[8,128]{1,0:T(8,128)S(1)}, u32[]{:S(2)}, u32[]{:S(2)}) collective-permute-start(f32[8,128]{1,0:T(8,128)S(1)} %get-tuple-element.38), channel_id=1, source_target_pairs={{0,1},{2,3},{4,5},{6,7},{8,9},{10,11},{12,13},{14,15},{16,17},{18,... | collective-permute-start | bytes 12296 | tf_op jit(solution)/shard_map/ppermute | solution.py:454
  28.4 0.8 %collective-permute-start.3 = (f32[8,128]{1,0:T(8,128)S(1)}, f32[8,128]{1,0:T(8,128)S(1)}, u32[]{:S(2)}, u32[]{:S(2)}) collective-permute-start(f32[8,128]{1,0:T(8,128)S(1)} %get-tuple-element.39), channel_id=1, source_target_pairs={{1,2},{3,4},{5,6},{7,8},{9,10},{11,12},{13,14},{15,16},{17,18},{19... | collective-permute-start | bytes 12296 | tf_op jit(solution)/shard_map/ppermute | solution.py:454
  30.1 5.7 %collective-permute-start.4 = (f32[8,128]{1,0:T(8,128)S(1)}, f32[8,128]{1,0:T(8,128)S(1)}, u32[]{:S(2)}, u32[]{:S(2)}) collective-permute-start(f32[8,128]{1,0:T(8,128)S(1)} %get-tuple-element.41), channel_id=1, source_target_pairs={{0,1},{2,3},{4,5},{6,7},{8,9},{10,11},{12,13},{14,15},{16,17},{18,... | collective-permute-start | bytes 12296 | tf_op jit(solution)/shard_map/ppermute | solution.py:454
  34.3 2.7 %collective-permute-start.5 = (f32[8,128]{1,0:T(8,128)S(1)}, f32[8,128]{1,0:T(8,128)S(1)}, u32[]{:S(2)}, u32[]{:S(2)}) collective-permute-start(f32[8,128]{1,0:T(8,128)S(1)} %get-tuple-element.42), channel_id=1, source_target_pairs={{1,2},{3,4},{5,6},{7,8},{9,10},{11,12},{13,14},{15,16},{17,18},{19... | collective-permute-start | bytes 12296 | tf_op jit(solution)/shard_map/ppermute | solution.py:454
  37.7 29.0 %copy-start.3 = (f32[24,128]{1,0:T(8,128)S(1)}, f32[24,128]{1,0:T(8,128)}, u32[]{:S(2)}) copy-start(f32[24,128]{1,0:T(8,128)} %table_ref.1) | copy-start | bytes 36868

commit v8 on v7

--- a/solution.py
+++ b/solution.py
@@ -44,20 +44,23 @@
     return jnp.take_along_axis(table, index, axis=1, mode="promise_in_bounds")
 
 
-def gather_corners(field, connectivity):
+def gather_corners(field, connectivity, blocks, known=None):
     elements = connectivity.shape[1]
     rows = {}
     for c in range(3):
-        for h in range(9):
+        for h in blocks:
             rows[c, h] = jnp.broadcast_to(field[c * FIELD_ROWS + h:c * FIELD_ROWS + h + 1], (CORNERS, LANES))
     parts = [[], [], []]
     for start in range(0, elements, LANES):
         index = connectivity[:, start:start + LANES]
         low, high = index & 127, index >> 7
-        masks = [high == h for h in range(9)]
+        masks = {h: high == h for h in blocks}
         for c in range(3):
-            total = jnp.zeros((CORNERS, LANES), F32)
-            for h in range(9):
+            if known is None:
+                total = jnp.zeros((CORNERS, LANES), F32)
+            else:
+                total = known[c * CORNERS:(c + 1) * CORNERS, start:start + LANES]
+            for h in blocks:
                 total = jnp.where(masks[h], take_lanes(rows[c, h], low), total)
             parts[c].append(total)
     return [jnp.concatenate(part, axis=1) for part in parts]
@@ -222,15 +225,21 @@
     weight_ref[...] = as_field(support_ref[...], own_rows) * inverse[:1, :1]
 
 
+def inner_kernel(own_rows, partial_ref, connectivity_ref, after_ref, out_ref):
+    del after_ref
+    out_ref[...] = jnp.concatenate(
+        gather_corners(partial_ref[...], connectivity_ref[...], range(1, own_rows)), axis=0)
+
+
 def product_kernel(own_rows, odd_ref, partial_ref, swap_a_in, swap_b_in, weight_ref, scale_ref, connectivity_ref,
-                   stiffness_ref, columns_ref, field_ref, values_ref, forces_ref, next_ref, swap_a_ref, swap_b_ref):
+                   stiffness_ref, columns_ref, inner_ref, field_ref, values_ref, forces_ref, next_ref, swap_a_ref, swap_b_ref):
     odd = odd_ref[0] == 1
 
     @pl.when(odd_ref[0] >= 0)
     def _():
         field = add_ends(partial_ref[...], odd, own_rows, swap_a_in[...], swap_b_in[...])
         field_ref[...] = field
-        values = gather_corners(field, connectivity_ref[...])
+        values = gather_corners(field, connectivity_ref[...], (0, own_rows), inner_ref)
         values_ref[...] = jnp.concatenate(values, axis=0)
         forces_ref[...] = matvec(stiffness_ref, values)
 
@@ -280,7 +289,7 @@
 
 
 def moment_kernel(own_rows, devices, odd_ref, partial_ref, swap_a_in, swap_b_in, weight_ref, scale_ref,
-                  connectivity_ref, stiffness_ref, own0_ref, own1_ref, values0_ref, turned_ref, numbers_ref,
+                  connectivity_ref, stiffness_ref, own0_ref, own1_ref, values0_ref, turned_ref, numbers_ref, inner_ref,
                   pick0_ref, pick1_ref, field_ref, values_ref, moments_ref):
     del pick0_ref, pick1_ref
     odd = odd_ref[0] == 1
@@ -293,7 +302,7 @@
     psi = jnp.sum(second * third) * numbers_ref[2:3]
     third = third - psi * second - phi * first
     values0, values1 = values0_ref[...], turned_ref[...]
-    values2 = jnp.concatenate(gather_corners(field, connectivity_ref[...]), axis=0)
+    values2 = jnp.concatenate(gather_corners(field, connectivity_ref[...], (0, own_rows), inner_ref), axis=0)
     values_ref[...] = values2
     values2 = values2 - psi[:, :1] * values1 - phi[:, :1] * values0
     forces2 = matvec(stiffness_ref, [values2[c * CORNERS:(c + 1) * CORNERS] for c in range(3)])
@@ -489,15 +498,21 @@
         [field, values, values, field, ends, ends],
     )
     end_a, end_b = swap(end_a, end_b)
+    (inner,) = call(
+        functools.partial(inner_kernel, own_rows), [values], (partial, connectivity, end_a), time=0.1)
     (columns,) = call(
         columns_kernel, [((CORNERS, elements, LANES), BF16)], (connectivity, end_a), time=0.1)
     first, values0, forces0, partial, end_a, end_b = call(
-        *stage, (odd, partial, end_a, end_b, weight, scale, connectivity, stiffness, columns), scalars=1)
+        *stage, (odd, partial, end_a, end_b, weight, scale, connectivity, stiffness, columns, inner), scalars=1)
     end_a, end_b = swap(end_a, end_b)
+    (inner,) = call(
+        functools.partial(inner_kernel, own_rows), [values], (partial, connectivity, end_a), time=0.1)
     (pick0,) = call(pick_kernel, [block], (values0, codes, end_a), time=0.1)
     second, values1, forces1, partial, end_a, end_b = call(
-        *stage, (odd, partial, end_a, end_b, weight, scale, connectivity, stiffness, columns), scalars=1)
+        *stage, (odd, partial, end_a, end_b, weight, scale, connectivity, stiffness, columns, inner), scalars=1)
     end_a, end_b = swap(end_a, end_b)
+    (inner,) = call(
+        functools.partial(inner_kernel, own_rows), [values], (partial, connectivity, end_a), time=0.1)
     (pick1,) = call(pick_kernel, [block], (values1, codes, end_a), time=0.1)
     own0, own1, turned, numbers = call(
         functools.partial(lower_kernel, own_rows),
@@ -508,7 +523,7 @@
     third, values2, moments = call(
         functools.partial(moment_kernel, own_rows, devices),
         [field, values, ((devices, LANES), F32)],
-        (odd, partial, end_a, end_b, weight, scale, connectivity, stiffness, own0, own1, values0, turned, numbers,
+        (odd, partial, end_a, end_b, weight, scale, connectivity, stiffness, own0, own1, values0, turned, numbers, inner,
          pick0, pick1),
         scalars=1,
     )

time: 68.5 us -> 68.3 us (level)
    pallas_call x11 -> x14, Pallas kernels: 11.2 us -> 11.8 us  [call(): pl.pallas_call(kernel, name=getattr(kernel, 'func', kernel).__name__, out...]
  transfers between devices with their start and end apart: 6 -> 6, of which waited for: 2 -> 2; matrix products, arithmetic and copies ran while one was open for 0% -> 0% of each run, Pallas kernels for 4% -> 5%
where the time goes in v8:
time: 68.3 us; the launch traced here: 68.1 us
  blocking collectives  45.5 us (67%)
  Pallas kernels  11.8 us (17%)
  starting transfers between devices  9.22 us (13%)
  between operations  0.78 us (1%)
    all_to_all x3, blocking collectives, everywhere(): return lax.all_to_all(rows, AXES, split_axis=0, concat_axis=0, tiled=True)  45.5 us
    pallas_call x14, Pallas kernels, call(): pl.pallas_call(kernel, name=getattr(kernel, 'func', kernel).__name__, out...  11.8 us
    ppermute x6, starting transfers between devices, swap(): return (lax.ppermute(a, AXES, pairs_a), lax.ppermute(b, AXES, pairs_b))  9.22 us
  transfers between devices with their start and end apart: 6, of which 2 were waited for; matrix products, arithmetic and copies ran while one was open for 0% of the time, Pallas kernels for 5%

profile of v8, /device:TPU:0, one launch (start us, length us, event | category | flops | bytes accessed | tf_op | source)
XLA Modules:
  0.0 68.1 jit_solution(15638597637605985443)
XLA Ops:
  0.7 1.9 %send_kernel.1 = (f32[512,128]{1,0:T(8,128)S(1)}, s32[8,1024]{1,0:T(8,128)S(1)}) custom-call(s32[1]{0:T(128)} %bitcast.odd_ref, f32[1024,128]{1,0:T(8,128)} %pressure_hbm.1, s32[1,1024]{1,0:T(1,128)} %bitcast.17, s32[1,1024]{1,0:T(1,128)} %bitcast.18, f32[24,128]{1,0:T(8,128)} %table_ref.1, f32[3,1024]{1,0:T(4,128)} %support_ref.1, f32[24,24,1024]{2,1,0:T(8,128)} %stiffness_ref.5), custom_call_target="tpu_custom_call" | custom-call | flops 1000000000 | bytes 1000000 | tf_op jit(solution)/shard_map/send_kernel/pallas_call | solution.py:433
  2.6 17.7 %all_to_all.33 = f32[32,16,128]{2,1,0:T(8,128)S(1)} all-to-all(f32[32,16,128]{2,1,0:T(8,128)S(1)} %bitcast.14), channel_id=1, replica_groups=mesh['fluid'=4,'solid'=8] {'fluid','solid'}, dimensions={0} | all-to-all | bytes 524288 | tf_op jit(solution)/shard_map/all_to_all | solution.py:466
  20.3 0.0 copy-done.2
  20.3 1.5 %load_kernel.1 = (f32[48,128]{1,0:T(8,128)S(1)}, f32[8,128]{1,0:T(8,128)S(1)}, f32[8,128]{1,0:T(8,128)S(1)}, f32[48,128]{1,0:T(8,128)S(1)}, f32[8,128]{1,0:T(8,128)S(1)}, /*index=5*/s32[8,512]{1,0:T(8,128)S(1)}) custom-call(s32[1]{0:T(128)} %bitcast.odd_ref, f32[512,128]{1,0:T(8,128)S(1)} %bitcast.13, s32[8,1024]{1,0:T(8,128)S(1)} %copy-done.1, ...), custom_call_target="tpu_custom_call" | custom-call | flops 1000000000 | bytes 1000000 | tf_op jit(solution)/shard_map/load_kernel/pallas_call | solution.py:433
  21.8 0.1 collective-permute-start
  21.9 0.7 collective-permute-start.1
  22.6 0.5 collective-permute-done.after_ref.swap_a_in
  23.1 0.7 %columns_kernel.1.columns_ref = bf16[8,1024,128]{2,1,0:T(8,128)(2,1)S(1)} custom-call(s32[8,1024]{1,0:T(8,128)S(1)} %copy-done.1, f32[8,128]{1,0:T(8,128)S(1)} %collective-permute-done.after_ref.swap_a_in), custom_call_target="tpu_custom_call" | custom-call | flops 100000000 | bytes 100000 | tf_op jit(solution)/shard_map/columns_kernel/pallas_call | solution.py:433
  23.8 0.3 inner_kernel.3.inner_ref
  24.1 0.0 collective-permute-done.1.swap_b_in
  24.1 0.0 copy-done
  24.1 0.9 %product_kernel.2 = (f32[48,128]{1,0:T(8,128)S(1)}, f32[24,1024]{1,0:T(8,128)S(1)}, f32[24,1024]{1,0:T(8,128)S(1)}, f32[48,128]{1,0:T(8,128)S(1)}, f32[8,128]{1,0:T(8,128)S(1)}, /*index=5*/f32[8,128]{1,0:T(8,128)S(1)}) custom-call(s32[1]{0:T(128)} %bitcast.odd_ref, f32[48,128]{1,0:T(8,128)S(1)} %get-tuple-element.32.partial_ref, ...), custom_call_target="tpu_custom_call" | custom-call | flops 1000000000 | bytes 1000000 | tf_op jit(solution)/shard_map/product_kernel/pallas_call | solution.py:433
  25.0 3.3 %collective-permute-start.2 = (f32[8,128]{1,0:T(8,128)S(1)}, f32[8,128]{1,0:T(8,128)S(1)}, u32[]{:S(2)}, u32[]{:S(2)}) collective-permute-start(f32[8,128]{1,0:T(8,128)S(1)} %get-tuple-element.38), channel_id=1, source_target_pairs={{0,1},{2,3},{4,5},{6,7},{8,9},{10,11},{12,13},{14,15},{16,17},{18,... | collective-permute-start | bytes 12296 | tf_op jit(solution)/shard_map/ppermute | solution.py:463
  28.3 0.6 collective-permute-start.3
  29.0 0.2 collective-permute-done.2.after_ref.swap_a_in
  29.1 0.3 inner_kernel.4.inner_ref
  29.4 0.0 collective-permute-done.3.swap_b_in
  29.4 0.9 %product_kernel.3 = (f32[48,128]{1,0:T(8,128)S(1)}, f32[24,1024]{1,0:T(8,128)S(1)}, f32[24,1024]{1,0:T(8,128)S(1)}, f32[48,128]{1,0:T(8,128)S(1)}, f32[8,128]{1,0:T(8,128)S(1)}, /*index=5*/f32[8,128]{1,0:T(8,128)S(1)}) custom-call(s32[1]{0:T(128)} %bitcast.odd_ref, f32[48,128]{1,0:T(8,128)S(1)} %get-tuple-element.37.partial_ref, ...), custom_call_target="tpu_custom_call" | custom-call | flops 1000000000 | bytes 1000000 | tf_op jit(solution)/shard_map/product_kernel/pallas_call | solution.py:433
  30.3 3.9 %collective-permute-start.4 = (f32[8,128]{1,0:T(8,128)S(1)}, f32[8,128]{1,0:T(8,128)S(1)}, u32[]{:S(2)}, u32[]{:S(2)}) collective-permute-start(f32[8,128]{1,0:T(8,128)S(1)} %get-tuple-element.41), channel_id=1, source_target_pairs={{0,1},{2,3},{4,5},{6,7},{8,9},{10,11},{12,13},{14,15},{16,17},{18,... | collective-permute-start | bytes 12296 | tf_op jit(solution)/shard_map/ppermute | solution.py:463
  34.2 0.6 collective-permute-start.5
  34.9 0.8 %pick_kernel.2.pick0_ref = f32[512,128]{1,0:T(8,128)S(1)} custom-call(f32[24,1024]{1,0:T(8,128)S(1)} %get-tuple-element.45.values0_ref.values_ref, s32[8,512]{1,0:T(8,128)S(1)} %get-tuple-element.53.code_ref, f32[8,128]{1,0:T(8,128)S(1)} %collective-permute-done.2.after_ref.swap_a_in), custom_call_target="tpu_custom_call" | custom-call | flops 100000000 | bytes 100000 | tf_op jit(solution)/shard_map/pick_kernel/pallas_call | solution.py:433
  35.7 0.0 collective-permute-done.4.after_ref.swap_a_in
  35.7 0.3 inner_kernel.5.inner_ref
  35.9 0.8 %pick_kernel.3.pick1_ref = f32[512,128]{1,0:T(8,128)S(1)} custom-call(f32[24,1024]{1,0:T(8,128)S(1)} %get-tuple-element.46.values1_ref.values_ref, s32[8,512]{1,0:T(8,128)S(1)} %get-tuple-element.53.code_ref, f32[8,128]{1,0:T(8,128)S(1)} %collective-permute-done.4.after_ref.swap_a_in), custom_call_target="tpu_custom_call" | custom-call | flops 100000000 | bytes 100000 | tf_op jit(solution)/shard_map/pick_kernel/pallas_call | solution.py:433
  36.8 0.4 lower_kernel.1
  37.1 0.0 collective-permute-done.5.swap_b_in
  37.1 0.7 moment_kernel.1
  37.8 15.5 %all_to_all.34 = f32[32,1,128]{2,1,0:T(1,128)S(1)} all-to-all(f32[32,1,128]{2,1,0:T(1,128)S(1)} %bitcast.15), channel_id=1, replica_groups=mesh['fluid'=4,'solid'=8] {'fluid','solid'}, dimensions={0} | all-to-all | bytes 32768 | tf_op jit(solution)/shard_map/all_to_all | solution.py:466
  53.3 0.9 %blend_kernel.1 = (f32[24,128]{1,0:T(8,128)S(1)}, f32[512,128]{1,0:T(8,128)S(1)}) custom-call(f32[32,128]{1,0:T(8,128)S(1)} %bitcast.16, f32[8,128]{1,0:T(8,128)S(1)} %get-tuple-element.36.scale_ref, s32[8,512]{1,0:T(8,128)S(1)} %get-tuple-element.53.code_ref, f32[512,128]{1,0:T(8,128)S(1)} %pick_kernel.2.pick0_ref, f32[512,128]{1,0:T(8,128)S(1)} %pick_kernel.3.pick1_ref, ...), custom_call_target="tpu_custom_call" | custom-call | flops 1000000000 | bytes 1000000 | tf_op jit(solution)/shard_map/blend_kernel/pallas_call | solution.py:433
  54.2 12.3 %all_to_all.35 = f32[32,16,128]{2,1,0:T(8,128)S(1)} all-to-all(f32[32,16,128]{2,1,0:T(8,128)S(1)} %bitcast.12), channel_id=1, replica_groups=mesh['fluid'=4,'solid'=8] {'fluid','solid'}, dimensions={0} | all-to-all | bytes 524288 | tf_op jit(solution)/shard_map/all_to_all | solution.py:466
  66.5 0.0 copy-done.3
  66.5 1.5 %motion_kernel.1 = (f32[3,1024]{1,0:T(4,128)}, f32[1024,128]{1,0:T(8,128)}) custom-call(f32[512,128]{1,0:T(8,128)S(1)} %bitcast.11, s32[8,1024]{1,0:T(8,128)S(1)} %get-tuple-element.57.place_ref, f32[24,128]{1,0:T(8,128)S(1)} %copy-done.3, f32[24,128]{1,0:T(8,128)S(1)} %get-tuple-element.58.weights_ref, f32[48,128]{1,0:T(8,128)S(1)} %get-tuple-element.43.first_ref, ...), custom_call_target="tpu_custom_call" | custom-call | flops 1000000000 | bytes 1000000 | tf_op jit(solution)/shard_map/motion_kernel/pallas_call | solution.py:433
  (5 shorter events, 0.0 us)
Async XLA Ops:
  0.6 19.7 %copy-start.2 = (f32[3,1024]{1,0:T(4,128)S(1)}, f32[3,1024]{1,0:T(4,128)}, u32[]{:S(2)}) copy-start(f32[3,1024]{1,0:T(4,128)} %support_ref.1) | copy-start | bytes 36868
  0.6 19.7 %copy-start.1 = (s32[8,1024]{1,0:T(8,128)S(1)}, s32[8,1024]{1,0:T(8,128)}, u32[]{:S(2)}) copy-start(s32[8,1024]{1,0:T(8,128)} %connectivity_ref.15) | copy-start | bytes 98308
  20.3 3.8 %copy-start = (f32[24,24,1024]{2,1,0:T(8,128)S(1)}, f32[24,24,1024]{2,1,0:T(8,128)}, u32[]{:S(2)}) copy-start(f32[24,24,1024]{2,1,0:T(8,128)} %stiffness_ref.5) | copy-start | bytes 7077892
  21.8 1.2 %collective-permute-start = (f32[8,128]{1,0:T(8,128)S(1)}, f32[8,128]{1,0:T(8,128)S(1)}, u32[]{:S(2)}, u32[]{:S(2)}) collective-permute-start(f32[8,128]{1,0:T(8,128)S(1)} %get-tuple-element.33), channel_id=1, source_target_pairs={{0,1},{2,3},{4,5},{6,7},{8,9},{10,11},{12,13},{14,15},{16,17},{18,... | collective-permute-start | bytes 12296 | tf_op jit(solution)/shard_map/ppermute | solution.py:463
  21.9 2.2 %collective-permute-start.1 = (f32[8,128]{1,0:T(8,128)S(1)}, f32[8,128]{1,0:T(8,128)S(1)}, u32[]{:S(2)}, u32[]{:S(2)}) collective-permute-start(f32[8,128]{1,0:T(8,128)S(1)} %get-tuple-element.34), channel_id=1, source_target_pairs={{1,2},{3,4},{5,6},{7,8},{9,10},{11,12},{13,14},{15,16},{17,18},{19... | collective-permute-start | bytes 12296 | tf_op jit(solution)/shard_map/ppermute | solution.py:463
  25.0 4.1 %collective-permute-start.2 = (f32[8,128]{1,0:T(8,128)S(1)}, f32[8,128]{1,0:T(8,128)S(1)}, u32[]{:S(2)}, u32[]{:S(2)}) collective-permute-start(f32[8,128]{1,0:T(8,128)S(1)} %get-tuple-element.38), channel_id=1, source_target_pairs={{0,1},{2,3},{4,5},{6,7},{8,9},{10,11},{12,13},{14,15},{16,17},{18,... | collective-permute-start | bytes 12296 | tf_op jit(solution)/shard_map/ppermute | solution.py:463
  28.3 1.1 %collective-permute-start.3 = (f32[8,128]{1,0:T(8,128)S(1)}, f32[8,128]{1,0:T(8,128)S(1)}, u32[]{:S(2)}, u32[]{:S(2)}) collective-permute-start(f32[8,128]{1,0:T(8,128)S(1)} %get-tuple-element.39), channel_id=1, source_target_pairs={{1,2},{3,4},{5,6},{7,8},{9,10},{11,12},{13,14},{15,16},{17,18},{19... | collective-permute-start | bytes 12296 | tf_op jit(solution)/shard_map/ppermute | solution.py:463
  30.3 5.4 %collective-permute-start.4 = (f32[8,128]{1,0:T(8,128)S(1)}, f32[8,128]{1,0:T(8,128)S(1)}, u32[]{:S(2)}, u32[]{:S(2)}) collective-permute-start(f32[8,128]{1,0:T(8,128)S(1)} %get-tuple-element.41), channel_id=1, source_target_pairs={{0,1},{2,3},{4,5},{6,7},{8,9},{10,11},{12,13},{14,15},{16,17},{18,... | collective-permute-start | bytes 12296 | tf_op jit(solution)/shard_map/ppermute | solution.py:463
  34.2 3.0 %collective-permute-start.5 = (f32[8,128]{1,0:T(8,128)S(1)}, f32[8,128]{1,0:T(8,128)S(1)}, u32[]{:S(2)}, u32[]{:S(2)}) collective-permute-start(f32[8,128]{1,0:T(8,128)S(1)} %get-tuple-element.42), channel_id=1, source_target_pairs={{1,2},{3,4},{5,6},{7,8},{9,10},{11,12},{13,14},{15,16},{17,18},{19... | collective-permute-start | bytes 12296 | tf_op jit(solution)/shard_map/ppermute | solution.py:463
  37.8 28.7 %copy-start.3 = (f32[24,128]{1,0:T(8,128)S(1)}, f32[24,128]{1,0:T(8,128)}, u32[]{:S(2)}) copy-start(f32[24,128]{1,0:T(8,128)} %table_ref.1) | copy-start | bytes 36868

commit v9 on v8

--- a/solution.py
+++ b/solution.py
@@ -14,6 +14,7 @@
 FIELD_ROWS = 16
 LANES = 128
 WIDE = 256
+SPOTS = 3
 VMEM_BYTES = 24 * 1024 * 1024
 F32 = jnp.float32
 BF16 = jnp.bfloat16
@@ -232,7 +233,8 @@
 
 
 def product_kernel(own_rows, odd_ref, partial_ref, swap_a_in, swap_b_in, weight_ref, scale_ref, connectivity_ref,
-                   stiffness_ref, columns_ref, inner_ref, field_ref, values_ref, forces_ref, next_ref, swap_a_ref, swap_b_ref):
+                   stiffness_ref, columns_ref, inner_ref, after_ref, field_ref, values_ref, forces_ref, next_ref, swap_a_ref, swap_b_ref):
+    del after_ref
     odd = odd_ref[0] == 1
 
     @pl.when(odd_ref[0] >= 0)
@@ -356,10 +358,34 @@
     ]
 
 
-def pick(values, code_ref, out_ref, blend):
+def spots_kernel(code_ref, after_ref, out_ref):
+    del after_ref
+    for i in range(out_ref.shape[0]):
+        code = code_ref[GROUPS - out_ref.shape[0] + i:GROUPS - out_ref.shape[0] + i + 1]
+        out_ref[i] = onehot(iota(out_ref.shape[1:], 0) == (code & 255))
+
+
+def pick(values, code_ref, out_ref, blend, spots_ref=None):
+    gathered, found = GROUPS, {}
+    if spots_ref is not None:
+        gathered = GROUPS - spots_ref.shape[0]
+        halves = split(values)
+        stack = jnp.concatenate(
+            [half[:, i * WIDE:(i + 1) * WIDE] for i in range(values.shape[1] // WIDE) for half in halves], axis=0)
+        for g in range(gathered, GROUPS):
+            product = dot_nn(stack, spots_ref[g - gathered])
+            high = code_ref[g:g + 1] >> 8
+            total = jnp.zeros((DOF, code_ref.shape[1]), F32)
+            for i in range(values.shape[1] // WIDE):
+                part = product[i * 2 * DOF:i * 2 * DOF + DOF] + product[i * 2 * DOF + DOF:(i + 1) * 2 * DOF]
+                total = jnp.where(high == i, part, total)
+            found[g] = total
     for start in range(0, code_ref.shape[1], LANES):
         sections = []
         for g in range(GROUPS):
+            if g >= gathered:
+                sections.append(found[g][:, start:start + LANES])
+                continue
             code = jnp.broadcast_to(code_ref[g:g + 1, start:start + LANES], (CORNERS, LANES))
             low, high = code & 127, code >> 7
             masks = [high == i for i in range(8)]
@@ -379,7 +405,8 @@
     pick(values_ref[...], code_ref, out_ref, lambda tile, rows: tile)
 
 
-def blend_kernel(moments_ref, scale_ref, code_ref, pick0_ref, pick1_ref, values_ref, weights_ref, out_ref):
+def blend_kernel(moments_ref, scale_ref, code_ref, spots_ref, pick0_ref, pick1_ref, values_ref,
+                 weights_ref, out_ref):
     weights = step_weights(moments_ref[...])
     weights = [weight * scale_ref[:1, :1] for weight in weights]
     weights_ref[...] = jnp.concatenate([jnp.broadcast_to(weight, (8, LANES)) for weight in weights], axis=0)
@@ -387,7 +414,7 @@
     def blend(tile, rows):
         return weights[0] * pick0_ref[rows, :] + weights[1] * pick1_ref[rows, :] + weights[2] * tile
 
-    pick(values_ref[...], code_ref, out_ref, blend)
+    pick(values_ref[...], code_ref, out_ref, blend, spots_ref)
 
 
 def motion_kernel(own_rows, rows_ref, place_ref, table_ref, weights_ref, first_ref, second_ref, third_ref,
@@ -503,13 +530,14 @@
     (columns,) = call(
         columns_kernel, [((CORNERS, elements, LANES), BF16)], (connectivity, end_a), time=0.1)
     first, values0, forces0, partial, end_a, end_b = call(
-        *stage, (odd, partial, end_a, end_b, weight, scale, connectivity, stiffness, columns, inner), scalars=1)
+        *stage, (odd, partial, end_a, end_b, weight, scale, connectivity, stiffness, columns, inner, weight), scalars=1)
     end_a, end_b = swap(end_a, end_b)
     (inner,) = call(
         functools.partial(inner_kernel, own_rows), [values], (partial, connectivity, end_a), time=0.1)
+    (spots,) = call(spots_kernel, [((SPOTS, WIDE, slots), BF16)], (codes, end_a), time=0.1)
     (pick0,) = call(pick_kernel, [block], (values0, codes, end_a), time=0.1)
     second, values1, forces1, partial, end_a, end_b = call(
-        *stage, (odd, partial, end_a, end_b, weight, scale, connectivity, stiffness, columns, inner), scalars=1)
+        *stage, (odd, partial, end_a, end_b, weight, scale, connectivity, stiffness, columns, inner, spots), scalars=1)
     end_a, end_b = swap(end_a, end_b)
     (inner,) = call(
         functools.partial(inner_kernel, own_rows), [values], (partial, connectivity, end_a), time=0.1)
@@ -531,7 +559,7 @@
     weights, leaving = call(
         blend_kernel,
         [((24, LANES), F32), block],
-        (moments, scale, codes, pick0, pick1, values2),
+        (moments, scale, codes, spots, pick0, pick1, values2),
     )
     returned = everywhere(leaving)
     return call(

time: 68.3 us -> 68 us (level)
    pallas_call x14 -> x15, Pallas kernels: 11.8 us -> 11.7 us  [call(): pl.pallas_call(kernel, name=getattr(kernel, 'func', kernel).__name__, out...]
where the time goes in v9:
time: 68 us; the launch traced here: 67.8 us
  blocking collectives  45.6 us (67%)
  Pallas kernels  11.7 us (17%)
  starting transfers between devices  9.07 us (13%)
  between operations  0.79 us (1%)
    all_to_all x3, blocking collectives, everywhere(): return lax.all_to_all(rows, AXES, split_axis=0, concat_axis=0, tiled=True)  45.6 us
    pallas_call x15, Pallas kernels, call(): pl.pallas_call(kernel, name=getattr(kernel, 'func', kernel).__name__, out...  11.7 us
    ppermute x6, starting transfers between devices, swap(): return (lax.ppermute(a, AXES, pairs_a), lax.ppermute(b, AXES, pairs_b))  9.07 us
  transfers between devices with their start and end apart: 6, of which 2 were waited for; matrix products, arithmetic and copies ran while one was open for 0% of the time, Pallas kernels for 5%

profile of v9, /device:TPU:0, one launch (start us, length us, event | category | flops | bytes accessed | tf_op | source)
XLA Modules:
  0.0 67.8 jit_solution(13578317400590101625)
XLA Ops:
  0.7 1.9 %send_kernel.1 = (f32[512,128]{1,0:T(8,128)S(1)}, s32[8,1024]{1,0:T(8,128)S(1)}) custom-call(s32[1]{0:T(128)} %bitcast.odd_ref, f32[1024,128]{1,0:T(8,128)} %pressure_hbm.1, s32[1,1024]{1,0:T(1,128)} %bitcast.17, s32[1,1024]{1,0:T(1,128)} %bitcast.18, f32[24,128]{1,0:T(8,128)} %table_ref.1, f32[3,1024]{1,0:T(4,128)} %support_ref.1, f32[24,24,1024]{2,1,0:T(8,128)} %stiffness_ref.5), custom_call_target="tpu_custom_call" | custom-call | flops 1000000000 | bytes 1000000 | tf_op jit(solution)/shard_map/send_kernel/pallas_call | solution.py:460
  2.6 17.7 %all_to_all.33 = f32[32,16,128]{2,1,0:T(8,128)S(1)} all-to-all(f32[32,16,128]{2,1,0:T(8,128)S(1)} %bitcast.14), channel_id=1, replica_groups=mesh['fluid'=4,'solid'=8] {'fluid','solid'}, dimensions={0} | all-to-all | bytes 524288 | tf_op jit(solution)/shard_map/all_to_all | solution.py:493
  20.3 0.0 copy-done.2
  20.3 1.5 %load_kernel.1 = (f32[48,128]{1,0:T(8,128)S(1)}, f32[8,128]{1,0:T(8,128)S(1)}, f32[8,128]{1,0:T(8,128)S(1)}, f32[48,128]{1,0:T(8,128)S(1)}, f32[8,128]{1,0:T(8,128)S(1)}, /*index=5*/s32[8,512]{1,0:T(8,128)S(1)}) custom-call(s32[1]{0:T(128)} %bitcast.odd_ref, f32[512,128]{1,0:T(8,128)S(1)} %bitcast.13, s32[8,1024]{1,0:T(8,128)S(1)} %copy-done.1, ...), custom_call_target="tpu_custom_call" | custom-call | flops 1000000000 | bytes 1000000 | tf_op jit(solution)/shard_map/load_kernel/pallas_call | solution.py:460
  21.8 0.1 collective-permute-start
  21.9 0.7 collective-permute-start.1
  22.6 0.5 collective-permute-done.after_ref.swap_a_in
  23.1 0.7 %columns_kernel.1.columns_ref = bf16[8,1024,128]{2,1,0:T(8,128)(2,1)S(1)} custom-call(s32[8,1024]{1,0:T(8,128)S(1)} %copy-done.1, f32[8,128]{1,0:T(8,128)S(1)} %collective-permute-done.after_ref.swap_a_in), custom_call_target="tpu_custom_call" | custom-call | flops 100000000 | bytes 100000 | tf_op jit(solution)/shard_map/columns_kernel/pallas_call | solution.py:460
  23.8 0.3 inner_kernel.3.inner_ref
  24.1 0.0 collective-permute-done.1.swap_b_in
  24.1 0.0 copy-done
  24.1 0.9 %product_kernel.2 = (f32[48,128]{1,0:T(8,128)S(1)}, f32[24,1024]{1,0:T(8,128)S(1)}, f32[24,1024]{1,0:T(8,128)S(1)}, f32[48,128]{1,0:T(8,128)S(1)}, f32[8,128]{1,0:T(8,128)S(1)}, /*index=5*/f32[8,128]{1,0:T(8,128)S(1)}) custom-call(s32[1]{0:T(128)} %bitcast.odd_ref, f32[48,128]{1,0:T(8,128)S(1)} %get-tuple-element.32.partial_ref, ...), custom_call_target="tpu_custom_call" | custom-call | flops 1000000000 | bytes 1000000 | tf_op jit(solution)/shard_map/product_kernel/pallas_call | solution.py:460
  25.0 3.3 %collective-permute-start.2 = (f32[8,128]{1,0:T(8,128)S(1)}, f32[8,128]{1,0:T(8,128)S(1)}, u32[]{:S(2)}, u32[]{:S(2)}) collective-permute-start(f32[8,128]{1,0:T(8,128)S(1)} %get-tuple-element.38), channel_id=1, source_target_pairs={{0,1},{2,3},{4,5},{6,7},{8,9},{10,11},{12,13},{14,15},{16,17},{18,... | collective-permute-start | bytes 12296 | tf_op jit(solution)/shard_map/ppermute | solution.py:490
  28.3 0.6 collective-permute-start.3
  29.0 0.2 collective-permute-done.2.after_ref.swap_a_in
  29.1 0.1 spots_kernel.1.after_ref.spots_ref
  29.3 0.3 inner_kernel.4.inner_ref
  29.5 0.0 collective-permute-done.3.swap_b_in
  29.5 0.9 %product_kernel.3 = (f32[48,128]{1,0:T(8,128)S(1)}, f32[24,1024]{1,0:T(8,128)S(1)}, f32[24,1024]{1,0:T(8,128)S(1)}, f32[48,128]{1,0:T(8,128)S(1)}, f32[8,128]{1,0:T(8,128)S(1)}, /*index=5*/f32[8,128]{1,0:T(8,128)S(1)}) custom-call(s32[1]{0:T(128)} %bitcast.odd_ref, f32[48,128]{1,0:T(8,128)S(1)} %get-tuple-element.37.partial_ref, ...), custom_call_target="tpu_custom_call" | custom-call | flops 1000000000 | bytes 1000000 | tf_op jit(solution)/shard_map/product_kernel/pallas_call | solution.py:460
  30.4 3.7 %collective-permute-start.4 = (f32[8,128]{1,0:T(8,128)S(1)}, f32[8,128]{1,0:T(8,128)S(1)}, u32[]{:S(2)}, u32[]{:S(2)}) collective-permute-start(f32[8,128]{1,0:T(8,128)S(1)} %get-tuple-element.42), channel_id=1, source_target_pairs={{0,1},{2,3},{4,5},{6,7},{8,9},{10,11},{12,13},{14,15},{16,17},{18,... | collective-permute-start | bytes 12296 | tf_op jit(solution)/shard_map/ppermute | solution.py:490
  34.2 0.6 collective-permute-start.5
  34.8 0.8 %pick_kernel.2.pick0_ref = f32[512,128]{1,0:T(8,128)S(1)} custom-call(f32[24,1024]{1,0:T(8,128)S(1)} %get-tuple-element.46.values0_ref.values_ref, s32[8,512]{1,0:T(8,128)S(1)} %get-tuple-element.40.code_ref, f32[8,128]{1,0:T(8,128)S(1)} %collective-permute-done.2.after_ref.swap_a_in), custom_call_target="tpu_custom_call" | custom-call | flops 100000000 | bytes 100000 | tf_op jit(solution)/shard_map/pick_kernel/pallas_call | solution.py:460
  35.7 0.0 collective-permute-done.4.after_ref.swap_a_in
  35.7 0.8 %pick_kernel.3.pick1_ref = f32[512,128]{1,0:T(8,128)S(1)} custom-call(f32[24,1024]{1,0:T(8,128)S(1)} %get-tuple-element.47.values1_ref.values_ref, s32[8,512]{1,0:T(8,128)S(1)} %get-tuple-element.40.code_ref, f32[8,128]{1,0:T(8,128)S(1)} %collective-permute-done.4.after_ref.swap_a_in), custom_call_target="tpu_custom_call" | custom-call | flops 100000000 | bytes 100000 | tf_op jit(solution)/shard_map/pick_kernel/pallas_call | solution.py:460
  36.5 0.3 inner_kernel.5.inner_ref
  36.8 0.4 lower_kernel.1
  37.1 0.0 collective-permute-done.5.swap_b_in
  37.1 0.7 moment_kernel.1
  37.8 15.5 %all_to_all.34 = f32[32,1,128]{2,1,0:T(1,128)S(1)} all-to-all(f32[32,1,128]{2,1,0:T(1,128)S(1)} %bitcast.15), channel_id=1, replica_groups=mesh['fluid'=4,'solid'=8] {'fluid','solid'}, dimensions={0} | all-to-all | bytes 32768 | tf_op jit(solution)/shard_map/all_to_all | solution.py:493
  53.4 0.6 blend_kernel.1
  53.9 12.3 %all_to_all.35 = f32[32,16,128]{2,1,0:T(8,128)S(1)} all-to-all(f32[32,16,128]{2,1,0:T(8,128)S(1)} %bitcast.12), channel_id=1, replica_groups=mesh['fluid'=4,'solid'=8] {'fluid','solid'}, dimensions={0} | all-to-all | bytes 524288 | tf_op jit(solution)/shard_map/all_to_all | solution.py:493
  66.3 1.5 %motion_kernel.1 = (f32[3,1024]{1,0:T(4,128)}, f32[1024,128]{1,0:T(8,128)}) custom-call(f32[512,128]{1,0:T(8,128)S(1)} %bitcast.11, s32[8,1024]{1,0:T(8,128)S(1)} %get-tuple-element.57.place_ref, f32[24,128]{1,0:T(8,128)S(1)} %copy-done.3, f32[24,128]{1,0:T(8,128)S(1)} %get-tuple-element.58.weights_ref, f32[48,128]{1,0:T(8,128)S(1)} %get-tuple-element.44.first_ref, ...), custom_call_target="tpu_custom_call" | custom-call | flops 1000000000 | bytes 1000000 | tf_op jit(solution)/shard_map/motion_kernel/pallas_call | solution.py:460
  (6 shorter events, 0.0 us)
Async XLA Ops:
  0.6 19.7 %copy-start.2 = (f32[3,1024]{1,0:T(4,128)S(1)}, f32[3,1024]{1,0:T(4,128)}, u32[]{:S(2)}) copy-start(f32[3,1024]{1,0:T(4,128)} %support_ref.1) | copy-start | bytes 36868
  0.6 19.7 %copy-start.1 = (s32[8,1024]{1,0:T(8,128)S(1)}, s32[8,1024]{1,0:T(8,128)}, u32[]{:S(2)}) copy-start(s32[8,1024]{1,0:T(8,128)} %connectivity_ref.15) | copy-start | bytes 98308
  20.3 3.8 %copy-start = (f32[24,24,1024]{2,1,0:T(8,128)S(1)}, f32[24,24,1024]{2,1,0:T(8,128)}, u32[]{:S(2)}) copy-start(f32[24,24,1024]{2,1,0:T(8,128)} %stiffness_ref.5) | copy-start | bytes 7077892
  21.8 1.2 %collective-permute-start = (f32[8,128]{1,0:T(8,128)S(1)}, f32[8,128]{1,0:T(8,128)S(1)}, u32[]{:S(2)}, u32[]{:S(2)}) collective-permute-start(f32[8,128]{1,0:T(8,128)S(1)} %get-tuple-element.33), channel_id=1, source_target_pairs={{0,1},{2,3},{4,5},{6,7},{8,9},{10,11},{12,13},{14,15},{16,17},{18,... | collective-permute-start | bytes 12296 | tf_op jit(solution)/shard_map/ppermute | solution.py:490
  21.9 2.2 %collective-permute-start.1 = (f32[8,128]{1,0:T(8,128)S(1)}, f32[8,128]{1,0:T(8,128)S(1)}, u32[]{:S(2)}, u32[]{:S(2)}) collective-permute-start(f32[8,128]{1,0:T(8,128)S(1)} %get-tuple-element.34), channel_id=1, source_target_pairs={{1,2},{3,4},{5,6},{7,8},{9,10},{11,12},{13,14},{15,16},{17,18},{19... | collective-permute-start | bytes 12296 | tf_op jit(solution)/shard_map/ppermute | solution.py:490
  25.0 4.1 %collective-permute-start.2 = (f32[8,128]{1,0:T(8,128)S(1)}, f32[8,128]{1,0:T(8,128)S(1)}, u32[]{:S(2)}, u32[]{:S(2)}) collective-permute-start(f32[8,128]{1,0:T(8,128)S(1)} %get-tuple-element.38), channel_id=1, source_target_pairs={{0,1},{2,3},{4,5},{6,7},{8,9},{10,11},{12,13},{14,15},{16,17},{18,... | collective-permute-start | bytes 12296 | tf_op jit(solution)/shard_map/ppermute | solution.py:490
  28.3 1.2 %collective-permute-start.3 = (f32[8,128]{1,0:T(8,128)S(1)}, f32[8,128]{1,0:T(8,128)S(1)}, u32[]{:S(2)}, u32[]{:S(2)}) collective-permute-start(f32[8,128]{1,0:T(8,128)S(1)} %get-tuple-element.39), channel_id=1, source_target_pairs={{1,2},{3,4},{5,6},{7,8},{9,10},{11,12},{13,14},{15,16},{17,18},{19... | collective-permute-start | bytes 12296 | tf_op jit(solution)/shard_map/ppermute | solution.py:490
  30.4 5.2 %collective-permute-start.4 = (f32[8,128]{1,0:T(8,128)S(1)}, f32[8,128]{1,0:T(8,128)S(1)}, u32[]{:S(2)}, u32[]{:S(2)}) collective-permute-start(f32[8,128]{1,0:T(8,128)S(1)} %get-tuple-element.42), channel_id=1, source_target_pairs={{0,1},{2,3},{4,5},{6,7},{8,9},{10,11},{12,13},{14,15},{16,17},{18,... | collective-permute-start | bytes 12296 | tf_op jit(solution)/shard_map/ppermute | solution.py:490
  34.2 3.0 %collective-permute-start.5 = (f32[8,128]{1,0:T(8,128)S(1)}, f32[8,128]{1,0:T(8,128)S(1)}, u32[]{:S(2)}, u32[]{:S(2)}) collective-permute-start(f32[8,128]{1,0:T(8,128)S(1)} %get-tuple-element.43), channel_id=1, source_target_pairs={{1,2},{3,4},{5,6},{7,8},{9,10},{11,12},{13,14},{15,16},{17,18},{19... | collective-permute-start | bytes 12296 | tf_op jit(solution)/shard_map/ppermute | solution.py:490
  37.8 28.4 %copy-start.3 = (f32[24,128]{1,0:T(8,128)S(1)}, f32[24,128]{1,0:T(8,128)}, u32[]{:S(2)}) copy-start(f32[24,128]{1,0:T(8,128)} %table_ref.1) | copy-start | bytes 36868
